TPU v7x, 32 devices: a whole 2x2x4 slice. The times are simulated.
32 devices in a mesh: dp: 4 (over y, x), cp: 8 (over z, core).
Axes of the slice: x: 2, y: 2, z: 4, core: 2. Of those that a mesh axis runs over, the one named last changes fastest.
Arguments:
- tokens: bfloat16 [4096, 1536], P(('dp', 'cp')), may hold values from -6 to 6
- cotangent: bfloat16 [4096, 1536], P(('dp', 'cp')), may hold values from -6 to 6
- doc_lengths: int32 [4, 4], P('dp'), may hold values from 1 to 1021, as said below
- routes: int32 [2, 4096, 4], P(None, ('dp', 'cp')), may hold values from 0 to 15, all different within a row; in each aligned block of 128 rows (0 to 127, 128 to 255, ..., all dimensions but the last counted through in order) at most 64 rows name the same one
- w_qkv: bfloat16 [2, 2048, 1536], P(None, ('dp', 'cp')), may hold values from -0.15625 to 0.15625
- w_out: bfloat16 [2, 1536, 1536], P(None, ('dp', 'cp')), may hold values from -1.25 to 1.25
- router: bfloat16 [2, 1536, 16], P(None, ('dp', 'cp')), may hold values from -0.078125 to 0.078125
- gains: bfloat16 [2, 1536, 2], P(None, ('dp', 'cp')), may hold values from 0.5 to 1.5
- w_gate_up: bfloat16 [2, 16, 1536, 1536], P(None, 'cp', 'dp'), may hold values from -0.15625 to 0.15625
- w_down: bfloat16 [2, 16, 768, 1536], P(None, 'cp', 'dp'), may hold values from -0.625 to 0.625
Outputs:
- output: float32 [4096, 1536], P(('dp', 'cp'))
- token_grad: float32 [4096, 1536], P(('dp', 'cp'))
- qkv_grad: float32 [2, 2048, 1536], P(None, ('dp', 'cp'))
- out_proj_grad: float32 [2, 1536, 1536], P(None, ('dp', 'cp'))
- router_grad: float32 [2, 1536, 16], P(None, ('dp', 'cp'))
- gains_grad: float32 [2, 1536, 2], P(None, ('dp', 'cp'))
- gate_up_grad: float32 [2, 16, 1536, 1536], P(None, 'cp', 'dp')
- down_grad: float32 [2, 16, 768, 1536], P(None, 'cp', 'dp')
Inputs may be any that keep to these rules, and one draw needn't show every extreme that they name: `routes`: in every layer each token names 4 different experts; among the rows of one device no expert is named by more than 64 tokens, and some device's rows reach that bound. `doc_lengths`: row b lists in order the lengths of the 4 documents packed into group b; they sum to 1024. Document 1 begins within the group's first 128 tokens and ends within its last 128; documents 0, 2 and 3 are shorter than 128. In one group documents 0, 2 and 3 have one token each.
All inputs are finite; a program needn't handle non-finite values.
Results may differ from a plain program's by a relative error of at most 0.033.
Values may be sent and summed in bfloat16 or wider, within the bound.
No kernel may reach another device: no remote copies, remote signals or barrier semaphores. Data moves between devices by JAX's collectives and lax.ppermute only.
A program may use at most 256 MiB of HBM per device.

v0:
```python
import jax
import jax.numpy as jnp
from jax import lax
from jax.sharding import PartitionSpec as P

D = 1536
HEADS = 12
KV_HEADS = 2
HEAD = 128
FF = 768
TOP = 4
EXP_DEV = 2
LAYERS = 2
DOCS = 4
HQ = 1536
KVW = 256
Q_PER_KV = 6


EPSILON = 1e-06
MASKED = -1e30
HIGHEST = lax.Precision.HIGHEST


def inverse_rms(values):
    return lax.rsqrt(jnp.mean(values * values, axis=-1, keepdims=True) + EPSILON)


def norm_backward(values, gain, upstream):
    scale_rows = inverse_rms(values)
    weighted = gain * upstream
    inner_mean = jnp.mean(values * weighted, axis=-1, keepdims=True)
    grad_values = scale_rows * weighted - values * scale_rows * scale_rows * scale_rows * inner_mean
    grad_gain = jnp.sum(values * scale_rows * upstream, axis=0)
    return (grad_values, grad_gain)


def doc_places(token_index, lengths_row):
    starts = jnp.cumsum(lengths_row) - lengths_row
    segment = jnp.sum((token_index[:, None] >= starts[None, 1:]).astype(jnp.int32), axis=1)
    picked = segment[:, None] == jnp.arange(DOCS, dtype=jnp.int32)[None, :]
    offset = jnp.sum(jnp.where(picked, starts[None, :], 0), axis=1)
    return (segment, token_index - offset)


def rope_tables(positions):
    half_width = HEAD // 2
    frequency = jnp.exp(-jnp.log(10000.0) * 2.0 * jnp.arange(half_width, dtype=jnp.float32) / HEAD)
    angles = positions.astype(jnp.float32)[:, None] * frequency[None, :]
    return (jnp.cos(angles)[:, None, :], jnp.sin(angles)[:, None, :])


def rotate(values, cosine, sine_table):
    half_width = values.shape[-1] // 2
    former = values[..., :half_width]
    latter = values[..., half_width:]
    return jnp.concatenate(
        [former * cosine - latter * sine_table, latter * cosine + former * sine_table], axis=-1
    )


def rotate_back(values, cosine, sine_table):
    half_width = values.shape[-1] // 2
    former = values[..., :half_width]
    latter = values[..., half_width:]
    return jnp.concatenate(
        [former * cosine + latter * sine_table, latter * cosine - former * sine_table], axis=-1
    )


def heads_first(values):
    token_rows = values.shape[0]
    shaped = values.reshape(token_rows, KV_HEADS, Q_PER_KV, HEAD).transpose(1, 2, 0, 3)
    return shaped.reshape(KV_HEADS, Q_PER_KV * token_rows, HEAD)


def heads_last(values):
    token_rows = values.shape[1] // Q_PER_KV
    shaped = values.reshape(KV_HEADS, Q_PER_KV, token_rows, HEAD).transpose(2, 0, 1, 3)
    return shaped.reshape(token_rows, HQ)


def route_plan(route_rows, expert_count, capacity):
    row_count = route_rows.shape[0]
    flat_routes = route_rows.reshape(-1)
    matches = (flat_routes[:, None] == jnp.arange(expert_count, dtype=jnp.int32)[None, :]).astype(
        jnp.int32
    )
    earlier = jnp.cumsum(matches, axis=0) - matches
    position = jnp.sum(earlier * matches, axis=1)
    target = flat_routes * capacity + position
    route_total = flat_routes.shape[0]
    source = jnp.full((expert_count * capacity,), route_total, jnp.int32)
    source = source.at[target].set(jnp.arange(route_total, dtype=jnp.int32))
    chosen = matches.reshape(row_count, TOP, expert_count).astype(jnp.float32)
    return (target, source, chosen)


def gate_weights(mixed, router_weight, chosen):
    logits = jnp.dot(mixed, router_weight, preferred_element_type=jnp.float32)
    picked = jnp.sum(logits[:, None, :] * chosen, axis=-1)
    return jax.nn.softmax(picked, axis=-1)


def send_back(values):
    return lax.all_to_all(values, "cp", split_axis=0, concat_axis=0, tiled=True)


def shards(tokens, cotangent, doc_lengths, routes, w_qkv, w_out, router, gains, w_gate_up, w_down):
    row_count = tokens.shape[0]
    cycle_size = lax.axis_size("cp")
    cycle_place = lax.axis_index("cp")
    expert_count = EXP_DEV * cycle_size
    capacity = 2 * row_count * TOP // expert_count
    lengths_row = doc_lengths[0]
    my_index = cycle_place * row_count + jnp.arange(row_count, dtype=jnp.int32)
    my_segment, my_position = doc_places(my_index, lengths_row)
    cosine, sine_table = rope_tables(my_position)
    score_scale = HEAD ** (-0.5)

    def key_mask(key_count):
        key_index = jnp.arange(key_count, dtype=jnp.int32)
        key_segment, unused_position = doc_places(key_index, lengths_row)
        allowed = (my_segment[:, None] == key_segment[None, :]) & (
            key_index[None, :] <= my_index[:, None]
        )
        return jnp.tile(allowed, (Q_PER_KV, 1))

    def project(normed, query_weight):
        joined = jnp.dot(normed, query_weight.T, preferred_element_type=jnp.float32)
        queries = rotate(joined[:, :HQ].reshape(row_count, HEADS, HEAD), cosine, sine_table)
        keys_rot = rotate(
            joined[:, HQ : HQ + KVW].reshape(row_count, KV_HEADS, HEAD), cosine, sine_table
        )
        queries = heads_first(queries.reshape(row_count, HQ).astype(jnp.bfloat16))
        keys_rows = keys_rot.reshape(row_count, KVW).astype(jnp.bfloat16)
        values_rows = joined[:, HQ + KVW :].astype(jnp.bfloat16)
        return (queries, keys_rows, values_rows)

    layer_value = tokens.astype(jnp.float32)
    stored = []
    for layer_index in range(LAYERS):
        attention_set = (
            lax.all_gather(w_qkv[layer_index], ("dp", "cp"), axis=0, tiled=True),
            lax.all_gather(w_out[layer_index], ("dp", "cp"), axis=0, tiled=True),
            lax.all_gather(router[layer_index], ("dp", "cp"), axis=0, tiled=True),
            lax.all_gather(gains[layer_index], ("dp", "cp"), axis=0, tiled=True),
        )
        expert_set = (
            lax.all_gather(w_gate_up[layer_index], "dp", axis=1, tiled=True),
            lax.all_gather(w_down[layer_index], "dp", axis=1, tiled=True),
        )
        route_set = route_plan(routes[layer_index], expert_count, capacity)
        forward_query_weight, forward_output_weight, forward_router_weight, forward_gain_pair = (
            attention_set
        )
        forward_gate_up_weight, forward_down_weight = expert_set
        forward_target, forward_source, forward_chosen = route_set
        forward_first_gain = forward_gain_pair[:, 0].astype(jnp.float32)
        forward_second_gain = forward_gain_pair[:, 1].astype(jnp.float32)
        forward_normed = (layer_value * inverse_rms(layer_value) * forward_first_gain).astype(
            jnp.bfloat16
        )
        forward_queries, forward_keys_rows, forward_values_rows = project(
            forward_normed, forward_query_weight
        )
        attend_query_rows = forward_queries.shape[1]
        top_score = jnp.full((KV_HEADS, attend_query_rows), MASKED, jnp.float32)
        fold_key_piece = lax.all_gather(forward_keys_rows, "cp", axis=0, tiled=True)
        fold_value_piece = lax.all_gather(forward_values_rows, "cp", axis=0, tiled=True)
        fold_key_count = fold_key_piece.shape[0]
        fold_key_heads = fold_key_piece.reshape(fold_key_count, KV_HEADS, HEAD)
        fold_value_heads = fold_value_piece.reshape(fold_key_count, KV_HEADS, HEAD)
        fold_scores = (
            jnp.einsum(
                "kqh,nkh->kqn", forward_queries, fold_key_heads, preferred_element_type=jnp.float32
            )
            * score_scale
        )
        fold_allowed = key_mask(fold_key_count)[None]
        fold_scores = jnp.where(fold_allowed, fold_scores, MASKED)
        new_top = jnp.maximum(top_score, jnp.max(fold_scores, axis=-1))
        weights = jnp.where(fold_allowed, jnp.exp(fold_scores - new_top[..., None]), 0.0)
        total_weight = jnp.sum(weights, axis=-1)
        weighted = jnp.einsum(
            "kqn,nkh->kqh",
            weights.astype(jnp.bfloat16),
            fold_value_heads,
            preferred_element_type=jnp.float32,
        )
        top_score, total_weight, weighted = (new_top, total_weight, weighted)
        forward_attended = heads_last(weighted / total_weight[..., None])
        forward_log_total = top_score + jnp.log(total_weight)
        forward_attended_low = forward_attended.astype(jnp.bfloat16)
        forward_middle = layer_value + jnp.dot(
            forward_attended_low, forward_output_weight, preferred_element_type=jnp.float32
        )
        forward_mixed = (forward_middle * inverse_rms(forward_middle) * forward_second_gain).astype(
            jnp.bfloat16
        )
        forward_gate_values = gate_weights(forward_mixed, forward_router_weight, forward_chosen)
        forward_padded = jnp.concatenate([forward_mixed, jnp.zeros((1, D), jnp.bfloat16)], axis=0)
        forward_outgoing = forward_padded[forward_source // TOP].reshape(
            cycle_size, EXP_DEV, capacity, D
        )
        run_arrived = lax.all_to_all(
            forward_outgoing, "cp", split_axis=0, concat_axis=0, tiled=True
        )
        run_gate_up = jnp.einsum(
            "sjcd,jdf->sjcf",
            run_arrived,
            forward_gate_up_weight,
            preferred_element_type=jnp.float32,
        )
        run_hidden = (jax.nn.silu(run_gate_up[..., :FF]) * run_gate_up[..., FF:]).astype(
            jnp.bfloat16
        )
        produced = jnp.einsum(
            "sjcf,jfd->sjcd", run_hidden, forward_down_weight, preferred_element_type=jnp.float32
        ).astype(jnp.bfloat16)
        returned = lax.all_to_all(produced, "cp", split_axis=0, concat_axis=0, tiled=True)
        forward_expert_rows = returned.reshape(expert_count * capacity, D)[forward_target].reshape(
            row_count, TOP, D
        )
        result = forward_middle + jnp.sum(
            forward_gate_values[..., None] * forward_expert_rows.astype(jnp.float32), axis=1
        )
        kept_state = (
            forward_attended,
            forward_log_total,
            forward_expert_rows,
            run_arrived,
            forward_middle,
        )
        stored.append((layer_value, kept_state, attention_set, expert_set, route_set))
        layer_value = result
    upstream = cotangent.astype(jnp.float32)
    attention_grads = []
    expert_grads = []
    for layer_index in reversed(range(LAYERS)):
        layer_input, kept_state, attention_set, expert_set, route_set = stored[layer_index]
        attention_set = (
            lax.all_gather(w_qkv[layer_index], ("dp", "cp"), axis=0, tiled=True),
            lax.all_gather(w_out[layer_index], ("dp", "cp"), axis=0, tiled=True),
            lax.all_gather(router[layer_index], ("dp", "cp"), axis=0, tiled=True),
            lax.all_gather(gains[layer_index], ("dp", "cp"), axis=0, tiled=True),
        )
        expert_set = (
            lax.all_gather(w_gate_up[layer_index], "dp", axis=1, tiled=True),
            lax.all_gather(w_down[layer_index], "dp", axis=1, tiled=True),
        )
        attended, backward_log_total, expert_rows, arrived_all, middle = kept_state
        backward_query_weight, output_weight, router_weight, gain_pair = attention_set
        gate_up_weight, down_weight = expert_set
        target, source, chosen = route_set
        first_gain = gain_pair[:, 0].astype(jnp.float32)
        second_gain = gain_pair[:, 1].astype(jnp.float32)
        backward_normed = (layer_input * inverse_rms(layer_input) * first_gain).astype(jnp.bfloat16)
        backward_queries, backward_keys_rows, backward_values_rows = project(
            backward_normed, backward_query_weight
        )
        attended_low = attended.astype(jnp.bfloat16)
        mixed = (middle * inverse_rms(middle) * second_gain).astype(jnp.bfloat16)
        gate_values = gate_weights(mixed, router_weight, chosen)
        grad_gates = jnp.sum(upstream[:, None, :] * expert_rows.astype(jnp.float32), axis=-1)
        grad_picked = gate_values * (
            grad_gates - jnp.sum(gate_values * grad_gates, axis=-1, keepdims=True)
        )
        grad_logits = jnp.sum(grad_picked[..., None] * chosen, axis=1)
        grad_router = jnp.dot(mixed.astype(jnp.float32).T, grad_logits, precision=HIGHEST)
        grad_mixed = jnp.dot(grad_logits, router_weight.astype(jnp.float32).T, precision=HIGHEST)
        route_grads = (
            (gate_values[..., None] * upstream[:, None, :])
            .astype(jnp.bfloat16)
            .reshape(row_count * TOP, D)
        )
        route_padded = jnp.concatenate([route_grads, jnp.zeros((1, D), jnp.bfloat16)], axis=0)
        grad_outgoing = route_padded[source].reshape(cycle_size, EXP_DEV, capacity, D)
        padded = jnp.concatenate([mixed, jnp.zeros((1, D), jnp.bfloat16)], axis=0)
        outgoing = padded[source // TOP].reshape(cycle_size, EXP_DEV, capacity, D)
        arrived = lax.all_to_all(outgoing, "cp", split_axis=0, concat_axis=0, tiled=True)
        arrived_grads = lax.all_to_all(grad_outgoing, "cp", split_axis=0, concat_axis=0, tiled=True)
        gate_up = jnp.einsum(
            "sjcd,jdf->sjcf", arrived, gate_up_weight, preferred_element_type=jnp.float32
        )
        gate_part = gate_up[..., :FF]
        up_part = gate_up[..., FF:]
        logistic = jax.nn.sigmoid(gate_part)
        activated = jax.nn.silu(gate_part)
        hidden = (activated * up_part).astype(jnp.bfloat16)
        grad_hidden = jnp.einsum(
            "sjcd,jfd->sjcf", arrived_grads, down_weight, preferred_element_type=jnp.float32
        )
        grad_gate = grad_hidden * up_part * logistic * (1.0 + gate_part * (1.0 - logistic))
        grad_up = grad_hidden * activated
        grad_gate_up = jnp.concatenate([grad_gate, grad_up], axis=-1).astype(jnp.bfloat16)
        grad_arrived = jnp.einsum(
            "sjcf,jdf->sjcd", grad_gate_up, gate_up_weight, preferred_element_type=jnp.float32
        ).astype(jnp.bfloat16)
        grad_back, grad_gate_up, hidden, arrived, arrived_grads = (
            send_back(grad_arrived),
            grad_gate_up,
            hidden,
            arrived,
            arrived_grads,
        )
        grad_gate_up_weight = jnp.einsum(
            "sjcd,sjcf->jdf", arrived, grad_gate_up, preferred_element_type=jnp.float32
        )
        grad_down_weight = jnp.einsum(
            "sjcf,sjcd->jfd", hidden, arrived_grads, preferred_element_type=jnp.float32
        )
        grad_routes = grad_back.reshape(expert_count * capacity, D)[target].reshape(
            row_count, TOP, D
        )
        grad_mixed = grad_mixed + jnp.sum(grad_routes.astype(jnp.float32), axis=1)
        grad_middle, grad_second_gain = norm_backward(middle, second_gain, grad_mixed)
        grad_middle = grad_middle + upstream
        grad_middle_low = grad_middle.astype(jnp.bfloat16)
        grad_output_weight = jnp.dot(
            attended_low.T, grad_middle_low, preferred_element_type=jnp.float32
        )
        grad_attended = jnp.dot(
            grad_middle_low, output_weight.T, preferred_element_type=jnp.float32
        ).astype(jnp.bfloat16)
        backward_grad_heads = heads_first(grad_attended)
        backward_row_delta = jnp.sum(
            backward_grad_heads.astype(jnp.float32) * heads_first(attended), axis=-1
        )
        key_piece = lax.all_gather(backward_keys_rows, "cp", axis=0, tiled=True)
        value_piece = lax.all_gather(backward_values_rows, "cp", axis=0, tiled=True)
        attend_key_count = key_piece.shape[0]
        key_heads = key_piece.reshape(attend_key_count, KV_HEADS, HEAD)
        value_heads = value_piece.reshape(attend_key_count, KV_HEADS, HEAD)
        scores = (
            jnp.einsum(
                "kqh,nkh->kqn", backward_queries, key_heads, preferred_element_type=jnp.float32
            )
            * score_scale
        )
        attend_allowed = key_mask(attend_key_count)[None]
        scores = jnp.where(attend_allowed, scores, MASKED)
        probs = jnp.where(attend_allowed, jnp.exp(scores - backward_log_total[..., None]), 0.0)
        grad_probs = jnp.einsum(
            "kqh,nkh->kqn", backward_grad_heads, value_heads, preferred_element_type=jnp.float32
        )
        grad_scores = (probs * (grad_probs - backward_row_delta[..., None])).astype(jnp.bfloat16)
        grad_queries = (
            jnp.einsum("kqn,nkh->kqh", grad_scores, key_heads, preferred_element_type=jnp.float32)
            * score_scale
        )
        grad_keys = (
            jnp.einsum(
                "kqn,kqh->nkh", grad_scores, backward_queries, preferred_element_type=jnp.float32
            )
            * score_scale
        )
        grad_values = jnp.einsum(
            "kqn,kqh->nkh",
            probs.astype(jnp.bfloat16),
            backward_grad_heads,
            preferred_element_type=jnp.float32,
        )
        block_terms = jnp.concatenate(
            [grad_keys.reshape(attend_key_count, KVW), grad_values.reshape(attend_key_count, KVW)],
            axis=1,
        )
        grad_keys_values = block_terms
        grad_queries, grad_keys_values = (grad_queries, grad_keys_values)
        mine_kv = lax.psum_scatter(
            grad_keys_values.astype(jnp.bfloat16), "cp", scatter_dimension=0, tiled=True
        ).astype(jnp.float32)
        backward_grad_queries = heads_last(grad_queries)
        grad_query_rot = rotate_back(
            backward_grad_queries.reshape(row_count, HEADS, HEAD), cosine, sine_table
        ).reshape(row_count, HQ)
        grad_key_rot = rotate_back(
            mine_kv[:, :KVW].reshape(row_count, KV_HEADS, HEAD), cosine, sine_table
        ).reshape(row_count, KVW)
        grad_joined = jnp.concatenate(
            [grad_query_rot, grad_key_rot, mine_kv[:, KVW:]], axis=1
        ).astype(jnp.bfloat16)
        grad_query_weight = jnp.dot(
            grad_joined.T, backward_normed, preferred_element_type=jnp.float32
        )
        grad_normed = jnp.dot(
            grad_joined, backward_query_weight, preferred_element_type=jnp.float32
        )
        grad_input, grad_first_gain = norm_backward(layer_input, first_gain, grad_normed)
        grad_input = grad_input + grad_middle
        grad_gain_pair = jnp.stack([grad_first_gain, grad_second_gain], axis=1)
        attention_terms = (grad_query_weight, grad_output_weight, grad_router, grad_gain_pair)
        upstream, attention_terms, expert_terms = (
            grad_input,
            attention_terms,
            (grad_gate_up_weight, grad_down_weight),
        )
        attention_grads.insert(
            0,
            (
                lax.psum_scatter(attention_terms[0], ("dp", "cp"), scatter_dimension=0, tiled=True),
                lax.psum_scatter(attention_terms[1], ("dp", "cp"), scatter_dimension=0, tiled=True),
                lax.psum_scatter(attention_terms[2], ("dp", "cp"), scatter_dimension=0, tiled=True),
                lax.psum_scatter(attention_terms[3], ("dp", "cp"), scatter_dimension=0, tiled=True),
            ),
        )
        expert_grads.insert(
            0,
            (
                lax.psum_scatter(
                    expert_terms[0].astype(jnp.bfloat16), "dp", scatter_dimension=1, tiled=True
                ).astype(jnp.float32),
                lax.psum_scatter(
                    expert_terms[1].astype(jnp.bfloat16), "dp", scatter_dimension=1, tiled=True
                ).astype(jnp.float32),
            ),
        )
    qkv_grad = jnp.stack([grads_entry[0] for grads_entry in attention_grads])
    out_proj_grad = jnp.stack([grads_entry[1] for grads_entry in attention_grads])
    router_grad = jnp.stack([grads_entry[2] for grads_entry in attention_grads])
    gains_grad = jnp.stack([grads_entry[3] for grads_entry in attention_grads])
    gate_up_grad = jnp.stack([grads_entry[0] for grads_entry in expert_grads])
    down_grad = jnp.stack([grads_entry[1] for grads_entry in expert_grads])
    return (
        layer_value,
        upstream,
        qkv_grad,
        out_proj_grad,
        router_grad,
        gains_grad,
        gate_up_grad,
        down_grad,
    )


def solution(mesh):
    return jax.shard_map(
        shards,
        mesh=mesh,
        in_specs=(
            P(("dp", "cp"), None),
            P(("dp", "cp"), None),
            P("dp", None),
            P(None, ("dp", "cp"), None),
            P(None, ("dp", "cp"), None),
            P(None, ("dp", "cp"), None),
            P(None, ("dp", "cp"), None),
            P(None, ("dp", "cp"), None),
            P(None, "cp", "dp", None),
            P(None, "cp", "dp", None),
        ),
        out_specs=(
            P(("dp", "cp"), None),
            P(("dp", "cp"), None),
            P(None, ("dp", "cp"), None),
            P(None, ("dp", "cp"), None),
            P(None, ("dp", "cp"), None),
            P(None, ("dp", "cp"), None),
            P(None, "cp", "dp", None),
            P(None, "cp", "dp", None),
        ),
        check_vma=False,
    )
```

profile of v0, /device:TPU:0, one launch (start us, length us, event | category | flops | bytes accessed | tf_op | source)
XLA Modules:
  0.0 2601.4 jit_solution(9077691069251541113)
XLA Ops:
  22.7 50.0 %all-gather = bf16[1,1536,2]{2,0,1:T(2,128)(2,1)S(1)} all-gather(bf16[1,48,2]{2,0,1:T(2,128)(2,1)S(1)} %copy.394), channel_id=2, replica_groups=mesh['dp'=4,'cp'=8] {'dp','cp'}, dimensions={1}, use_global_device_ids=true | all-gather | bytes 6336 | tf_op jit(solution)/shard_map/all_gather | solution.py:147
  78.5 7.1 all-gather.21.cloned.1.call-done
  91.4 14.3 all_gather.66
  108.2 16.1 all_gather.67
  129.5 22.0 all-gather.23.cloned.1.call-done
  155.9 5.6 gather_fusion
  165.2 84.0 %all-gather.25.cloned.1.call-done = bf16[1,2,1536,1536]{3,2,1,0:T(8,128)(2,1)} async-done(((bf16[1,2,384,1536]{3,2,1,0:T(8,128)(2,1)}), bf16[1,2,1536,1536]{3,2,1,0:T(8,128)(2,1)}) %all-gather.25.cloned.1.call-update) | async-done | bytes 9437200 | tf_op jit(solution)/shard_map/all_gather | solution.py:150
  249.2 8.7 fusion.41
  262.8 45.2 %all-gather.27.cloned.1.call-done = bf16[1,2,768,1536]{3,2,1,0:T(8,128)(2,1)} async-done(((bf16[1,2,192,1536]{3,2,1,0:T(8,128)(2,1)}), bf16[1,2,768,1536]{3,2,1,0:T(8,128)(2,1)}) %all-gather.27.cloned.1.call-update) | async-done | bytes 4718608 | tf_op jit(solution)/shard_map/all_gather | solution.py:151
  325.3 134.1 %all-gather.3 = bf16[1,1536,16]{2,0,1:T(2,128)(2,1)} all-gather(bf16[1,48,16]{2,0,1:T(2,128)(2,1)} %copy.395), channel_id=5, replica_groups=mesh['dp'=4,'cp'=8] {'dp','cp'}, dimensions={1}, use_global_device_ids=true | all-gather | bytes 50688 | tf_op jit(solution)/shard_map/all_gather | solution.py:146
  463.5 46.2 %all-gather.6 = bf16[1,1536,2]{2,0,1:T(2,128)(2,1)} all-gather(bf16[1,48,2]{2,0,1:T(2,128)(2,1)} %copy.396), channel_id=8, replica_groups=mesh['dp'=4,'cp'=8] {'dp','cp'}, dimensions={1}, use_global_device_ids=true | all-gather | bytes 6336 | tf_op jit(solution)/shard_map/all_gather | solution.py:147
  546.7 14.2 all_gather.74
  562.5 15.4 all_gather.75
  587.6 5.6 gather_fusion.2
  598.7 103.8 %all-gather.9 = bf16[1,1536,16]{2,0,1:T(2,128)(2,1)S(1)} all-gather(bf16[1,48,16]{2,0,1:T(2,128)(2,1)S(1)} %copy.397), channel_id=11, replica_groups=mesh['dp'=4,'cp'=8] {'dp','cp'}, dimensions={1}, use_global_device_ids=true | all-gather | bytes 50688 | tf_op jit(solution)/shard_map/all_gather | solution.py:146
  713.0 5.6 gather_fusion.4
  722.3 11.1 fusion.38
  733.4 60.3 %all-to-all-done.4 = bf16[8,2,64,1536]{3,2,1,0:T(8,128)(2,1)S(1)} async-done(((bf16[8,2,64,1536]{3,2,1,0:T(8,128)(2,1)}), bf16[8,2,64,1536]{3,2,1,0:T(8,128)(2,1)S(1)}, u32[]{:S(2)}, u32[]{:S(2)}) %all-to-all-start.4) | async-done | bytes 3145760 | tf_op jit(solution)/shard_map/all_to_all | solution.py:282
  793.7 9.3 fusion.76
  811.6 8.6 fusion.61
  822.2 60.9 %all-to-all-done.3 = bf16[8,2,64,1536]{3,2,1,0:T(8,128)(2,1)S(1)} async-done(((bf16[8,2,64,1536]{3,2,1,0:T(8,128)(2,1)}), bf16[8,2,64,1536]{3,2,1,0:T(8,128)(2,1)S(1)}, u32[]{:S(2)}, u32[]{:S(2)}) %all-to-all-start.3) | async-done | bytes 3145760 | tf_op jit(solution)/shard_map/all_to_all | solution.py:221
  892.0 6.8 gather_fusion.3
  912.4 47.5 %all-to-all-done.5 = bf16[8,2,64,1536]{3,2,1,0:T(8,128)(2,1)S(1)} async-done(((bf16[8,2,64,1536]{3,2,1,0:T(8,128)(2,1)}), bf16[8,2,64,1536]{3,2,1,0:T(8,128)(2,1)S(1)}, u32[]{:S(2)}, u32[]{:S(2)}) %all-to-all-start.5) | async-done | bytes 3145760 | tf_op jit(solution)/shard_map/all_to_all | solution.py:106
  997.3 26.7 %reduce-scatter.43.cloned.1.call-done = bf16[128,512]{1,0:T(8,128)(2,1)} async-done(((bf16[1024,512]{1,0:T(8,128)(2,1)}), bf16[128,512]{1,0:T(8,128)(2,1)}) %reduce-scatter.43.cloned.1.call-update) | async-done | bytes 131088
  1037.8 5.5 gather_fusion.6
  1043.4 75.3 %all_to_all.42 = bf16[8,2,64,1536]{3,2,1,0:T(8,128)(2,1)S(1)} all-to-all(bf16[8,2,64,1536]{3,2,1,0:T(8,128)(2,1)} %bitcast.369), channel_id=1, replica_groups=mesh['dp'=4,'cp'=8] {'cp'}, dimensions={0} | all-to-all | bytes 6291456 | tf_op jit(solution)/shard_map/all_to_all | solution.py:282
  1118.7 7.9 fusion.72
  1141.6 67.7 %all-to-all-done.7 = bf16[8,2,64,1536]{3,2,1,0:T(8,128)(2,1)S(1)} async-done(((bf16[8,2,64,1536]{3,2,1,0:T(8,128)(2,1)}), bf16[8,2,64,1536]{3,2,1,0:T(8,128)(2,1)S(1)}, u32[]{:S(2)}, u32[]{:S(2)}) %all-to-all-start.7) | async-done | bytes 3145760 | tf_op jit(solution)/shard_map/all_to_all | solution.py:106
  1254.8 18.1 reduce-scatter.45.cloned.1.call-done
  1280.6 7.2 bitcast_convert_fusion.2
  1287.9 7.2 bitcast_convert_fusion.3
  1308.1 9.8 bitcast_convert_fusion
  1318.1 9.9 bitcast_convert_fusion.1
  1329.2 7.3 fusion.147
  1337.3 6.5 fusion.146
  1343.9 28.5 %reduce-scatter.49.cloned.1.call-done = f32[48,16]{1,0:T(8,128)} async-done(((f32[1536,16]{1,0:T(8,128)}), f32[48,16]{1,0:T(8,128)}) %reduce-scatter.49.cloned.1.call-update) | async-done | bytes 3088
  1373.2 98.7 %reduce-scatter.53.cloned.1.call-done = f32[48,2]{1,0:T(8,128)} async-done(((f32[1536,2]{1,0:T(8,128)}), f32[48,2]{1,0:T(8,128)}) %reduce-scatter.53.cloned.1.call-update) | async-done | bytes 400
  1472.7 98.9 %reduce-scatter.47.cloned.1.call-done = f32[48,16]{1,0:T(8,128)} async-done(((f32[1536,16]{1,0:T(8,128)}), f32[48,16]{1,0:T(8,128)}) %reduce-scatter.47.cloned.1.call-update) | async-done | bytes 3088
  1574.2 96.9 %reduce-scatter.51.cloned.1.call-done = f32[48,2]{1,0:T(8,128)} async-done(((f32[1536,2]{1,0:T(8,128)}), f32[48,2]{1,0:T(8,128)}) %reduce-scatter.51.cloned.1.call-update) | async-done | bytes 400
  1672.5 58.2 %reduce-scatter.41.cloned.1.call-done = bf16[2,192,1536]{2,1,0:T(8,128)(2,1)} async-done(((bf16[2,768,1536]{2,1,0:T(8,128)(2,1)}), bf16[2,192,1536]{2,1,0:T(8,128)(2,1)}) %reduce-scatter.41.cloned.1.call-update) | async-done | bytes 1179664 | tf_op jit(solution)/shard_map/reduce_scatter | solution.py:413
  1730.7 59.9 %reduce-scatter.39.cloned.1.call-done = bf16[2,192,1536]{2,1,0:T(8,128)(2,1)} async-done(((bf16[2,768,1536]{2,1,0:T(8,128)(2,1)}), bf16[2,192,1536]{2,1,0:T(8,128)(2,1)}) %reduce-scatter.39.cloned.1.call-update) | async-done | bytes 1179664 | tf_op jit(solution)/shard_map/reduce_scatter | solution.py:413
  1794.7 137.7 %reduce-scatter.33.cloned.1.call-done = f32[48,1536]{1,0:T(8,128)} async-done(((f32[1536,1536]{1,0:T(8,128)}), f32[48,1536]{1,0:T(8,128)}) %reduce-scatter.33.cloned.1.call-update) | async-done | bytes 294928 | tf_op jit(solution)/shard_map/reduce_scatter | solution.py:402
  1932.5 141.4 %reduce-scatter.31.cloned.1.call-done = f32[48,1536]{1,0:T(8,128)} async-done(((f32[1536,1536]{1,0:T(8,128)}), f32[48,1536]{1,0:T(8,128)}) %reduce-scatter.31.cloned.1.call-update) | async-done | bytes 294928 | tf_op jit(solution)/shard_map/reduce_scatter | solution.py:402
  2075.7 95.4 %reduce-scatter.37.cloned.1.call-done = bf16[2,384,1536]{2,1,0:T(8,128)(2,1)} async-done(((bf16[2,1536,1536]{2,1,0:T(8,128)(2,1)}), bf16[2,384,1536]{2,1,0:T(8,128)(2,1)}) %reduce-scatter.37.cloned.1.call-update) | async-done | bytes 2359312 | tf_op jit(solution)/shard_map/reduce_scatter | solution.py:410
  2171.1 98.0 %reduce-scatter.35.cloned.1.call-done = bf16[2,384,1536]{2,1,0:T(8,128)(2,1)} async-done(((bf16[2,1536,1536]{2,1,0:T(8,128)(2,1)}), bf16[2,384,1536]{2,1,0:T(8,128)(2,1)}) %reduce-scatter.35.cloned.1.call-update) | async-done | bytes 2359312 | tf_op jit(solution)/shard_map/reduce_scatter | solution.py:410
  2269.1 6.7 maximum_convert_fusion
  2275.9 154.7 %reduce-scatter.29.cloned.1.call-done = f32[64,1536]{1,0:T(8,128)} async-done(((f32[2048,1536]{1,0:T(8,128)}), f32[64,1536]{1,0:T(8,128)}) %reduce-scatter.29.cloned.1.call-update) | async-done | bytes 393232 | tf_op jit(solution)/shard_map/reduce_scatter | solution.py:401
  2430.5 161.5 %reduce-scatter.27.cloned.1.call-done = f32[64,1536]{1,0:T(8,128)} async-done(((f32[2048,1536]{1,0:T(8,128)}), f32[64,1536]{1,0:T(8,128)}) %reduce-scatter.27.cloned.1.call-update) | async-done | bytes 393232 | tf_op jit(solution)/shard_map/reduce_scatter | solution.py:401
  (565 shorter events, 316.2 us)
Async XLA Ops:
  7.2 78.4 %all-gather.21.cloned.1.call-start = ((), (), s32[]{:S(2)}) async-start(), calls=%async_computation.30 | async-start | bytes 6488064 | tf_op jit(solution)/shard_map/all_gather | solution.py:144
  9.0 142.5 %all-gather.23.cloned.1.call-start = ((), (), s32[]{:S(2)}) async-start(), calls=%async_computation.31 | async-start | bytes 4866048 | tf_op jit(solution)/shard_map/all_gather | solution.py:145
  10.8 238.3 %all-gather.25.cloned.1.call-start = ((), (), s32[]{:S(2)}) async-start(), calls=%async_computation.32 | async-start | bytes 11796480 | tf_op jit(solution)/shard_map/all_gather | solution.py:150
  15.8 57.5 %copy-start.8 = (bf16[128,1536]{1,0:T(8,128)(2,1)S(1)}, bf16[128,1536]{1,0:T(8,128)(2,1)}, u32[]{:S(2)}) copy-start(bf16[128,1536]{1,0:T(8,128)(2,1)} %param.10) | copy-start | bytes 1179652
  15.8 292.2 %all-gather.27.cloned.1.call-start = ((), (), s32[]{:S(2)}) async-start(), calls=%async_computation.33 | async-start | bytes 5898240 | tf_op jit(solution)/shard_map/all_gather | solution.py:151
  19.0 520.9 %all-gather.29.cloned.1.call-start = ((), (), s32[]{:S(2)}) async-start(), calls=%async_computation.34 | async-start | bytes 6488064 | tf_op jit(solution)/shard_map/all_gather | solution.py:144
  19.6 563.6 %all-gather.31.cloned.1.call-start = ((), (), s32[]{:S(2)}) async-start(), calls=%async_computation.35 | async-start | bytes 4866048 | tf_op jit(solution)/shard_map/all_gather | solution.py:145
  21.9 84.0 %copy-start.56 = (f32[128,64]{0,1:T(8,128)}, f32[128,64]{0,1:T(8,128)S(1)}, u32[]{:S(2)}) copy-start(f32[128,64]{0,1:T(8,128)S(1)} %get-tuple-element.81) | copy-start | bytes 98308
  21.9 84.0 %copy-start.60 = (f32[128,64]{0,1:T(8,128)}, f32[128,64]{0,1:T(8,128)S(1)}, u32[]{:S(2)}) copy-start(f32[128,64]{0,1:T(8,128)S(1)} %get-tuple-element.82) | copy-start | bytes 98308
  22.0 68.8 %copy-start.44 = (f32[128,64]{1,0:T(8,128)}, f32[128,64]{1,0:T(8,128)S(1)}, u32[]{:S(2)}) copy-start(f32[128,64]{1,0:T(8,128)S(1)} %copy.300) | copy-start | bytes 98308
  22.1 68.7 %copy-start.48 = (f32[128,64]{1,0:T(8,128)}, f32[128,64]{1,0:T(8,128)S(1)}, u32[]{:S(2)}) copy-start(f32[128,64]{1,0:T(8,128)S(1)} %copy.301) | copy-start | bytes 98308
  73.3 81.5 %copy-start.82 = (f32[1536]{0:T(1024)}, f32[1536]{0:T(1024)S(1)}, u32[]{:S(2)}) copy-start(f32[1536]{0:T(1024)S(1)} %get-tuple-element.20) | copy-start | bytes 18436
  155.8 371.0 %copy-start.27 = (bf16[128,1536]{1,0:T(8,128)(2,1)}, bf16[128,1536]{1,0:T(8,128)(2,1)S(1)}, u32[]{:S(2)}) copy-start(bf16[128,1536]{1,0:T(8,128)(2,1)S(1)} %multiply_convert_fusion.8) | copy-start | bytes 1179652
  161.4 87.7 %all-to-all-start = ((bf16[8,2,64,1536]{3,2,1,0:T(8,128)(2,1)}), bf16[8,2,64,1536]{3,2,1,0:T(8,128)(2,1)S(1)}, u32[]{:S(2)}, u32[]{:S(2)}) async-start(bf16[8,2,64,1536]{3,2,1,0:T(8,128)(2,1)} %bitcast.368), calls=%async_computation | async-start | bytes 6291456 | tf_op jit(solution)/shard_map/all_to_all | solution.py:206
  315.3 214.5 %all-to-all-start.1 = ((bf16[8,2,64,1536]{3,2,1,0:T(8,128)(2,1)}), bf16[8,2,64,1536]{3,2,1,0:T(8,128)(2,1)S(1)}, u32[]{:S(2)}, u32[]{:S(2)}) async-start(bf16[8,2,64,1536]{3,2,1,0:T(8,128)(2,1)} %copy.314), calls=%async_computation.1 | async-start | bytes 6291456 | tf_op jit(solution)/shard_map/all_to_all | solution.py:221
  319.9 402.3 %all-gather.33.cloned.1.call-start = ((), (), s32[]{:S(2)}) async-start(), calls=%async_computation.36 | async-start | bytes 11796480 | tf_op jit(solution)/shard_map/all_gather | solution.py:150
  539.9 43.3 %copy-start.1 = (f32[128,1536]{1,0:T(8,128)}, f32[128,1536]{1,0:T(8,128)S(1)}, u32[]{:S(2)}) copy-start(f32[128,1536]{1,0:T(8,128)S(1)} %get-tuple-element.23) | copy-start | bytes 2359300
  587.6 121.7 %copy-start.29 = (bf16[128,1536]{1,0:T(8,128)(2,1)}, bf16[128,1536]{1,0:T(8,128)(2,1)S(1)}, u32[]{:S(2)}) copy-start(bf16[128,1536]{1,0:T(8,128)(2,1)S(1)} %multiply_convert_fusion.6) | copy-start | bytes 1179652
  593.2 110.8 %copy-start.36 = (bf16[128,1536]{1,0:T(8,128)(2,1)S(1)}, bf16[128,1536]{1,0:T(8,128)(2,1)}, u32[]{:S(2)}) copy-start(bf16[128,1536]{1,0:T(8,128)(2,1)} %param.11) | copy-start | bytes 1179652
  593.2 125.4 %all-to-all-start.2 = ((bf16[8,2,64,1536]{3,2,1,0:T(8,128)(2,1)}), bf16[8,2,64,1536]{3,2,1,0:T(8,128)(2,1)}, u32[]{:S(2)}, u32[]{:S(2)}) async-start(bf16[8,2,64,1536]{3,2,1,0:T(8,128)(2,1)} %bitcast.366), calls=%async_computation.2 | async-start | bytes 6291456 | tf_op jit(solution)/shard_map/all_to_all | solution.py:206
  597.8 135.6 %all-gather.35.cloned.1.call-start = ((), (), s32[]{:S(2)}) async-start(), calls=%async_computation.37 | async-start | bytes 5898240 | tf_op jit(solution)/shard_map/all_gather | solution.py:151
  718.6 75.1 %all-to-all-start.4 = ((bf16[8,2,64,1536]{3,2,1,0:T(8,128)(2,1)}), bf16[8,2,64,1536]{3,2,1,0:T(8,128)(2,1)S(1)}, u32[]{:S(2)}, u32[]{:S(2)}) async-start(bf16[8,2,64,1536]{3,2,1,0:T(8,128)(2,1)} %bitcast.367), calls=%async_computation.4 | async-start | bytes 6291456 | tf_op jit(solution)/shard_map/all_to_all | solution.py:282
  807.8 75.3 %all-to-all-start.3 = ((bf16[8,2,64,1536]{3,2,1,0:T(8,128)(2,1)}), bf16[8,2,64,1536]{3,2,1,0:T(8,128)(2,1)S(1)}, u32[]{:S(2)}, u32[]{:S(2)}) async-start(bf16[8,2,64,1536]{3,2,1,0:T(8,128)(2,1)} %copy.331), calls=%async_computation.3 | async-start | bytes 6291456 | tf_op jit(solution)/shard_map/all_to_all | solution.py:221
  822.2 66.2 %copy-start.37 = (bf16[128,1536]{1,0:T(8,128)(2,1)S(1)}, bf16[128,1536]{1,0:T(8,128)(2,1)}, u32[]{:S(2)}) copy-start(bf16[128,1536]{1,0:T(8,128)(2,1)} %param.11) | copy-start | bytes 1179652
  884.7 75.1 %all-to-all-start.5 = ((bf16[8,2,64,1536]{3,2,1,0:T(8,128)(2,1)}), bf16[8,2,64,1536]{3,2,1,0:T(8,128)(2,1)S(1)}, u32[]{:S(2)}, u32[]{:S(2)}) async-start(bf16[8,2,64,1536]{3,2,1,0:T(8,128)(2,1)} %copy.336), calls=%async_computation.5 | async-start | bytes 6291456 | tf_op jit(solution)/shard_map/all_to_all | solution.py:106
  888.4 135.6 %reduce-scatter.43.cloned.1.call-start = ((), (), s32[]{:S(2)}) async-start(), calls=%async_computation.38 | async-start | bytes 1179648
  996.5 28.7 %copy-start.46 = (f32[128,64]{1,0:T(8,128)S(1)}, f32[128,64]{1,0:T(8,128)}, u32[]{:S(2)}) copy-start(f32[128,64]{1,0:T(8,128)} %copy-done.44) | copy-start | bytes 98308
  996.6 29.3 %copy-start.2 = (f32[128,1536]{1,0:T(8,128)S(1)}, f32[128,1536]{1,0:T(8,128)}, u32[]{:S(2)}) copy-start(f32[128,1536]{1,0:T(8,128)} %copy-done.1) | copy-start | bytes 2359300
  996.6 29.3 %copy-start.108 = (f32[128]{0:T(128)S(1)}, f32[128]{0:T(128)}, u32[]{:S(2)}) copy-start(f32[128]{0:T(128)} %copy-done.107) | copy-start | bytes 1540
  997.3 33.3 %copy-start.34 = (bf16[128,12,128]{0,2,1:T(8,128)(2,1)}, bf16[128,12,128]{0,2,1:T(8,128)(2,1)S(1)}, u32[]{:S(2)}) copy-start(bf16[128,12,128]{0,2,1:T(8,128)(2,1)S(1)} %pad_maximum_fusion.10) | copy-start | bytes 1179652
  1043.4 83.3 %slice-start = ((s8[9437184]{0:T(1024)(128)(4,1)}), s8[4194304]{0:T(1024)(128)(4,1)S(1)}, s32[]{:S(2)}) async-start(s8[9437184]{0:T(1024)(128)(4,1)} %bitcast.440), calls=%async_computation.44 | async-start | bytes 8388608
  1134.0 75.2 %all-to-all-start.7 = ((bf16[8,2,64,1536]{3,2,1,0:T(8,128)(2,1)}), bf16[8,2,64,1536]{3,2,1,0:T(8,128)(2,1)S(1)}, u32[]{:S(2)}, u32[]{:S(2)}) async-start(bf16[8,2,64,1536]{3,2,1,0:T(8,128)(2,1)} %copy.352), calls=%async_computation.7 | async-start | bytes 6291456 | tf_op jit(solution)/shard_map/all_to_all | solution.py:106
  1137.8 71.4 %copy-start.101 = (s32[1024]{0:T(1024)S(1)}, s32[1024]{0:T(1024)}, u32[]{:S(2)}) copy-start(s32[1024]{0:T(1024)} %pad_clamp_fusion.1) | copy-start | bytes 12292
  1137.8 135.1 %reduce-scatter.45.cloned.1.call-start = ((), (), s32[]{:S(2)}) async-start(), calls=%async_computation.39 | async-start | bytes 1179648
  1141.6 78.9 %copy-start.85 = (f32[128,16]{0,1:T(8,128)}, f32[128,16]{0,1:T(8,128)S(1)}, u32[]{:S(2)}) copy-start(f32[128,16]{0,1:T(8,128)S(1)} %multiply_reduce_fusion.15) | copy-start | bytes 24580
  1241.5 130.9 %reduce-scatter.49.cloned.1.call-start = ((), (), s32[]{:S(2)}) async-start(), calls=%async_computation.41 | async-start | bytes 811008
  1245.3 226.6 %reduce-scatter.53.cloned.1.call-start = ((), (), s32[]{:S(2)}) async-start(), calls=%async_computation.43 | async-start | bytes 811008
  1249.3 322.4 %reduce-scatter.47.cloned.1.call-start = ((), (), s32[]{:S(2)}) async-start(), calls=%async_computation.40 | async-start | bytes 811008
  1251.5 419.7 %reduce-scatter.51.cloned.1.call-start = ((), (), s32[]{:S(2)}) async-start(), calls=%async_computation.42 | async-start | bytes 811008
  1280.6 450.1 %reduce-scatter.41.cloned.1.call-start = ((), (), s32[]{:S(2)}) async-start(), calls=%async_computation.29 | async-start | bytes 5898240 | tf_op jit(solution)/shard_map/reduce_scatter | solution.py:413
  1287.9 502.7 %reduce-scatter.39.cloned.1.call-start = ((), (), s32[]{:S(2)}) async-start(), calls=%async_computation.28 | async-start | bytes 5898240 | tf_op jit(solution)/shard_map/reduce_scatter | solution.py:413
  1295.2 637.2 %reduce-scatter.33.cloned.1.call-start = ((), (), s32[]{:S(2)}) async-start(), calls=%async_computation.25 | async-start | bytes 9732096 | tf_op jit(solution)/shard_map/reduce_scatter | solution.py:402
  1301.6 772.3 %reduce-scatter.31.cloned.1.call-start = ((), (), s32[]{:S(2)}) async-start(), calls=%async_computation.24 | async-start | bytes 9732096 | tf_op jit(solution)/shard_map/reduce_scatter | solution.py:402
  1307.8 863.3 %reduce-scatter.37.cloned.1.call-start = ((), (), s32[]{:S(2)}) async-start(), calls=%async_computation.27 | async-start | bytes 11796480 | tf_op jit(solution)/shard_map/reduce_scatter | solution.py:410
  1318.0 951.1 %reduce-scatter.35.cloned.1.call-start = ((), (), s32[]{:S(2)}) async-start(), calls=%async_computation.26 | async-start | bytes 11796480 | tf_op jit(solution)/shard_map/reduce_scatter | solution.py:410
  1327.9 1102.6 %reduce-scatter.29.cloned.1.call-start = ((), (), s32[]{:S(2)}) async-start(), calls=%async_computation.23 | async-start | bytes 12976128 | tf_op jit(solution)/shard_map/reduce_scatter | solution.py:401
  1336.5 1255.5 %reduce-scatter.27.cloned.1.call-start = ((), (), s32[]{:S(2)}) async-start(), calls=%async_computation.22 | async-start | bytes 12976128 | tf_op jit(solution)/shard_map/reduce_scatter | solution.py:401
  1343.9 229.2 %copy-start.122 = (f32[128]{0:T(128)S(1)}, f32[128]{0:T(128)}, u32[]{:S(2)}) copy-start(f32[128]{0:T(128)} %get-tuple-element.17) | copy-start | bytes 1540
  (112 other events, 631.7 us)
Sparse Core Ops, SparseCore 0:
  11.6 73.9 all-gather.20
  89.2 62.3 all-gather.22
  154.0 95.1 all-gather.24
  250.9 57.0 all-gather.26
  311.4 104.8 all-gather.28
  419.7 63.9 all-gather.30
  485.6 96.4 all-gather.32
  600.5 57.6 all-gather.34
  994.2 29.7 reduce-scatter.42
  1241.6 31.2 reduce-scatter.44
  1278.6 93.7 reduce-scatter.48
  1377.4 94.4 reduce-scatter.52
  1477.0 94.5 reduce-scatter.46
  1576.6 94.5 reduce-scatter.50
  1674.5 56.1 reduce-scatter.40
  1733.5 57.0 reduce-scatter.38
  1796.9 135.4 reduce-scatter.32
  1939.2 134.5 reduce-scatter.30
  2076.9 94.1 reduce-scatter.36
  2174.1 95.0 reduce-scatter.34
  2275.2 155.3 reduce-scatter.28
  2437.6 154.4 reduce-scatter.26
where the time goes:
time: 2610 us; the launch traced here: 2600 us
  waiting for transfers between devices  1670 us (64%)
  blocking collectives  469 us (18%)
  matrix products  194 us (7%)
  local copies, waits for them, and re-layouts  148 us (6%)
  other arithmetic  70.7 us (3%)
  starting transfers between devices  29.3 us (1%)
    unnamed x28, waiting for transfers between devices  371 us
    reduce_scatter x2, waiting for transfers between devices, shards(): lax.psum_scatter(attention_terms[0], ('dp', 'cp'), scatter_dimension=0, t...  316 us
    reduce_scatter x2, waiting for transfers between devices, shards(): lax.psum_scatter(attention_terms[1], ('dp', 'cp'), scatter_dimension=0, t...  279 us
    all_gather x2, blocking collectives, shards(): lax.all_gather(router[layer_index], ('dp', 'cp'), axis=0, tiled=True)  238 us
    reduce_scatter x2, waiting for transfers between devices, shards(): lax.psum_scatter(expert_terms[0].astype(jnp.bfloat16), 'dp', scatter_dime...  193 us
    reduce_scatter x2, waiting for transfers between devices, shards(): lax.psum_scatter(expert_terms[1].astype(jnp.bfloat16), 'dp', scatter_dime...  118 us
    all_to_all x2, waiting for transfers between devices, send_back(): return lax.all_to_all(values, 'cp', split_axis=0, concat_axis=0, tiled=True)  115 us
    all_gather x2, blocking collectives, shards(): lax.all_gather(gains[layer_index], ('dp', 'cp'), axis=0, tiled=True)  96.2 us
  transfers between devices with their start and end apart: 29, of which 22 were waited for; matrix products, arithmetic and copies ran while one was open for 11% of the time, Pallas kernels for 0%

commit v1 on v0

v1 whole, which is shorter than its diff:
```python
import jax
import jax.numpy as jnp
from jax import lax
from jax.sharding import PartitionSpec as P

D = 1536
HEADS = 12
KV_HEADS = 2
HEAD = 128
FF = 768
TOP = 4
EXP_DEV = 2
LAYERS = 2
DOCS = 4
HQ = 1536
KVW = 256
QKV = 2048
Q_PER_KV = 6

EPSILON = 1e-06
MASKED = -1e30
LOW = jnp.bfloat16
WIDE = jnp.float32


def inverse_rms(values):
    return lax.rsqrt(jnp.mean(values * values, axis=-1, keepdims=True) + EPSILON)


def norm_backward(values, gain, upstream):
    scale_rows = inverse_rms(values)
    weighted = gain * upstream
    inner_mean = jnp.mean(values * weighted, axis=-1, keepdims=True)
    grad_values = scale_rows * weighted - values * scale_rows * scale_rows * scale_rows * inner_mean
    grad_gain = jnp.sum(values * scale_rows * upstream, axis=0)
    return (grad_values, grad_gain)


def doc_places(token_index, lengths_row):
    starts = jnp.cumsum(lengths_row) - lengths_row
    segment = jnp.sum((token_index[:, None] >= starts[None, 1:]).astype(jnp.int32), axis=1)
    picked = segment[:, None] == jnp.arange(DOCS, dtype=jnp.int32)[None, :]
    offset = jnp.sum(jnp.where(picked, starts[None, :], 0), axis=1)
    return (segment, token_index - offset)


def rope_tables(positions):
    half_width = HEAD // 2
    frequency = jnp.exp(-jnp.log(10000.0) * 2.0 * jnp.arange(half_width, dtype=WIDE) / HEAD)
    angles = positions.astype(WIDE)[:, None] * frequency[None, :]
    return (jnp.cos(angles)[:, None, :], jnp.sin(angles)[:, None, :])


def rotate(values, cosine, sine_table):
    half_width = values.shape[-1] // 2
    former = values[..., :half_width]
    latter = values[..., half_width:]
    return jnp.concatenate(
        [former * cosine - latter * sine_table, latter * cosine + former * sine_table], axis=-1
    )


def heads_first(values):
    token_rows = values.shape[0]
    shaped = values.reshape(token_rows, KV_HEADS, Q_PER_KV, HEAD).transpose(1, 2, 0, 3)
    return shaped.reshape(KV_HEADS, Q_PER_KV * token_rows, HEAD)


def heads_last(values):
    token_rows = values.shape[1] // Q_PER_KV
    shaped = values.reshape(KV_HEADS, Q_PER_KV, token_rows, HEAD).transpose(2, 0, 1, 3)
    return shaped.reshape(token_rows, HQ)


def dot(left, right):
    return jnp.dot(left, right, preferred_element_type=WIDE)


def dot_t(left, right):
    return lax.dot_general(left, right, (((1,), (1,)), ((), ())), preferred_element_type=WIDE)


def t_dot(left, right):
    return lax.dot_general(left, right, (((0,), (0,)), ((), ())), preferred_element_type=WIDE)


def after(value, *earlier):
    return lax.optimization_barrier((value, *earlier))[0]


LINE = 4


def swap_core(value):
    return lax.ppermute(value, "cp", [(i, i ^ 1) for i in range(2 * LINE)])


def hop(value, upward, sources):
    step = 1 if upward else -1
    pairs = [(2 * z + core, 2 * (z + step) + core) for z in sources for core in range(2)]
    return lax.ppermute(value, "cp", pairs)


def across(value, flip):
    return lax.ppermute(value, "dp", [(i, i ^ flip) for i in range(4)])


def line_gather(value):
    place = lax.axis_index("cp") // 2
    rising, falling = value, value
    risen, fallen = [], []
    for step in range(1, LINE):
        rising = hop(rising, True, range(step - 1, LINE - 1))
        falling = hop(falling, False, range(1, LINE - step + 1))
        risen.insert(0, rising)
        fallen.append(falling)
    every = jnp.stack(risen + [value] + fallen)
    return lax.dynamic_slice_in_dim(every, LINE - 1 - place, LINE, 0)


def line_scatter(parts):
    place = lax.axis_index("cp") // 2

    def pick(index):
        return lax.dynamic_index_in_dim(parts, jnp.clip(index, 0, LINE - 1), 0, keepdims=False)

    rising = falling = None
    for step in range(1, LINE):
        up = pick(LINE + place - step)
        down = pick(place - LINE + step)
        if step > 1:
            up = (up.astype(WIDE) + rising.astype(WIDE)).astype(LOW)
            down = (down.astype(WIDE) + falling.astype(WIDE)).astype(LOW)
        rising = hop(up, True, range(step))
        falling = hop(down, False, range(LINE - step, LINE))
    return pick(place).astype(WIDE) + rising.astype(WIDE) + falling.astype(WIDE)


def square_gather(value):
    half = value.shape[0] // 2
    by_x = across(value, 1)
    by_y = across(value, 2)
    far = jnp.concatenate([across(by_x[:half], 2), across(by_y[half:], 1)], axis=0)
    return (value, by_x, by_y, far)


def square_scatter(piece):
    far = piece(3)
    half = far.shape[0] // 2
    from_x = across(far[:half], 1)
    from_y = across(far[half:], 2)
    to_x, to_y = piece(1), piece(2)
    to_x = jnp.concatenate(
        [to_x[:half], (to_x[half:].astype(WIDE) + from_y.astype(WIDE)).astype(LOW)], axis=0
    )
    to_y = jnp.concatenate(
        [(to_y[:half].astype(WIDE) + from_x.astype(WIDE)).astype(LOW), to_y[half:]], axis=0
    )
    got_x = across(to_x, 1)
    got_y = across(to_y, 2)
    return piece(0).astype(WIDE) + got_x.astype(WIDE) + got_y.astype(WIDE)


class SquareLine:
    def order(self, rows):
        core = lax.axis_index("cp") % 2
        blocks = jnp.concatenate(
            [2 * jnp.arange(LINE) + core, 2 * jnp.arange(LINE) + 1 - core]
        ).astype(jnp.int32)
        return (blocks[:, None] * rows + jnp.arange(rows, dtype=jnp.int32)[None, :]).reshape(-1)

    def group_gather(self, value):
        mine = line_gather(value)
        other = swap_core(mine)
        return jnp.concatenate([mine, other], axis=0).reshape(-1, *value.shape[1:])

    def group_scatter(self, terms):
        parts = terms.astype(LOW).reshape(2, LINE, -1, *terms.shape[1:])
        other = swap_core(parts[1])
        return line_scatter((parts[0].astype(WIDE) + other.astype(WIDE)).astype(LOW))

    def expert_gather(self, block):
        place = lax.axis_index("dp")
        pieces = square_gather(block)
        whole = jnp.zeros((block.shape[0], 4, *block.shape[1:]), block.dtype)
        for flip, part in enumerate(pieces):
            whole = lax.dynamic_update_slice_in_dim(whole, part[:, None], place ^ flip, 1)
        return whole.reshape(block.shape[0], 4 * block.shape[1], *block.shape[2:])

    def expert_scatter(self, terms):
        place = lax.axis_index("dp")
        parts = terms.reshape(terms.shape[0], 4, -1, *terms.shape[2:])
        return square_scatter(
            lambda flip: lax.dynamic_index_in_dim(parts, place ^ flip, 1, keepdims=False)
        )

    def dense_gather(self, block):
        place = lax.axis_index("dp")
        core = lax.axis_index("cp") % 2
        rows = block.shape[0]
        whole = jnp.zeros((4, LINE, 2, *block.shape), block.dtype)
        for flip, part in enumerate(square_gather(line_gather(block))):
            other = swap_core(part)
            for held, side in ((part, core), (other, 1 - core)):
                whole = lax.dynamic_update_slice(
                    whole, held[None, :, None], (place ^ flip, 0, side, 0, 0)
                )
        return whole.reshape(8 * LINE * rows, *block.shape[1:])

    def dense_scatter(self, terms):
        place = lax.axis_index("dp")
        core = lax.axis_index("cp") % 2
        parts = terms.astype(LOW).reshape(4, LINE, 2, -1, *terms.shape[1:])
        mine = lax.dynamic_index_in_dim(parts, core, 2, keepdims=False)
        other = swap_core(lax.dynamic_index_in_dim(parts, 1 - core, 2, keepdims=False))
        both = (mine.astype(WIDE) + other.astype(WIDE)).astype(LOW)
        plane = square_scatter(
            lambda flip: lax.dynamic_index_in_dim(both, place ^ flip, 0, keepdims=False)
        )
        return line_scatter(plane.astype(LOW))


class AnyMesh:
    def order(self, rows):
        return jnp.arange(lax.axis_size("cp") * rows, dtype=jnp.int32)

    def group_gather(self, value):
        return lax.all_gather(value, "cp", axis=0, tiled=True)

    def group_scatter(self, terms):
        return lax.psum_scatter(
            terms.astype(LOW), "cp", scatter_dimension=0, tiled=True
        ).astype(WIDE)

    def expert_gather(self, block):
        return lax.all_gather(block, "dp", axis=1, tiled=True)

    def expert_scatter(self, terms):
        return lax.psum_scatter(terms, "dp", scatter_dimension=1, tiled=True).astype(WIDE)

    def dense_gather(self, block):
        return lax.all_gather(block, ("dp", "cp"), axis=0, tiled=True)

    def dense_scatter(self, terms):
        return lax.psum_scatter(
            terms.astype(LOW), ("dp", "cp"), scatter_dimension=0, tiled=True
        ).astype(WIDE)


def shards(tokens, cotangent, doc_lengths, routes, w_qkv, w_out, router, gains, w_gate_up, w_down):
    dp_size = lax.axis_size("dp")
    cp_size = lax.axis_size("cp")
    device_count = dp_size * cp_size
    move = SquareLine() if (dp_size, cp_size) == (4, 2 * LINE) else AnyMesh()
    row_count = tokens.shape[0]
    group_rows = row_count * cp_size
    cycle_place = lax.axis_index("cp")
    expert_count = EXP_DEV * cp_size
    lengths_row = doc_lengths[0]
    my_index = cycle_place * row_count + jnp.arange(row_count, dtype=jnp.int32)
    my_segment, my_position = doc_places(my_index, lengths_row)
    cosine, sine_table = rope_tables(my_position)
    score_scale = HEAD ** (-0.5)
    key_index = move.order(row_count)
    key_segment, unused_position = doc_places(key_index, lengths_row)
    allowed = (my_segment[:, None] == key_segment[None, :]) & (
        key_index[None, :] <= my_index[:, None]
    )
    allowed = jnp.tile(allowed, (Q_PER_KV, 1))[None]

    part_rows = router.shape[1]
    small_width = expert_count + 2
    small = jnp.concatenate([router, gains], axis=2).reshape(-1)
    small_size = small.shape[0]
    small = jnp.pad(small, (0, -small_size % 2048)).reshape(-1, 128)
    small = lax.all_gather(small, ("dp", "cp"), axis=0, tiled=False).reshape(device_count, -1)
    small = small[:, :small_size].reshape(device_count, LAYERS, part_rows, small_width)
    small = small.transpose(1, 0, 2, 3).reshape(LAYERS, D, small_width)
    router_all = small[:, :, :expert_count]
    gains_all = small[:, :, expert_count:].astype(WIDE)
    route_block = routes.reshape(-1, 128)
    route_blocks = lax.all_gather(route_block, "cp", axis=0, tiled=False)
    route_blocks = route_blocks.reshape(cp_size, LAYERS, row_count, TOP)
    route_rows = route_blocks.transpose(1, 0, 2, 3).reshape(LAYERS, group_rows, TOP)
    expert_ids = jnp.arange(expert_count, dtype=jnp.int32)

    weights = []
    for layer in range(LAYERS):
        query_weight = move.dense_gather(w_qkv[layer])
        output_weight = move.dense_gather(w_out[layer])
        gate_up_weight = move.expert_gather(w_gate_up[layer])
        down_weight = move.expert_gather(w_down[layer])
        weights.append((query_weight, output_weight, gate_up_weight, down_weight))
    cotangent_group = move.group_gather(cotangent)

    def norm_rows(values, gain):
        return (values * inverse_rms(values) * gain).astype(LOW)

    def forward_layer(layer, layer_value):
        query_weight, output_weight, gate_up_weight, down_weight = weights[layer]
        normed = norm_rows(layer_value, gains_all[layer, :, 0])
        joined = dot_t(normed, query_weight)
        queries = rotate(joined[:, :HQ].reshape(row_count, HEADS, HEAD), cosine, sine_table)
        keys = rotate(
            joined[:, HQ : HQ + KVW].reshape(row_count, KV_HEADS, HEAD), cosine, sine_table
        )
        queries = heads_first(queries.reshape(row_count, HQ).astype(LOW))
        keys_values = jnp.concatenate(
            [keys.reshape(row_count, KVW), joined[:, HQ + KVW :]], axis=1
        ).astype(LOW)
        keys_values = move.group_gather(keys_values)
        key_heads = keys_values[:, :KVW].reshape(group_rows, KV_HEADS, HEAD)
        value_heads = keys_values[:, KVW:].reshape(group_rows, KV_HEADS, HEAD)
        scores = (
            jnp.einsum("kqh,nkh->kqn", queries, key_heads, preferred_element_type=WIDE)
            * score_scale
        )
        scores = jnp.where(allowed, scores, MASKED)
        top_score = jnp.max(scores, axis=-1, keepdims=True)
        shares = jnp.exp(scores - top_score)
        total = jnp.sum(shares, axis=-1, keepdims=True)
        probs = (shares / total).astype(LOW)
        attended = jnp.einsum("kqn,nkh->kqh", probs, value_heads, preferred_element_type=WIDE)
        attended = heads_last(attended)
        attended_low = attended.astype(LOW)
        middle = layer_value + dot(attended_low, output_weight)
        mixed = norm_rows(middle, gains_all[layer, :, 1])
        mixed_group = move.group_gather(mixed)
        route_group = jnp.take(
            route_rows[layer].reshape(cp_size, row_count, TOP),
            key_index[::row_count] // row_count,
            axis=0,
        ).reshape(group_rows, TOP)
        chosen = jnp.any(route_group[:, :, None] == expert_ids[None, None, :], axis=1)
        logits = jnp.where(chosen, dot(mixed_group, router_all[layer]), MASKED)
        gates = jax.nn.softmax(logits, axis=-1)
        own_gates = lax.dynamic_slice_in_dim(gates, EXP_DEV * cycle_place, EXP_DEV, 1)
        gate_up = [dot(mixed_group, gate_up_weight[e]).astype(LOW) for e in range(EXP_DEV)]
        hidden = []
        for e in range(EXP_DEV):
            gate_part = gate_up[e][:, :FF].astype(WIDE)
            up_part = gate_up[e][:, FF:].astype(WIDE)
            hidden.append(jax.nn.silu(gate_part) * up_part * own_gates[:, e : e + 1])
        hidden = jnp.concatenate(hidden, axis=1).astype(LOW)
        terms = dot(hidden, down_weight.reshape(EXP_DEV * FF, D))
        result = middle + move.group_scatter(terms)
        kept = (
            layer_value,
            normed,
            queries,
            keys_values,
            probs,
            attended,
            middle,
            mixed_group,
            gates,
            own_gates,
            gate_up,
            hidden,
        )
        return (result, kept)

    def backward_layer(layer, upstream, upstream_group, kept):
        query_weight, output_weight, gate_up_weight, down_weight = weights[layer]
        (
            layer_value,
            normed,
            queries,
            keys_values,
            probs,
            attended,
            middle,
            mixed_group,
            gates,
            own_gates,
            gate_up,
            hidden,
        ) = kept
        grad_hidden = dot_t(upstream_group, down_weight.reshape(EXP_DEV * FF, D))
        grad_gate_up = []
        grad_gates = []
        for e in range(EXP_DEV):
            gate_part = gate_up[e][:, :FF].astype(WIDE)
            up_part = gate_up[e][:, FF:].astype(WIDE)
            bare = grad_hidden[:, e * FF : (e + 1) * FF]
            logistic = jax.nn.sigmoid(gate_part)
            activated = gate_part * logistic
            grad_gates.append(jnp.sum(bare * activated * up_part, axis=1, keepdims=True))
            gated = bare * own_gates[:, e : e + 1]
            grad_gate = gated * up_part * logistic * (1.0 + gate_part * (1.0 - logistic))
            grad_gate_up.append(
                jnp.concatenate([grad_gate, gated * activated], axis=1).astype(LOW)
            )
        own_terms = own_gates * jnp.concatenate(grad_gates, axis=1)
        own_ids = EXP_DEV * cycle_place + jnp.arange(EXP_DEV, dtype=jnp.int32)
        placed = jnp.sum(
            jnp.where(own_ids[None, :, None] == expert_ids[None, None, :], own_terms[:, :, None], 0.0),
            axis=1,
        )
        grad_logits = (placed - jnp.sum(own_terms, axis=1, keepdims=True) * gates).astype(LOW)
        terms = dot_t(grad_gate_up[0], gate_up_weight[0]) + dot_t(
            grad_gate_up[1], gate_up_weight[1]
        )
        terms = terms + dot_t(grad_logits, router_all[layer])
        grad_mixed = move.group_scatter(terms)
        grad_router = t_dot(mixed_group, grad_logits)
        grad_gate_up_weight = jnp.stack(
            [t_dot(mixed_group, grad_gate_up[e]).astype(LOW) for e in range(EXP_DEV)]
        )
        grad_down_weight = t_dot(hidden, upstream_group).astype(LOW).reshape(EXP_DEV, FF, D)
        expert_grads = (
            move.expert_scatter(grad_gate_up_weight),
            move.expert_scatter(grad_down_weight),
        )

        grad_middle, grad_second_gain = norm_backward(
            middle, gains_all[layer, :, 1], grad_mixed
        )
        grad_middle = grad_middle + upstream
        grad_middle_low = grad_middle.astype(LOW)
        grad_output_weight = move.dense_scatter(t_dot(attended.astype(LOW), grad_middle_low))
        grad_attended = dot_t(grad_middle_low, output_weight).astype(LOW)
        grad_heads = heads_first(grad_attended)
        delta = jnp.sum(grad_heads.astype(WIDE) * heads_first(attended), axis=-1, keepdims=True)
        key_heads = keys_values[:, :KVW].reshape(group_rows, KV_HEADS, HEAD)
        value_heads = keys_values[:, KVW:].reshape(group_rows, KV_HEADS, HEAD)
        grad_probs = jnp.einsum(
            "kqh,nkh->kqn", grad_heads, value_heads, preferred_element_type=WIDE
        )
        grad_scores = (probs.astype(WIDE) * (grad_probs - delta) * score_scale).astype(LOW)
        grad_queries = jnp.einsum(
            "kqn,nkh->kqh", grad_scores, key_heads, preferred_element_type=WIDE
        )
        grad_keys = jnp.einsum(
            "kqn,kqh->nkh", grad_scores, queries, preferred_element_type=WIDE
        )
        grad_values = jnp.einsum(
            "kqn,kqh->nkh", probs, grad_heads, preferred_element_type=WIDE
        )
        grad_keys_values = move.group_scatter(
            jnp.concatenate(
                [grad_keys.reshape(group_rows, KVW), grad_values.reshape(group_rows, KVW)], axis=1
            )
        )
        grad_queries = rotate(
            heads_last(grad_queries).reshape(row_count, HEADS, HEAD), cosine, -sine_table
        ).reshape(row_count, HQ)
        grad_keys = rotate(
            grad_keys_values[:, :KVW].reshape(row_count, KV_HEADS, HEAD), cosine, -sine_table
        ).reshape(row_count, KVW)
        grad_joined = jnp.concatenate(
            [grad_queries, grad_keys, grad_keys_values[:, KVW:]], axis=1
        ).astype(LOW)
        grad_query_weight = t_dot(grad_joined, normed)
        grad_normed = dot(grad_joined, query_weight)
        grad_input, grad_first_gain = norm_backward(
            layer_value, gains_all[layer, :, 0], grad_normed
        )
        grad_input = grad_input + grad_middle
        small_terms = jnp.concatenate(
            [grad_router, grad_first_gain[:, None], grad_second_gain[:, None]], axis=1
        )
        return (grad_input, grad_query_weight, grad_output_weight, expert_grads, small_terms)

    layer_value = tokens.astype(WIDE)
    stored = []
    for layer in range(LAYERS):
        layer_value, kept = forward_layer(layer, layer_value)
        stored.append(kept)
    upstream = cotangent.astype(WIDE)
    upstream_group = cotangent_group
    query_grads, output_grads, expert_grads, small_terms = ([None] * LAYERS for _ in range(4))
    for layer in reversed(range(LAYERS)):
        if layer < LAYERS - 1:
            upstream_group = move.group_gather(upstream.astype(LOW))
        upstream, query_terms, output_grads[layer], expert_grads[layer], small_terms[layer] = (
            backward_layer(layer, upstream, upstream_group, stored[layer])
        )
        if layer > 0:
            query_grads[layer] = move.dense_scatter(query_terms)
    small_grads = jnp.stack(small_terms).reshape(LAYERS, device_count, part_rows, small_width)
    small_grads = small_grads.transpose(1, 0, 2, 3).reshape(device_count, -1)
    small_size = small_grads.shape[1]
    extra_rows = -(-small_size // (8 * D)) * 8
    small_grads = jnp.pad(small_grads, ((0, 0), (0, extra_rows * D - small_size)))
    query_rows = query_terms.shape[0] // device_count
    last_terms = jnp.concatenate(
        [
            query_terms.astype(LOW).reshape(device_count, query_rows, D),
            small_grads.astype(LOW).reshape(device_count, extra_rows, D),
        ],
        axis=1,
    )
    last_grads = move.dense_scatter(last_terms.reshape(-1, D))
    query_grads[0] = last_grads[:query_rows]
    small_grads = last_grads[query_rows:].reshape(-1)[:small_size]
    small_grads = small_grads.reshape(LAYERS, part_rows, small_width)
    return (
        layer_value,
        upstream,
        jnp.stack(query_grads),
        jnp.stack(output_grads),
        small_grads[:, :, :expert_count],
        small_grads[:, :, expert_count:],
        jnp.stack([pair[0] for pair in expert_grads]),
        jnp.stack([pair[1] for pair in expert_grads]),
    )


def solution(mesh):
    return jax.shard_map(
        shards,
        mesh=mesh,
        in_specs=(
            P(("dp", "cp"), None),
            P(("dp", "cp"), None),
            P("dp", None),
            P(None, ("dp", "cp"), None),
            P(None, ("dp", "cp"), None),
            P(None, ("dp", "cp"), None),
            P(None, ("dp", "cp"), None),
            P(None, ("dp", "cp"), None),
            P(None, "cp", "dp", None),
            P(None, "cp", "dp", None),
        ),
        out_specs=(
            P(("dp", "cp"), None),
            P(("dp", "cp"), None),
            P(None, ("dp", "cp"), None),
            P(None, ("dp", "cp"), None),
            P(None, ("dp", "cp"), None),
            P(None, ("dp", "cp"), None),
            P(None, "cp", "dp", None),
            P(None, "cp", "dp", None),
        ),
        check_vma=False,
    )
```

time: 2610 us -> 1550 us (0.59)
  waiting for transfers between devices: 1670 us -> 582 us
  blocking collectives: 469 us -> 53.5 us
  starting transfers between devices: 29.3 us -> 334 us
  local copies, waits for them, and re-layouts: 148 us -> 231 us
  other arithmetic: 70.7 us -> 150 us
    reduce_scatter x8 -> x0, waiting for transfers between devices: 907 us -> none  [the longest x2 316 us: shards(): lax.psum_scatter(attention_terms[0], ('dp', 'cp'), scatter_dimension=0, t...]
    ppermute x0 -> x216, waiting for transfers between devices: none -> 582 us  [the longest x64 347 us: across(): return lax.ppermute(value, 'dp', [(i, i ^ flip) for i in range(4)])]
    unnamed x28 -> x0, waiting for transfers between devices: 371 us -> none
    all_gather x8 -> x2, blocking collectives: 394 us -> 53.5 us  [the longest x1 39.5 us: shards(): lax.all_gather(small, ('dp', 'cp'), axis=0, tiled=False)]
    ppermute x0 -> x216, starting transfers between devices: none -> 334 us  [the longest x120 267 us: hop(): return lax.ppermute(value, 'cp', pairs)]
    all_to_all x7 -> x0, waiting for transfers between devices: 236 us -> none  [the longest x2 115 us: send_back(): return lax.all_to_all(values, 'cp', split_axis=0, concat_axis=0, tiled=True)]
    all_gather x8 -> x0, waiting for transfers between devices: 158 us -> none  [the longest x2 84 us: shards(): lax.all_gather(w_gate_up[layer_index], 'dp', axis=1, tiled=True)]
    all_to_all x1 -> x0, blocking collectives: 75.3 us -> none  [shards(): lax.all_to_all(grad_outgoing, 'cp', split_axis=0, concat_axis=0, tiled=True)]
  transfers between devices with their start and end apart: 29 -> 216, of which waited for: 22 -> 91; matrix products, arithmetic and copies ran while one was open for 11% -> 30% of each run, Pallas kernels for 0% -> 0%
where the time goes in v1:
time: 1550 us; the launch traced here: 1540 us
  waiting for transfers between devices  582 us (38%)
  starting transfers between devices  334 us (22%)
  local copies, waits for them, and re-layouts  231 us (15%)
  matrix products  184 us (12%)
  other arithmetic  150 us (10%)
  blocking collectives  53.5 us (3%)
    ppermute x64, waiting for transfers between devices, across(): return lax.ppermute(value, 'dp', [(i, i ^ flip) for i in range(4)])  347 us
    ppermute x120, starting transfers between devices, hop(): return lax.ppermute(value, 'cp', pairs)  267 us
    ppermute x120, waiting for transfers between devices, hop(): return lax.ppermute(value, 'cp', pairs)  228 us
    ppermute x64, starting transfers between devices, across(): return lax.ppermute(value, 'dp', [(i, i ^ flip) for i in range(4)])  64.9 us
    unnamed x513, local copies, waits for them, and re-layouts  55.8 us
    dot_general x12, matrix products, dot_t(): lax.dot_general(left, right, (((1,), (1,)), ((), ())), preferred_element_...  53.4 us
    dot_general x12, matrix products, t_dot(): lax.dot_general(left, right, (((0,), (0,)), ((), ())), preferred_element_...  51.5 us
    dot_general x12, matrix products, dot(): return jnp.dot(left, right, preferred_element_type=WIDE)  50.7 us
  transfers between devices with their start and end apart: 216, of which 91 were waited for; matrix products, arithmetic and copies ran while one was open for 30% of the time, Pallas kernels for 0%

profile of v1, /device:TPU:0, one launch (start us, length us, event | category | flops | bytes accessed | tf_op | source)
XLA Modules:
  0.0 1541.9 jit_solution(12584753505030139554)
XLA Ops:
  25.9 39.5 %all_gather.6 = bf16[32,16,128]{2,1,0:T(8,128)(2,1)S(1)} all-gather(bf16[1,16,128]{2,1,0:T(8,128)(2,1)S(1)} %pad_bitcast_fusion), channel_id=1, replica_groups=mesh['dp'=4,'cp'=8] {'dp','cp'}, dimensions={0}, use_global_device_ids=true | all-gather | bytes 135168 | tf_op jit(solution)/shard_map/all_gather | solution.py:276
  89.9 14.0 all_gather.7
  116.9 7.0 collective-permute-start
  130.1 7.9 collective-permute-done.81
  143.3 6.5 collective-permute-done.25
  192.5 8.4 collective-permute-done.85
  206.0 7.4 collective-permute-done.117
  216.5 11.8 collective-permute-done.118
  233.4 10.7 collective-permute-done.119
  266.6 58.5 %collective-permute-done.33 = bf16[2,48,1536]{2,1,0:T(8,128)(2,1)S(1)} collective-permute-done((bf16[2,48,1536]{2,1,0:T(8,128)(2,1)S(1)}, bf16[2,48,1536]{2,1,0:T(8,128)(2,1)S(1)}, u32[]{:S(2)}, u32[]{:S(2)}) %collective-permute-start.33) | collective-permute-done | bytes 294944 | tf_op jit(solution)/shard_map/ppermute | solution.py:105
  335.4 14.9 collective-permute-done.7
  350.3 10.5 collective-permute-done.9
  364.0 6.2 collective-permute-done.11
  416.9 27.8 %collective-permute-done.100 = bf16[2,384,1536]{2,1,0:T(8,128)(2,1)} collective-permute-done((bf16[2,384,1536]{2,1,0:T(8,128)(2,1)}, bf16[2,384,1536]{2,1,0:T(8,128)(2,1)}, u32[]{:S(2)}, u32[]{:S(2)}) %collective-permute-start.100) | collective-permute-done | bytes 2359328 | tf_op jit(solution)/shard_map/ppermute | solution.py:105
  452.2 43.1 %collective-permute-done.43 = bf16[2,384,1536]{2,1,0:T(8,128)(2,1)} collective-permute-done((bf16[2,384,1536]{2,1,0:T(8,128)(2,1)}, bf16[2,384,1536]{2,1,0:T(8,128)(2,1)}, u32[]{:S(2)}, u32[]{:S(2)}) %collective-permute-start.43) | collective-permute-done | bytes 2359328 | tf_op jit(solution)/shard_map/ppermute | solution.py:105
  512.6 6.2 fusion.256
  561.5 7.9 collective-permute-done.40
  575.0 9.8 collective-permute-done.45
  589.2 8.1 fusion.244
  633.6 8.9 collective-permute-done.51
  647.9 8.0 collective-permute-done.52
  656.9 15.3 collective-permute-start.53
  730.6 6.3 fusion.259
  753.3 6.6 collective-permute-done.92
  779.6 9.4 collective-permute-done.97
  790.4 6.9 fusion.262
  797.3 7.9 fusion.243
  826.5 6.4 convolution_convert_fusion.10
  832.9 7.0 convolution_convert_fusion
  839.9 6.4 fusion.45
  846.3 6.6 fusion.88
  852.9 7.0 convolution_convert_fusion.2
  860.0 7.6 fusion.89
  867.6 7.6 convolution_convert_fusion.3
  905.8 17.8 %collective-permute-done.204 = bf16[1,384,1536]{2,1,0:T(8,128)(2,1)} collective-permute-done((bf16[1,384,1536]{2,1,0:T(8,128)(2,1)}, bf16[1,384,1536]{2,1,0:T(8,128)(2,1)}, u32[]{:S(2)}, u32[]{:S(2)}) %collective-permute-start.204) | collective-permute-done | bytes 1179680 | tf_op jit(solution)/shard_map/ppermute | solution.py:105
  934.4 6.3 collective-permute-done.122
  953.0 6.3 collective-permute-done.123
  970.9 7.1 collective-permute-start.124
  1089.1 20.4 %collective-permute-done.207 = bf16[2,384,1536]{2,1,0:T(8,128)(2,1)} collective-permute-done((bf16[2,384,1536]{2,1,0:T(8,128)(2,1)}, bf16[2,384,1536]{2,1,0:T(8,128)(2,1)}, u32[]{:S(2)}, u32[]{:S(2)}) %collective-permute-start.207) | collective-permute-done | bytes 2359328 | tf_op jit(solution)/shard_map/ppermute | solution.py:105
  1109.5 6.3 fusion.7
  1134.2 9.5 collective-permute-done.191
  1195.2 9.6 fusion.86
  1221.7 7.1 fusion.87
  1243.9 26.3 %collective-permute-done.168 = bf16[2,64,1536]{2,1,0:T(8,128)(2,1)S(1)} collective-permute-done((bf16[2,64,1536]{2,1,0:T(8,128)(2,1)S(1)}, bf16[2,64,1536]{2,1,0:T(8,128)(2,1)S(1)}, u32[]{:S(2)}, u32[]{:S(2)}) %collective-permute-start.168) | collective-permute-done | bytes 393248 | tf_op jit(solution)/shard_map/ppermute | solution.py:105
  1281.4 34.6 %collective-permute-done.169 = bf16[4,64,1536]{2,1,0:T(8,128)(2,1)S(1)} collective-permute-done((bf16[4,64,1536]{2,1,0:T(8,128)(2,1)S(1)}, bf16[4,64,1536]{2,1,0:T(8,128)(2,1)S(1)}, u32[]{:S(2)}, u32[]{:S(2)}) %collective-permute-start.169) | collective-permute-done | bytes 786464 | tf_op jit(solution)/shard_map/ppermute | solution.py:105
  1349.6 8.8 collective-permute-start.145
  1468.2 8.8 collective-permute-done.180
  1493.8 11.4 collective-permute-done.158
  (1350 shorter events, 929.7 us)
Async XLA Ops:
  2.5 136.8 %collective-permute-start.57 = (bf16[64,1536]{1,0:T(8,128)(2,1)}, bf16[64,1536]{1,0:T(8,128)(2,1)}, u32[]{:S(2)}, u32[]{:S(2)}) collective-permute-start(bf16[64,1536]{1,0:T(8,128)(2,1)} %get-tuple-element.221), channel_id=1, source_target_pairs={{0,2},{1,3},{2,4},{3,5},{4,6},{5,7},{8,10},{9,11},{10,12},{11,13},... | collective-permute-start | bytes 589832 | tf_op jit(solution)/shard_map/ppermute | solution.py:101
  8.1 133.2 %collective-permute-start.60 = (bf16[64,1536]{1,0:T(8,128)(2,1)}, bf16[64,1536]{1,0:T(8,128)(2,1)}, u32[]{:S(2)}, u32[]{:S(2)}) collective-permute-start(bf16[64,1536]{1,0:T(8,128)(2,1)} %get-tuple-element.221), channel_id=1, source_target_pairs={{2,0},{3,1},{4,2},{5,3},{6,4},{7,5},{10,8},{11,9},{12,10},{13,11},... | collective-permute-start | bytes 589832 | tf_op jit(solution)/shard_map/ppermute | solution.py:101
  11.1 100.8 %collective-permute-start.21 = (bf16[48,1536]{1,0:T(8,128)(2,1)}, bf16[48,1536]{1,0:T(8,128)(2,1)}, u32[]{:S(2)}, u32[]{:S(2)}) collective-permute-start(bf16[48,1536]{1,0:T(8,128)(2,1)} %get-tuple-element.226), channel_id=1, source_target_pairs={{0,2},{1,3},{2,4},{3,5},{4,6},{5,7},{8,10},{9,11},{10,12},{11,13},... | collective-permute-start | bytes 442376 | tf_op jit(solution)/shard_map/ppermute | solution.py:101
  16.3 111.6 %collective-permute-start.24 = (bf16[48,1536]{1,0:T(8,128)(2,1)}, bf16[48,1536]{1,0:T(8,128)(2,1)}, u32[]{:S(2)}, u32[]{:S(2)}) collective-permute-start(bf16[48,1536]{1,0:T(8,128)(2,1)} %get-tuple-element.226), channel_id=1, source_target_pairs={{2,0},{3,1},{4,2},{5,3},{6,4},{7,5},{10,8},{11,9},{12,10},{13,11},... | collective-permute-start | bytes 442376 | tf_op jit(solution)/shard_map/ppermute | solution.py:101
  17.6 96.2 %collective-permute-start.78 = (bf16[48,1536]{1,0:T(8,128)(2,1)}, bf16[48,1536]{1,0:T(8,128)(2,1)}, u32[]{:S(2)}, u32[]{:S(2)}) collective-permute-start(bf16[48,1536]{1,0:T(8,128)(2,1)} %get-tuple-element.225), channel_id=1, source_target_pairs={{0,2},{1,3},{2,4},{3,5},{4,6},{5,7},{8,10},{9,11},{10,12},{11,13},... | collective-permute-start | bytes 442376 | tf_op jit(solution)/shard_map/ppermute | solution.py:101
  189.4 40.0 %collective-permute-start.46 = (bf16[2,192,1536]{2,1,0:T(8,128)(2,1)S(1)}, bf16[2,192,1536]{2,1,0:T(8,128)(2,1)S(1)}, u32[]{:S(2)}, u32[]{:S(2)}) collective-permute-start(bf16[2,192,1536]{2,1,0:T(8,128)(2,1)S(1)} %copy-done.130), channel_id=1, source_target_pairs={{0,8},{8,0},{16,24},{24,16},{1,9},{9,1},{17,25},{25,17},{2,10},{10... | collective-permute-start | bytes 3538952 | tf_op jit(solution)/shard_map/ppermute | solution.py:105
  204.5 47.0 %collective-permute-start.103 = (bf16[2,192,1536]{2,1,0:T(8,128)(2,1)S(1)}, bf16[2,192,1536]{2,1,0:T(8,128)(2,1)S(1)}, u32[]{:S(2)}, u32[]{:S(2)}) collective-permute-start(bf16[2,192,1536]{2,1,0:T(8,128)(2,1)S(1)} %copy-done.129), channel_id=1, source_target_pairs={{0,8},{8,0},{16,24},{24,16},{1,9},{9,1},{17,25},{25,17},{2,10},{10... | collective-permute-start | bytes 3538952 | tf_op jit(solution)/shard_map/ppermute | solution.py:105
  213.5 41.6 %collective-permute-start.104 = (bf16[2,192,1536]{2,1,0:T(8,128)(2,1)S(1)}, bf16[2,192,1536]{2,1,0:T(8,128)(2,1)S(1)}, u32[]{:S(2)}, u32[]{:S(2)}) collective-permute-start(bf16[2,192,1536]{2,1,0:T(8,128)(2,1)S(1)} %copy-done.129), channel_id=1, source_target_pairs={{0,16},{8,24},{16,0},{24,8},{1,17},{9,25},{17,1},{25,9},{2,18},{10... | collective-permute-start | bytes 3538952 | tf_op jit(solution)/shard_map/ppermute | solution.py:105
  228.3 185.9 %collective-permute-start.99 = (bf16[2,384,1536]{2,1,0:T(8,128)(2,1)}, bf16[2,384,1536]{2,1,0:T(8,128)(2,1)S(1)}, u32[]{:S(2)}, u32[]{:S(2)}) collective-permute-start(bf16[2,384,1536]{2,1,0:T(8,128)(2,1)} %get-tuple-element.113), channel_id=1, source_target_pairs={{0,8},{8,0},{16,24},{24,16},{1,9},{9,1},{17,25},{25,17},{2,10},{10... | collective-permute-start | bytes 7077896 | tf_op jit(solution)/shard_map/ppermute | solution.py:105
  251.5 80.0 %collective-permute-start.63 = (bf16[4,64,1536]{2,1,0:T(8,128)(2,1)S(1)}, bf16[4,64,1536]{2,1,0:T(8,128)(2,1)S(1)}, u32[]{:S(2)}, u32[]{:S(2)}) collective-permute-start(bf16[4,64,1536]{2,1,0:T(8,128)(2,1)S(1)} %copy-done.132), channel_id=1, source_target_pairs={{0,1},{1,0},{2,3},{3,2},{4,5},{5,4},{6,7},{7,6},{8,9},{9,8},{10,11... | collective-permute-start | bytes 2359304 | tf_op jit(solution)/shard_map/ppermute | solution.py:95
  255.1 77.2 %collective-permute-start.64 = (bf16[4,64,1536]{2,1,0:T(8,128)(2,1)S(1)}, bf16[4,64,1536]{2,1,0:T(8,128)(2,1)S(1)}, u32[]{:S(2)}, u32[]{:S(2)}) collective-permute-start(bf16[4,64,1536]{2,1,0:T(8,128)(2,1)S(1)} %copy-done.132), channel_id=1, source_target_pairs={{0,8},{8,0},{16,24},{24,16},{1,9},{9,1},{17,25},{25,17},{2,10},{10... | collective-permute-start | bytes 2359304 | tf_op jit(solution)/shard_map/ppermute | solution.py:105
  261.4 63.8 %collective-permute-start.33 = (bf16[2,48,1536]{2,1,0:T(8,128)(2,1)S(1)}, bf16[2,48,1536]{2,1,0:T(8,128)(2,1)S(1)}, u32[]{:S(2)}, u32[]{:S(2)}) collective-permute-start(bf16[2,48,1536]{2,1,0:T(8,128)(2,1)S(1)} %slice.818), channel_id=1, source_target_pairs={{0,8},{8,0},{16,24},{24,16},{1,9},{9,1},{17,25},{25,17},{2,10},{10... | collective-permute-start | bytes 884744 | tf_op jit(solution)/shard_map/ppermute | solution.py:105
  266.1 65.0 %collective-permute-start.90 = (bf16[2,48,1536]{2,1,0:T(8,128)(2,1)S(1)}, bf16[2,48,1536]{2,1,0:T(8,128)(2,1)S(1)}, u32[]{:S(2)}, u32[]{:S(2)}) collective-permute-start(bf16[2,48,1536]{2,1,0:T(8,128)(2,1)S(1)} %slice.847), channel_id=1, source_target_pairs={{0,8},{8,0},{16,24},{24,16},{1,9},{9,1},{17,25},{25,17},{2,10},{10... | collective-permute-start | bytes 884744 | tf_op jit(solution)/shard_map/ppermute | solution.py:105
  390.3 54.4 %collective-permute-start.100 = (bf16[2,384,1536]{2,1,0:T(8,128)(2,1)}, bf16[2,384,1536]{2,1,0:T(8,128)(2,1)}, u32[]{:S(2)}, u32[]{:S(2)}) collective-permute-start(bf16[2,384,1536]{2,1,0:T(8,128)(2,1)} %get-tuple-element.113), channel_id=1, source_target_pairs={{0,16},{8,24},{16,0},{24,8},{1,17},{9,25},{17,1},{25,9},{2,18},{10... | collective-permute-start | bytes 7077896 | tf_op jit(solution)/shard_map/ppermute | solution.py:105
  391.8 56.5 %collective-permute-start.42 = (bf16[2,384,1536]{2,1,0:T(8,128)(2,1)}, bf16[2,384,1536]{2,1,0:T(8,128)(2,1)}, u32[]{:S(2)}, u32[]{:S(2)}) collective-permute-start(bf16[2,384,1536]{2,1,0:T(8,128)(2,1)} %get-tuple-element.114), channel_id=1, source_target_pairs={{0,8},{8,0},{16,24},{24,16},{1,9},{9,1},{17,25},{25,17},{2,10},{10... | collective-permute-start | bytes 7077896 | tf_op jit(solution)/shard_map/ppermute | solution.py:105
  393.5 101.7 %collective-permute-start.43 = (bf16[2,384,1536]{2,1,0:T(8,128)(2,1)}, bf16[2,384,1536]{2,1,0:T(8,128)(2,1)}, u32[]{:S(2)}, u32[]{:S(2)}) collective-permute-start(bf16[2,384,1536]{2,1,0:T(8,128)(2,1)} %get-tuple-element.114), channel_id=1, source_target_pairs={{0,16},{8,24},{16,0},{24,8},{1,17},{9,25},{17,1},{25,9},{2,18},{10... | collective-permute-start | bytes 7077896 | tf_op jit(solution)/shard_map/ppermute | solution.py:105
  413.2 91.7 %collective-permute-start.20 = (bf16[4,128,512]{2,1,0:T(8,128)(2,1)S(1)}, bf16[4,128,512]{2,1,0:T(8,128)(2,1)}, u32[]{:S(2)}, u32[]{:S(2)}) collective-permute-start(bf16[4,128,512]{2,1,0:T(8,128)(2,1)S(1)} %constant_dynamic-slice_fusion.14), channel_id=1, source_target_pairs={{0,1},{1,0},{2,3},{3,2},{4,5},{5,4},{6,7},{7,6},{8,9},{9,8},{10,11... | collective-permute-start | bytes 1572872 | tf_op jit(solution)/shard_map/ppermute | solution.py:95
  415.4 157.5 %collective-permute-start.101 = (bf16[1,384,1536]{2,1,0:T(8,128)(2,1)}, bf16[1,384,1536]{2,1,0:T(8,128)(2,1)}, u32[]{:S(2)}, u32[]{:S(2)}) collective-permute-start(bf16[1,384,1536]{2,1,0:T(8,128)(2,1)} %slice.849), channel_id=1, source_target_pairs={{0,16},{8,24},{16,0},{24,8},{1,17},{9,25},{17,1},{25,9},{2,18},{10... | collective-permute-start | bytes 3538952 | tf_op jit(solution)/shard_map/ppermute | solution.py:105
  447.1 126.1 %collective-permute-start.102 = (bf16[1,384,1536]{2,1,0:T(8,128)(2,1)}, bf16[1,384,1536]{2,1,0:T(8,128)(2,1)}, u32[]{:S(2)}, u32[]{:S(2)}) collective-permute-start(bf16[1,384,1536]{2,1,0:T(8,128)(2,1)} %slice.850), channel_id=1, source_target_pairs={{0,8},{8,0},{16,24},{24,16},{1,9},{9,1},{17,25},{25,17},{2,10},{10... | collective-permute-start | bytes 3538952 | tf_op jit(solution)/shard_map/ppermute | solution.py:105
  450.7 122.7 %collective-permute-start.44 = (bf16[1,384,1536]{2,1,0:T(8,128)(2,1)}, bf16[1,384,1536]{2,1,0:T(8,128)(2,1)}, u32[]{:S(2)}, u32[]{:S(2)}) collective-permute-start(bf16[1,384,1536]{2,1,0:T(8,128)(2,1)} %slice.820), channel_id=1, source_target_pairs={{0,16},{8,24},{16,0},{24,8},{1,17},{9,25},{17,1},{25,9},{2,18},{10... | collective-permute-start | bytes 3538952 | tf_op jit(solution)/shard_map/ppermute | solution.py:105
  572.8 47.3 %collective-permute-start.86 = (bf16[4,48,1536]{2,1,0:T(8,128)(2,1)S(1)}, bf16[4,48,1536]{2,1,0:T(8,128)(2,1)}, u32[]{:S(2)}, u32[]{:S(2)}) collective-permute-start(bf16[4,48,1536]{2,1,0:T(8,128)(2,1)S(1)} %copy-done.118), channel_id=1, source_target_pairs={{0,1},{1,0},{2,3},{3,2},{4,5},{5,4},{6,7},{7,6},{8,9},{9,8},{10,11... | collective-permute-start | bytes 1769480 | tf_op jit(solution)/shard_map/ppermute | solution.py:95
  573.3 119.6 %collective-permute-start.88 = (bf16[4,48,1536]{2,1,0:T(8,128)(2,1)}, bf16[4,48,1536]{2,1,0:T(8,128)(2,1)}, u32[]{:S(2)}, u32[]{:S(2)}) collective-permute-start(bf16[4,48,1536]{2,1,0:T(8,128)(2,1)} %collective-permute-done.87), channel_id=1, source_target_pairs={{0,1},{1,0},{2,3},{3,2},{4,5},{5,4},{6,7},{7,6},{8,9},{9,8},{10,11... | collective-permute-start | bytes 1769480 | tf_op jit(solution)/shard_map/ppermute | solution.py:95
  573.4 50.8 %collective-permute-start.68 = (bf16[2,64,1536]{2,1,0:T(8,128)(2,1)}, bf16[2,64,1536]{2,1,0:T(8,128)(2,1)}, u32[]{:S(2)}, u32[]{:S(2)}) collective-permute-start(bf16[2,64,1536]{2,1,0:T(8,128)(2,1)} %slice.835), channel_id=1, source_target_pairs={{0,16},{8,24},{16,0},{24,8},{1,17},{9,25},{17,1},{25,9},{2,18},{10... | collective-permute-start | bytes 1179656 | tf_op jit(solution)/shard_map/ppermute | solution.py:105
  584.8 42.1 %collective-permute-start.69 = (bf16[2,64,1536]{2,1,0:T(8,128)(2,1)}, bf16[2,64,1536]{2,1,0:T(8,128)(2,1)}, u32[]{:S(2)}, u32[]{:S(2)}) collective-permute-start(bf16[2,64,1536]{2,1,0:T(8,128)(2,1)} %slice.836), channel_id=1, source_target_pairs={{0,8},{8,0},{16,24},{24,16},{1,9},{9,1},{17,25},{25,17},{2,10},{10... | collective-permute-start | bytes 1179656 | tf_op jit(solution)/shard_map/ppermute | solution.py:105
  624.1 143.1 %collective-permute-start.105 = (bf16[1,192,1536]{2,1,0:T(8,128)(2,1)}, bf16[1,192,1536]{2,1,0:T(8,128)(2,1)}, u32[]{:S(2)}, u32[]{:S(2)}) collective-permute-start(bf16[1,192,1536]{2,1,0:T(8,128)(2,1)} %slice.859), channel_id=1, source_target_pairs={{0,16},{8,24},{16,0},{24,8},{1,17},{9,25},{17,1},{25,9},{2,18},{10... | collective-permute-start | bytes 1769480 | tf_op jit(solution)/shard_map/ppermute | solution.py:105
  626.9 140.3 %collective-permute-start.106 = (bf16[1,192,1536]{2,1,0:T(8,128)(2,1)}, bf16[1,192,1536]{2,1,0:T(8,128)(2,1)}, u32[]{:S(2)}, u32[]{:S(2)}) collective-permute-start(bf16[1,192,1536]{2,1,0:T(8,128)(2,1)} %slice.860), channel_id=1, source_target_pairs={{0,8},{8,0},{16,24},{24,16},{1,9},{9,1},{17,25},{25,17},{2,10},{10... | collective-permute-start | bytes 1769480 | tf_op jit(solution)/shard_map/ppermute | solution.py:105
  678.6 90.9 %collective-permute-start.120 = (bf16[4,128,1536]{2,1,0:T(8,128)(2,1)}, bf16[4,128,1536]{2,1,0:T(8,128)(2,1)}, u32[]{:S(2)}, u32[]{:S(2)}) collective-permute-start(bf16[4,128,1536]{2,1,0:T(8,128)(2,1)} %constant_dynamic-slice_fusion.5), channel_id=1, source_target_pairs={{0,1},{1,0},{2,3},{3,2},{4,5},{5,4},{6,7},{7,6},{8,9},{9,8},{10,11... | collective-permute-start | bytes 4718600 | tf_op jit(solution)/shard_map/ppermute | solution.py:95
  877.3 53.9 %collective-permute-start.107 = (bf16[4,128,1536]{2,1,0:T(8,128)(2,1)}, bf16[4,128,1536]{2,1,0:T(8,128)(2,1)}, u32[]{:S(2)}, u32[]{:S(2)}) collective-permute-start(bf16[4,128,1536]{2,1,0:T(8,128)(2,1)} %bitcast.199), channel_id=1, source_target_pairs={{0,1},{1,0},{2,3},{3,2},{4,5},{5,4},{6,7},{7,6},{8,9},{9,8},{10,11... | collective-permute-start | bytes 4718600 | tf_op jit(solution)/shard_map/ppermute | solution.py:95
  880.9 46.5 %collective-permute-start.121 = (bf16[4,128,1536]{2,1,0:T(8,128)(2,1)}, bf16[4,128,1536]{2,1,0:T(8,128)(2,1)}, u32[]{:S(2)}, u32[]{:S(2)}) collective-permute-start(bf16[4,128,1536]{2,1,0:T(8,128)(2,1)} %bitcast.218), channel_id=1, source_target_pairs={{0,1},{1,0},{2,3},{3,2},{4,5},{5,4},{6,7},{7,6},{8,9},{9,8},{10,11... | collective-permute-start | bytes 4718600 | tf_op jit(solution)/shard_map/ppermute | solution.py:95
  887.5 36.2 %collective-permute-start.204 = (bf16[1,384,1536]{2,1,0:T(8,128)(2,1)}, bf16[1,384,1536]{2,1,0:T(8,128)(2,1)}, u32[]{:S(2)}, u32[]{:S(2)}) collective-permute-start(bf16[1,384,1536]{2,1,0:T(8,128)(2,1)} %get-tuple-element.137), channel_id=1, source_target_pairs={{0,16},{8,24},{16,0},{24,8},{1,17},{9,25},{17,1},{25,9},{2,18},{10... | collective-permute-start | bytes 3538952 | tf_op jit(solution)/shard_map/ppermute | solution.py:105
  899.6 128.0 %collective-permute-start.206 = (bf16[1,384,1536]{2,1,0:T(8,128)(2,1)}, bf16[1,384,1536]{2,1,0:T(8,128)(2,1)}, u32[]{:S(2)}, u32[]{:S(2)}) collective-permute-start(bf16[1,384,1536]{2,1,0:T(8,128)(2,1)} %get-tuple-element.138), channel_id=1, source_target_pairs={{0,8},{8,0},{16,24},{24,16},{1,9},{9,1},{17,25},{25,17},{2,10},{10... | collective-permute-start | bytes 3538952 | tf_op jit(solution)/shard_map/ppermute | solution.py:105
  903.4 171.3 %collective-permute-start.213 = (bf16[2,192,1536]{2,1,0:T(8,128)(2,1)}, bf16[2,192,1536]{2,1,0:T(8,128)(2,1)}, u32[]{:S(2)}, u32[]{:S(2)}) collective-permute-start(bf16[2,192,1536]{2,1,0:T(8,128)(2,1)} %pad_maximum_fusion.30), channel_id=1, source_target_pairs={{0,8},{8,0},{16,24},{24,16},{1,9},{9,1},{17,25},{25,17},{2,10},{10... | collective-permute-start | bytes 3538952 | tf_op jit(solution)/shard_map/ppermute | solution.py:105
  923.6 151.1 %collective-permute-start.215 = (bf16[2,192,1536]{2,1,0:T(8,128)(2,1)}, bf16[2,192,1536]{2,1,0:T(8,128)(2,1)}, u32[]{:S(2)}, u32[]{:S(2)}) collective-permute-start(bf16[2,192,1536]{2,1,0:T(8,128)(2,1)} %pad_maximum_fusion.31), channel_id=1, source_target_pairs={{0,16},{8,24},{16,0},{24,8},{1,17},{9,25},{17,1},{25,9},{2,18},{10... | collective-permute-start | bytes 3538952 | tf_op jit(solution)/shard_map/ppermute | solution.py:105
  993.8 95.4 %collective-permute-start.205 = (bf16[2,384,1536]{2,1,0:T(8,128)(2,1)}, bf16[2,384,1536]{2,1,0:T(8,128)(2,1)}, u32[]{:S(2)}, u32[]{:S(2)}) collective-permute-start(bf16[2,384,1536]{2,1,0:T(8,128)(2,1)} %pad_maximum_fusion.14), channel_id=1, source_target_pairs={{0,8},{8,0},{16,24},{24,16},{1,9},{9,1},{17,25},{25,17},{2,10},{10... | collective-permute-start | bytes 7077896 | tf_op jit(solution)/shard_map/ppermute | solution.py:105
  1057.7 51.9 %collective-permute-start.207 = (bf16[2,384,1536]{2,1,0:T(8,128)(2,1)}, bf16[2,384,1536]{2,1,0:T(8,128)(2,1)}, u32[]{:S(2)}, u32[]{:S(2)}) collective-permute-start(bf16[2,384,1536]{2,1,0:T(8,128)(2,1)} %pad_maximum_fusion.15), channel_id=1, source_target_pairs={{0,16},{8,24},{16,0},{24,8},{1,17},{9,25},{17,1},{25,9},{2,18},{10... | collective-permute-start | bytes 7077896 | tf_op jit(solution)/shard_map/ppermute | solution.py:105
  1162.3 74.7 %collective-permute-start.167 = (bf16[4,4,64,1536]{3,2,1,0:T(8,128)(2,1)}, bf16[4,4,64,1536]{3,2,1,0:T(8,128)(2,1)}, u32[]{:S(2)}, u32[]{:S(2)}) collective-permute-start(bf16[4,4,64,1536]{3,2,1,0:T(8,128)(2,1)} %dynamic-slice_bitcast_fusion), channel_id=1, source_target_pairs={{0,1},{1,0},{2,3},{3,2},{4,5},{5,4},{6,7},{7,6},{8,9},{9,8},{10,11... | collective-permute-start | bytes 9437192 | tf_op jit(solution)/shard_map/ppermute | solution.py:95
  1162.4 71.7 %collective-permute-start.196 = (bf16[48,1536]{1,0:T(8,128)(2,1)S(1)}, bf16[48,1536]{1,0:T(8,128)(2,1)S(1)}, u32[]{:S(2)}, u32[]{:S(2)}) collective-permute-start(bf16[48,1536]{1,0:T(8,128)(2,1)S(1)} %get-tuple-element.203), channel_id=1, source_target_pairs={{0,2},{1,3},{2,4},{3,5},{4,6},{5,7},{8,10},{9,11},{10,12},{11,13},... | collective-permute-start | bytes 442376 | tf_op jit(solution)/shard_map/ppermute | solution.py:101
  1167.8 67.6 %collective-permute-start.199 = (bf16[48,1536]{1,0:T(8,128)(2,1)}, bf16[48,1536]{1,0:T(8,128)(2,1)S(1)}, u32[]{:S(2)}, u32[]{:S(2)}) collective-permute-start(bf16[48,1536]{1,0:T(8,128)(2,1)} %fusion.165), channel_id=1, source_target_pairs={{2,0},{3,1},{4,2},{5,3},{6,4},{7,5},{10,8},{11,9},{12,10},{13,11},... | collective-permute-start | bytes 442376 | tf_op jit(solution)/shard_map/ppermute | solution.py:101
  1234.0 38.8 %collective-permute-start.200 = (bf16[1,384,1536]{2,1,0:T(8,128)(2,1)}, bf16[1,384,1536]{2,1,0:T(8,128)(2,1)}, u32[]{:S(2)}, u32[]{:S(2)}) collective-permute-start(bf16[1,384,1536]{2,1,0:T(8,128)(2,1)} %get-tuple-element.135), channel_id=1, source_target_pairs={{0,16},{8,24},{16,0},{24,8},{1,17},{9,25},{17,1},{25,9},{2,18},{10... | collective-permute-start | bytes 3538952 | tf_op jit(solution)/shard_map/ppermute | solution.py:105
  1235.4 41.8 %collective-permute-start.202 = (bf16[1,384,1536]{2,1,0:T(8,128)(2,1)}, bf16[1,384,1536]{2,1,0:T(8,128)(2,1)S(1)}, u32[]{:S(2)}, u32[]{:S(2)}) collective-permute-start(bf16[1,384,1536]{2,1,0:T(8,128)(2,1)} %get-tuple-element.136), channel_id=1, source_target_pairs={{0,8},{8,0},{16,24},{24,16},{1,9},{9,1},{17,25},{25,17},{2,10},{10... | collective-permute-start | bytes 3538952 | tf_op jit(solution)/shard_map/ppermute | solution.py:105
  1237.0 42.7 %collective-permute-start.142 = (bf16[4,128,1536]{2,1,0:T(8,128)(2,1)S(1)}, bf16[4,128,1536]{2,1,0:T(8,128)(2,1)S(1)}, u32[]{:S(2)}, u32[]{:S(2)}) collective-permute-start(bf16[4,128,1536]{2,1,0:T(8,128)(2,1)S(1)} %bitcast.1175), channel_id=1, source_target_pairs={{0,1},{1,0},{2,3},{3,2},{4,5},{5,4},{6,7},{7,6},{8,9},{9,8},{10,11... | collective-permute-start | bytes 4718600 | tf_op jit(solution)/shard_map/ppermute | solution.py:95
  1270.2 70.9 %collective-permute-start.209 = (bf16[2,192,1536]{2,1,0:T(8,128)(2,1)S(1)}, bf16[2,192,1536]{2,1,0:T(8,128)(2,1)S(1)}, u32[]{:S(2)}, u32[]{:S(2)}) collective-permute-start(bf16[2,192,1536]{2,1,0:T(8,128)(2,1)S(1)} %pad_maximum_fusion.28), channel_id=1, source_target_pairs={{0,8},{8,0},{16,24},{24,16},{1,9},{9,1},{17,25},{25,17},{2,10},{10... | collective-permute-start | bytes 3538952 | tf_op jit(solution)/shard_map/ppermute | solution.py:105
  1271.4 74.2 %collective-permute-start.211 = (bf16[2,192,1536]{2,1,0:T(8,128)(2,1)S(1)}, bf16[2,192,1536]{2,1,0:T(8,128)(2,1)S(1)}, u32[]{:S(2)}, u32[]{:S(2)}) collective-permute-start(bf16[2,192,1536]{2,1,0:T(8,128)(2,1)S(1)} %pad_maximum_fusion.29), channel_id=1, source_target_pairs={{0,16},{8,24},{16,0},{24,8},{1,17},{9,25},{17,1},{25,9},{2,18},{10... | collective-permute-start | bytes 3538952 | tf_op jit(solution)/shard_map/ppermute | solution.py:105
  1272.8 43.1 %collective-permute-start.169 = (bf16[4,64,1536]{2,1,0:T(8,128)(2,1)S(1)}, bf16[4,64,1536]{2,1,0:T(8,128)(2,1)S(1)}, u32[]{:S(2)}, u32[]{:S(2)}) collective-permute-start(bf16[4,64,1536]{2,1,0:T(8,128)(2,1)S(1)} %pad_maximum_fusion.36), channel_id=1, source_target_pairs={{0,8},{8,0},{16,24},{24,16},{1,9},{9,1},{17,25},{25,17},{2,10},{10... | collective-permute-start | bytes 2359304 | tf_op jit(solution)/shard_map/ppermute | solution.py:105
  1277.2 44.1 %collective-permute-start.171 = (bf16[4,64,1536]{2,1,0:T(8,128)(2,1)S(1)}, bf16[4,64,1536]{2,1,0:T(8,128)(2,1)S(1)}, u32[]{:S(2)}, u32[]{:S(2)}) collective-permute-start(bf16[4,64,1536]{2,1,0:T(8,128)(2,1)S(1)} %pad_maximum_fusion.37), channel_id=1, source_target_pairs={{0,16},{8,24},{16,0},{24,8},{1,17},{9,25},{17,1},{25,9},{2,18},{10... | collective-permute-start | bytes 2359304 | tf_op jit(solution)/shard_map/ppermute | solution.py:105
  1279.8 160.4 %collective-permute-start.201 = (bf16[2,384,1536]{2,1,0:T(8,128)(2,1)}, bf16[2,384,1536]{2,1,0:T(8,128)(2,1)}, u32[]{:S(2)}, u32[]{:S(2)}) collective-permute-start(bf16[2,384,1536]{2,1,0:T(8,128)(2,1)} %pad_maximum_fusion.12), channel_id=1, source_target_pairs={{0,8},{8,0},{16,24},{24,16},{1,9},{9,1},{17,25},{25,17},{2,10},{10... | collective-permute-start | bytes 7077896 | tf_op jit(solution)/shard_map/ppermute | solution.py:105
  1334.6 105.6 %collective-permute-start.203 = (bf16[2,384,1536]{2,1,0:T(8,128)(2,1)}, bf16[2,384,1536]{2,1,0:T(8,128)(2,1)}, u32[]{:S(2)}, u32[]{:S(2)}) collective-permute-start(bf16[2,384,1536]{2,1,0:T(8,128)(2,1)} %pad_maximum_fusion.13), channel_id=1, source_target_pairs={{0,16},{8,24},{16,0},{24,8},{1,17},{9,25},{17,1},{25,9},{2,18},{10... | collective-permute-start | bytes 7077896 | tf_op jit(solution)/shard_map/ppermute | solution.py:105
  1365.5 72.1 %collective-permute-start.174 = (bf16[64,1536]{1,0:T(8,128)(2,1)}, bf16[64,1536]{1,0:T(8,128)(2,1)}, u32[]{:S(2)}, u32[]{:S(2)}) collective-permute-start(bf16[64,1536]{1,0:T(8,128)(2,1)} %get-tuple-element.189), channel_id=1, source_target_pairs={{0,2},{1,3},{2,4},{3,5},{4,6},{5,7},{8,10},{9,11},{10,12},{11,13},... | collective-permute-start | bytes 589832 | tf_op jit(solution)/shard_map/ppermute | solution.py:101
  (386 other events, 7732.3 us)

commit v2 on v1

--- a/solution.py
+++ b/solution.py
@@ -1,6 +1,8 @@
 import jax
 import jax.numpy as jnp
 from jax import lax
+from jax.experimental import pallas as pl
+from jax.experimental.pallas import tpu as pltpu
 from jax.sharding import PartitionSpec as P
 
 D = 1536
@@ -88,7 +90,747 @@
     return lax.optimization_barrier((value, *earlier))[0]
 
 
+ROWS = 128
 LINE = 4
+GROUP = 2 * LINE * ROWS
+HALF = GROUP // 2
+QROWS = QKV // 32
+OROWS = HQ // 32
+GROWS = D // 4
+FROWS = FF // 4
+SMALL = 16
+EXPERTS = 2 * LINE * EXP_DEV
+
+
+def cost(microseconds):
+    return pl.CostEstimate(flops=0, bytes_accessed=int(microseconds * 0.4e6), transcendentals=0)
+
+
+LIMIT = 60 * 1024 * 1024
+SCALE = HEAD**-0.5
+
+
+def spec(shape, index=None):
+    if index is None:
+        index = lambda *unused: (0,) * len(shape)
+    return pl.BlockSpec(shape, index)
+
+
+ANYWHERE = pl.BlockSpec(memory_space=pl.ANY)
+SCALARS = pl.BlockSpec(memory_space=pltpu.SMEM)
+
+
+def place_scalars():
+    dp, cp = lax.axis_index("dp"), lax.axis_index("cp")
+    return jnp.stack([dp, cp % 2, cp, cp // 2]).astype(jnp.int32)
+
+
+def call(body, name, grid, arguments, in_specs, outs, out_specs, scratch, microseconds):
+    return pl.pallas_call(
+        body,
+        grid=grid,
+        out_shape=outs,
+        in_specs=in_specs,
+        out_specs=out_specs,
+        scratch_shapes=scratch,
+        name=name,
+        compiler_params=pltpu.CompilerParams(vmem_limit_bytes=LIMIT),
+        cost_estimate=cost(microseconds),
+    )(*arguments)
+
+
+def shape(dims, dtype):
+    return jax.ShapeDtypeStruct(dims, dtype)
+
+
+class Dense:
+    def __init__(self, pieces, first_row, rows):
+        self.pieces = pieces
+        self.rows = rows
+        self.first_row = first_row
+
+    def arrays(self):
+        return [piece[0] for piece in self.pieces]
+
+    def copies(self, refs, places, scratch, sems):
+        made = []
+        for number, (ref, piece) in enumerate(zip(refs, self.pieces)):
+            unused, part, flip, other, chip, chips = piece
+            rows = pl.ds(self.first_row, self.rows)
+            source = ref.at[:, rows] if part is None else ref.at[:, part, rows]
+            target = scratch.at[places[0] ^ flip, pl.ds(chip, chips), places[1] ^ other]
+            made.append(pltpu.make_async_copy(source, target, sems.at[number]))
+        return made
+
+    def scratch(self):
+        return [
+            pltpu.VMEM((4, LINE, 2, self.rows, D), LOW),
+            pltpu.SemaphoreType.DMA((len(self.pieces),)),
+        ]
+
+
+def expert_copies(refs, places, gate_up, down, sems):
+    made = []
+    for expert in range(EXP_DEV):
+        for flip in range(4):
+            part = places[0] ^ flip
+            first = pl.multiple_of(part * GROWS, GROWS)
+            target = gate_up.at[expert, pl.ds(first, GROWS)]
+            made.append((refs[4 * expert + flip], target))
+            source = refs[8 + flip].at[expert] if flip < 3 else refs[11 + expert]
+            first = pl.multiple_of(part * FROWS, FROWS)
+            made.append((source, down.at[expert, pl.ds(first, FROWS)]))
+    return [
+        pltpu.make_async_copy(source, target, sems.at[number])
+        for number, (source, target) in enumerate(made)
+    ]
+
+
+EXPERT_SCRATCH = [
+    pltpu.VMEM((EXP_DEV, D, 2 * FF), LOW),
+    pltpu.VMEM((EXP_DEV, FF, D), LOW),
+    pltpu.SemaphoreType.DMA((16,)),
+]
+
+
+def logistic_of(values):
+    return 0.5 * jnp.tanh(0.5 * values) + 0.5
+
+
+def norm_rows(values, gain):
+    return (values * inverse_rms(values) * gain).astype(LOW)
+
+
+def turn(values, cosine, sine):
+    return values * cosine + pltpu.roll(values, HEAD // 2, 1) * sine
+
+
+def small_call(pieces):
+    count = len(pieces.pieces)
+
+    def body(places, *rest):
+        refs, (out, sems) = rest[:count], rest[count:]
+        copies = pieces.copies(refs, places, out, sems)
+        for copy in copies:
+            copy.start()
+        for copy in copies:
+            copy.wait()
+
+    out = shape((4, LINE, 2, SMALL, D), LOW)
+    return call(
+        body,
+        "small",
+        (),
+        [place_scalars(), *pieces.arrays()],
+        [SCALARS] + [ANYWHERE] * count,
+        out,
+        spec(out.shape),
+        [pltpu.SemaphoreType.DMA((count,))],
+        3,
+    )
+
+
+def project_call(value, gain, query, tables):
+    count = len(query.pieces)
+
+    def body(places, value_ref, gain_ref, tables_ref, *rest):
+        refs, (normed_ref, heads_ref, kv_ref, weight, sems, joined) = rest[:count], rest[count:]
+        copies = query.copies(refs, places, weight, sems)
+        for copy in copies:
+            copy.start()
+        normed = norm_rows(value_ref[...], gain_ref[...])
+        normed_ref[...] = normed
+        for copy in copies:
+            copy.wait()
+        for part in range(4):
+            joined[part] = dot_t(normed, weight[part].reshape(8 * QROWS, D))
+        cosine, sine = tables_ref[0], tables_ref[1]
+        for head in range(HEADS + 2 * KV_HEADS):
+            at = pl.ds(head % 4 * HEAD, HEAD)
+            values = joined[head // 4, :, at]
+            if head < HEADS:
+                heads_ref[head] = turn(values, cosine, sine).astype(LOW)
+            else:
+                if head < HEADS + KV_HEADS:
+                    values = turn(values, cosine, sine)
+                kv_ref[:, pl.ds((head - HEADS) * HEAD, HEAD)] = values.astype(LOW)
+
+    outs = [shape((ROWS, D), LOW), shape((HEADS, ROWS, HEAD), LOW), shape((ROWS, 2 * KVW), LOW)]
+    arguments = [place_scalars(), value, gain, tables, *query.arrays()]
+    return call(
+        body,
+        "project",
+        (),
+        arguments,
+        [SCALARS, spec((ROWS, D)), spec((1, D)), spec((2, ROWS, HEAD))] + [ANYWHERE] * count,
+        outs,
+        [spec(o.shape) for o in outs],
+        [*query.scratch(), pltpu.VMEM((4, ROWS, 8 * QROWS), WIDE)],
+        7,
+    )
+
+
+def attend_call(value, heads, keys_values, query_meta, key_meta, output, gain):
+    count = len(output.pieces)
+
+    def body(places, value_ref, heads_ref, kv_own, kv_other, qmeta, kmeta, gain_ref, *rest):
+        refs, (low_ref, probs_ref, middle_ref, mixed_ref, weight, sems, joined, kv_ref) = (
+            rest[:count],
+            rest[count:],
+        )
+        copies = output.copies(refs, places, weight, sems)
+        for copy in copies:
+            copy.start()
+        kv_ref[pl.ds(0, HALF)] = kv_own[...]
+        kv_ref[pl.ds(HALF, HALF)] = kv_other[...]
+        allowed = (qmeta[:, 1:2] == kmeta[1:2, :]) & (kmeta[0:1, :] <= qmeta[:, 0:1])
+        for head in range(HEADS):
+            kv = head // Q_PER_KV
+            keys = kv_ref[:, pl.ds(kv * HEAD, HEAD)]
+            vals = kv_ref[:, pl.ds(KVW + kv * HEAD, HEAD)]
+            scores = dot_t(heads_ref[head], keys) * SCALE
+            scores = jnp.where(allowed, scores, MASKED)
+            shares = jnp.exp(scores - jnp.max(scores, axis=1, keepdims=True))
+            probs = (shares * (1.0 / jnp.sum(shares, axis=1, keepdims=True))).astype(LOW)
+            probs_ref[head] = probs
+            joined[:, pl.ds(head * HEAD, HEAD)] = dot(probs, vals).astype(LOW)
+        low = joined[...]
+        low_ref[...] = low
+        for copy in copies:
+            copy.wait()
+        middle = value_ref[...] + dot(low, weight[...].reshape(HQ, D))
+        middle_ref[...] = middle
+        mixed_ref[...] = norm_rows(middle, gain_ref[...])
+
+    outs = [
+        shape((ROWS, HQ), LOW),
+        shape((HEADS, ROWS, GROUP), LOW),
+        shape((ROWS, D), WIDE),
+        shape((ROWS, D), LOW),
+    ]
+    arguments = [
+        place_scalars(),
+        value,
+        heads,
+        *keys_values,
+        query_meta,
+        key_meta,
+        gain,
+        *output.arrays(),
+    ]
+    return call(
+        body,
+        "attend",
+        (),
+        arguments,
+        [
+            SCALARS,
+            spec((ROWS, D)),
+            spec((HEADS, ROWS, HEAD)),
+            spec((HALF, 2 * KVW)),
+            spec((HALF, 2 * KVW)),
+            spec((ROWS, 2)),
+            spec((2, GROUP)),
+            spec((1, D)),
+        ]
+        + [ANYWHERE] * count,
+        outs,
+        [spec(o.shape) for o in outs],
+        [*output.scratch(), pltpu.VMEM((ROWS, HQ), LOW), pltpu.VMEM((GROUP, 2 * KVW), LOW)],
+        9,
+    )
+
+
+BLOCK = 256
+STEPS = GROUP // BLOCK
+
+
+def own_half(step):
+    return (jnp.minimum(step, STEPS // 2 - 1), 0)
+
+
+def other_half(step):
+    return (jnp.maximum(step - STEPS // 2, 0), 0)
+
+
+def rows_at(step):
+    return (step, 0)
+
+
+def take_half(step, own_ref, other_ref):
+    return jnp.where(step < STEPS // 2, own_ref[...], other_ref[...])
+
+
+def put_halves(step, own_ref, other_ref, values):
+    @pl.when(step < STEPS // 2)
+    def own():
+        own_ref[...] = values
+
+    @pl.when(step >= STEPS // 2)
+    def other():
+        other_ref[...] = values
+
+
+def own_gate(gates, places, expert):
+    ids = lax.broadcasted_iota(jnp.int32, gates.shape, 1)
+    return jnp.sum(
+        jnp.where(ids == EXP_DEV * places[2] + expert, gates, 0.0), axis=1, keepdims=True
+    )
+
+
+def experts_call(mixed, routes, router, pieces):
+    def body(places, mixed_own, mixed_other, routes_ref, router_ref, *rest):
+        refs, (own_ref, other_ref, gu_ref, hidden_ref, gates_ref, gate_up, down, sems) = (
+            rest[:13],
+            rest[13:],
+        )
+        step = pl.program_id(0)
+        copies = expert_copies(refs, places, gate_up, down, sems)
+
+        @pl.when(step == 0)
+        def begin():
+            for copy in copies:
+                copy.start()
+            for copy in copies:
+                copy.wait()
+
+        mixed_rows = take_half(step, mixed_own, mixed_other)
+        logits = dot(mixed_rows, router_ref[...])
+        ids = lax.broadcasted_iota(jnp.int32, (BLOCK, EXPERTS), 1)
+        chosen = routes_ref[:, 0:1] == ids
+        for k in range(1, TOP):
+            chosen = chosen | (routes_ref[:, k : k + 1] == ids)
+        logits = jnp.where(chosen, logits, MASKED)
+        shares = jnp.where(chosen, jnp.exp(logits - jnp.max(logits, axis=1, keepdims=True)), 0.0)
+        gates = shares / jnp.sum(shares, axis=1, keepdims=True)
+        gates_ref[...] = gates
+
+        terms = None
+        for expert in range(EXP_DEV):
+            gu = dot(mixed_rows, gate_up[expert])
+            gu_ref[:, pl.ds(expert * 2 * FF, 2 * FF)] = gu.astype(LOW)
+            gate_part = gu[:, :FF]
+            hidden = gate_part * logistic_of(gate_part) * gu[:, FF:]
+            hidden = (hidden * own_gate(gates, places, expert)).astype(LOW)
+            hidden_ref[:, pl.ds(expert * FF, FF)] = hidden
+            product = dot(hidden, down[expert])
+            terms = product if terms is None else terms + product
+        put_halves(step, own_ref, other_ref, terms.astype(LOW))
+
+    outs = [
+        shape((HALF, D), LOW),
+        shape((HALF, D), LOW),
+        shape((GROUP, EXP_DEV * 2 * FF), LOW),
+        shape((GROUP, EXP_DEV * FF), LOW),
+        shape((GROUP, EXPERTS), WIDE),
+    ]
+    return call(
+        body,
+        "experts",
+        (STEPS,),
+        [place_scalars(), *mixed, routes, router, *pieces],
+        [
+            SCALARS,
+            spec((BLOCK, D), own_half),
+            spec((BLOCK, D), other_half),
+            spec((BLOCK, TOP), rows_at),
+            spec((D, EXPERTS)),
+        ]
+        + [ANYWHERE] * 13,
+        outs,
+        [
+            spec((BLOCK, D), own_half),
+            spec((BLOCK, D), other_half),
+            spec((BLOCK, EXP_DEV * 2 * FF), rows_at),
+            spec((BLOCK, EXP_DEV * FF), rows_at),
+            spec((BLOCK, EXPERTS), rows_at),
+        ],
+        EXPERT_SCRATCH,
+        26,
+    )
+
+
+def experts_back_call(upstream, gate_up_kept, gates, router, pieces):
+    def body(places, up_own, up_other, gu_ref, gates_ref, router_ref, *rest):
+        refs, (own_ref, other_ref, grad_ref, logits_ref, gate_up, down, sems) = (
+            rest[:13],
+            rest[13:],
+        )
+        step = pl.program_id(0)
+        copies = expert_copies(refs, places, gate_up, down, sems)
+
+        @pl.when(step == 0)
+        def begin():
+            for copy in copies:
+                copy.start()
+            for copy in copies:
+                copy.wait()
+
+        upstream_rows = take_half(step, up_own, up_other)
+        gates = gates_ref[...]
+        ids = lax.broadcasted_iota(jnp.int32, (BLOCK, EXPERTS), 1)
+        grad_logits = jnp.zeros((BLOCK, EXPERTS), WIDE)
+        terms = None
+        for expert in range(EXP_DEV):
+            bare = dot_t(upstream_rows, down[expert])
+            gate_part = gu_ref[:, pl.ds(expert * 2 * FF, FF)].astype(WIDE)
+            up_part = gu_ref[:, pl.ds(expert * 2 * FF + FF, FF)].astype(WIDE)
+            gate = own_gate(gates, places, expert)
+            logistic = logistic_of(gate_part)
+            activated = gate_part * logistic
+            share = gate * jnp.sum(bare * activated * up_part, axis=1, keepdims=True)
+            mine = jnp.where(ids == EXP_DEV * places[2] + expert, 1.0, 0.0)
+            grad_logits = grad_logits + share * (mine - gates)
+            gated = bare * gate
+            grad_gate = gated * up_part * logistic * (1.0 + gate_part * (1.0 - logistic))
+            grad_gate = grad_gate.astype(LOW)
+            grad_up = (gated * activated).astype(LOW)
+            grad_ref[:, pl.ds(expert * 2 * FF, FF)] = grad_gate
+            grad_ref[:, pl.ds(expert * 2 * FF + FF, FF)] = grad_up
+            grad_both = jnp.concatenate([grad_gate, grad_up], axis=1)
+            product = dot_t(grad_both, gate_up[expert])
+            terms = product if terms is None else terms + product
+        grad_logits = grad_logits.astype(LOW)
+        terms = terms + dot(grad_logits, router_ref[...])
+        put_halves(step, own_ref, other_ref, terms.astype(LOW))
+        logits_ref[...] = grad_logits
+
+    outs = [
+        shape((HALF, D), LOW),
+        shape((HALF, D), LOW),
+        shape((GROUP, EXP_DEV * 2 * FF), LOW),
+        shape((GROUP, EXPERTS), LOW),
+    ]
+    return call(
+        body,
+        "experts_back",
+        (STEPS,),
+        [place_scalars(), *upstream, gate_up_kept, gates, router, *pieces],
+        [
+            SCALARS,
+            spec((BLOCK, D), own_half),
+            spec((BLOCK, D), other_half),
+            spec((BLOCK, EXP_DEV * 2 * FF), rows_at),
+            spec((BLOCK, EXPERTS), rows_at),
+            spec((EXPERTS, D)),
+        ]
+        + [ANYWHERE] * 13,
+        outs,
+        [
+            spec((BLOCK, D), own_half),
+            spec((BLOCK, D), other_half),
+            spec((BLOCK, EXP_DEV * 2 * FF), rows_at),
+            spec((BLOCK, EXPERTS), rows_at),
+        ],
+        EXPERT_SCRATCH,
+        26,
+    )
+
+
+def expert_grads_call(
+    flips, mixed, grad_gate_up, hidden, upstream, received=(), layer=None, results=None
+):
+    last = layer is not None
+    apart = len(flips) == 1 and not last
+    kept = () if results is None else tuple(results)
+    count = len(flips)
+
+    def body(places, *rest):
+        mixed_refs, rest = rest[: 2 * count], rest[2 * count :]
+        hidden_refs, rest = rest[: 2 * count], rest[2 * count :]
+        grad_ref, up_own, up_other = rest[:3]
+        sums, outs = rest[3 : 3 + len(received)], rest[3 + len(received) + len(kept) :]
+        expert = pl.program_id(0)
+        for number, flip in enumerate(flips):
+            gate_up = t_dot(mixed_refs[2 * number][...], grad_ref[pl.ds(0, HALF)])
+            gate_up = gate_up + t_dot(mixed_refs[2 * number + 1][...], grad_ref[pl.ds(HALF, HALF)])
+            both = jnp.concatenate([hidden_refs[2 * number][...], hidden_refs[2 * number + 1][...]], axis=1)
+            down = t_dot(both[:HALF], up_own[...]) + t_dot(both[HALF:], up_other[...])
+            part = places[0] ^ flip
+            down = jnp.where(part % 2 == 0, down[:FROWS], down[2 * HEAD - FROWS :])
+            for ref, (unused, whose, only) in zip(sums, received):
+                if whose != number:
+                    continue
+                held = (ref[...] if only is not None else ref[0]).astype(WIDE)
+                if only is not None:
+                    held = jnp.where(expert == only, held, 0.0)
+                gate_up = gate_up + held[:GROWS]
+                down = down + held[GROWS:]
+            if last:
+                outs[0][0, 0] = gate_up
+                outs[1][0, 0] = down
+                continue
+            gate_up = gate_up.astype(LOW)
+            down = down.astype(LOW)
+            if apart:
+                for own in range(EXP_DEV):
+
+                    @pl.when(expert == own)
+                    def put():
+                        outs[own][pl.ds(0, GROWS)] = gate_up
+                        outs[own][pl.ds(GROWS, FROWS)] = down
+
+            else:
+                outs[number][0, pl.ds(0, GROWS)] = gate_up
+                outs[number][0, pl.ds(GROWS, FROWS)] = down
+
+    each = lambda e, places: (e, 0, 0)
+    whole = lambda e, places: (0, 0)
+    if last:
+        at_layer = lambda e, places: (layer, e, 0, 0)
+        outs = [shape((LAYERS, EXP_DEV, GROWS, D), WIDE), shape((LAYERS, EXP_DEV, FROWS, D), WIDE)]
+        out_specs = [
+            pl.BlockSpec((1, 1, GROWS, D), at_layer),
+            pl.BlockSpec((1, 1, FROWS, D), at_layer),
+        ]
+    elif apart:
+        outs = [shape((GROWS + FROWS, D), LOW)] * EXP_DEV
+        out_specs = [pl.BlockSpec((GROWS + FROWS, D), whole)] * EXP_DEV
+    else:
+        outs = [shape((EXP_DEV, GROWS + FROWS, D), LOW)] * count
+        out_specs = [pl.BlockSpec((1, GROWS + FROWS, D), each)] * count
+    in_specs = []
+    for flip in flips:
+        in_specs += [pl.BlockSpec((HALF, GROWS), lambda e, places, flip=flip: (0, places[0] ^ flip))] * 2
+    for flip in flips:
+        for side in range(2):
+            in_specs.append(
+                pl.BlockSpec(
+                    (GROUP, HEAD),
+                    lambda e, places, flip=flip, side=side: (
+                        0,
+                        e * (FF // HEAD) + (places[0] ^ flip) * 3 // 2 + side,
+                    ),
+                )
+            )
+    in_specs += [
+        pl.BlockSpec((GROUP, 2 * FF), lambda e, places: (0, e)),
+        pl.BlockSpec((HALF, D), whole),
+        pl.BlockSpec((HALF, D), whole),
+    ]
+    for unused, whose, only in received:
+        in_specs.append(
+            pl.BlockSpec((1, GROWS + FROWS, D), each)
+            if only is None
+            else pl.BlockSpec((GROWS + FROWS, D), whole)
+        )
+    in_specs += [ANYWHERE] * len(kept)
+    first_kept = 1 + 4 * count + 3 + len(received)
+    return pl.pallas_call(
+        body,
+        out_shape=outs,
+        input_output_aliases={first_kept + i: i for i in range(len(kept))},
+        grid_spec=pltpu.PrefetchScalarGridSpec(
+            num_scalar_prefetch=1, grid=(EXP_DEV,), in_specs=in_specs, out_specs=out_specs
+        ),
+        name="expert_grads",
+        compiler_params=pltpu.CompilerParams(vmem_limit_bytes=LIMIT),
+        cost_estimate=cost(15 if count > 1 else 11),
+    )(
+        place_scalars(),
+        *(list(mixed) * count),
+        *([hidden] * (2 * count)),
+        grad_gate_up,
+        *upstream,
+        *(array for array, unused, only in received),
+        *kept,
+    )
+
+
+def norm_back(values, gain, upstream):
+    scale_rows = inverse_rms(values)
+    weighted = gain * upstream
+    inner_mean = jnp.mean(values * weighted, axis=1, keepdims=True)
+    grads = scale_rows * (weighted - values * (scale_rows * scale_rows * inner_mean))
+    return (grads, jnp.sum(values * scale_rows * upstream, axis=0, keepdims=True))
+
+
+def attend_back_call(grad_mixed, middle, gain, upstream, output, low, probs, heads, keys_values):
+    count = len(output.pieces)
+
+    def body(
+        places, gm_ref, middle_ref, gain_ref, up_ref, low_in, probs_ref, heads_ref, kv_own, kv_other, *rest
+    ):
+        refs, (grad_ref, error_ref, gq_ref, own_ref, other_ref, gg_ref, weight, sems, kvs, kv_ref) = (
+            rest[:count],
+            rest[count:],
+        )
+        copies = output.copies(refs, places, weight, sems)
+        for copy in copies:
+            copy.start()
+        kv_ref[pl.ds(0, HALF)] = kv_own[...]
+        kv_ref[pl.ds(HALF, HALF)] = kv_other[...]
+        grads, gain_grad = norm_back(middle_ref[...], gain_ref[...], gm_ref[...])
+        gg_ref[...] = gain_grad
+        grads = grads + up_ref[...]
+        grad_ref[...] = grads
+        error = grads.astype(LOW)
+        error_ref[...] = error
+        for copy in copies:
+            copy.wait()
+        grad_attended = dot_t(error, weight[...].reshape(HQ, D)).astype(LOW)
+        for head in range(HEADS):
+            kv = head // Q_PER_KV
+            at = pl.ds(kv * HEAD, HEAD)
+            at_values = pl.ds(KVW + kv * HEAD, HEAD)
+            grad_head = grad_attended[:, head * HEAD : (head + 1) * HEAD]
+            delta = jnp.sum(
+                grad_head.astype(WIDE) * low_in[:, pl.ds(head * HEAD, HEAD)].astype(WIDE),
+                axis=1,
+                keepdims=True,
+            )
+            shares = probs_ref[head]
+            grad_scores = dot_t(grad_head, kv_ref[:, at_values]) - delta
+            grad_scores = (shares.astype(WIDE) * grad_scores * SCALE).astype(LOW)
+            gq_ref[head] = dot(grad_scores, kv_ref[:, at])
+            grad_keys = t_dot(grad_scores, heads_ref[head])
+            grad_values = t_dot(shares, grad_head)
+            if head % Q_PER_KV == 0:
+                kvs[:, at] = grad_keys
+                kvs[:, at_values] = grad_values
+            else:
+                kvs[:, at] += grad_keys
+                kvs[:, at_values] += grad_values
+        own_ref[...] = kvs[pl.ds(0, HALF)].astype(LOW)
+        other_ref[...] = kvs[pl.ds(HALF, HALF)].astype(LOW)
+
+    outs = [
+        shape((ROWS, D), WIDE),
+        shape((ROWS, D), LOW),
+        shape((HEADS, ROWS, HEAD), WIDE),
+        shape((HALF, 2 * KVW), LOW),
+        shape((HALF, 2 * KVW), LOW),
+        shape((1, D), WIDE),
+    ]
+    arguments = [
+        place_scalars(),
+        grad_mixed,
+        middle,
+        gain,
+        upstream,
+        low,
+        probs,
+        heads,
+        *keys_values,
+        *output.arrays(),
+    ]
+    return call(
+        body,
+        "attend_back",
+        (),
+        arguments,
+        [SCALARS] + [spec(a.shape) for a in arguments[1:10]] + [ANYWHERE] * count,
+        outs,
+        [spec(o.shape) for o in outs],
+        [*output.scratch(), pltpu.VMEM((GROUP, 2 * KVW), WIDE), pltpu.VMEM((GROUP, 2 * KVW), LOW)],
+        12,
+    )
+
+
+def project_back_call(grad_heads, grad_kv, tables, query, value, gain, grad_middle):
+    count = len(query.pieces)
+
+    def body(places, gq_ref, gkv_ref, tables_ref, value_ref, gain_ref, gm_ref, *rest):
+        refs, (joined_ref, grad_ref, low_ref, gg_ref, weight, sems) = rest[:count], rest[count:]
+        copies = query.copies(refs, places, weight, sems)
+        for copy in copies:
+            copy.start()
+        cosine, sine = tables_ref[0], -tables_ref[1]
+        for head in range(HEADS + 2 * KV_HEADS):
+            if head < HEADS:
+                values = turn(gq_ref[head], cosine, sine)
+            else:
+                values = gkv_ref[:, pl.ds((head - HEADS) * HEAD, HEAD)]
+                if head < HEADS + KV_HEADS:
+                    values = turn(values, cosine, sine)
+            joined_ref[:, pl.ds(head * HEAD, HEAD)] = values.astype(LOW)
+        for copy in copies:
+            copy.wait()
+        grad_normed = dot(joined_ref[...], weight[...].reshape(QKV, D))
+        grads, gain_grad = norm_back(value_ref[...], gain_ref[...], grad_normed)
+        gg_ref[...] = gain_grad
+        grads = grads + gm_ref[...]
+        grad_ref[...] = grads
+        low_ref[...] = grads.astype(LOW)
+
+    outs = [
+        shape((ROWS, QKV), LOW),
+        shape((ROWS, D), WIDE),
+        shape((ROWS, D), LOW),
+        shape((1, D), WIDE),
+    ]
+    arguments = [
+        place_scalars(),
+        grad_heads,
+        grad_kv,
+        tables,
+        value,
+        gain,
+        grad_middle,
+        *query.arrays(),
+    ]
+    return call(
+        body,
+        "project_back",
+        (),
+        arguments,
+        [SCALARS] + [spec(a.shape) for a in arguments[1:7]] + [ANYWHERE] * count,
+        outs,
+        [spec(o.shape) for o in outs],
+        query.scratch(),
+        7,
+    )
+
+
+def dense_grads_call(joined, normed, low, error, small):
+    rows = QROWS + OROWS + (SMALL if small is not None else 0)
+
+    def body(places, joined_ref, normed_ref, low_ref, error_ref, *rest):
+        mine_ref, other_ref = rest[-2:]
+        query = t_dot(joined_ref[...], normed_ref[...]).astype(LOW).reshape(LINE, 2, QROWS, D)
+        outs = t_dot(low_ref[...], error_ref[...]).astype(LOW).reshape(LINE, 2, OROWS, D)
+        for core in range(2):
+
+            def put(ref):
+                ref[0, :, pl.ds(0, QROWS)] = query[:, core]
+                ref[0, :, pl.ds(QROWS, OROWS)] = outs[:, core]
+                if small is not None:
+                    ref[0, :, pl.ds(QROWS + OROWS, SMALL)] = rest[0][0, :, core]
+
+            @pl.when(places[1] == core)
+            def mine():
+                put(mine_ref)
+
+            @pl.when(places[1] != core)
+            def other():
+                put(other_ref)
+
+    out = shape((4, LINE, rows, D), LOW)
+    part = lambda flip, places: (0, places[0] ^ flip)
+    whole = lambda flip, places: (0, 0)
+    in_specs = [
+        pl.BlockSpec((ROWS, QKV // 4), part),
+        pl.BlockSpec((ROWS, D), whole),
+        pl.BlockSpec((ROWS, HQ // 4), part),
+        pl.BlockSpec((ROWS, D), whole),
+    ]
+    arguments = [joined, normed, low, error]
+    if small is not None:
+        in_specs.append(
+            pl.BlockSpec((1, LINE, 2, SMALL, D), lambda flip, places: (places[0] ^ flip, 0, 0, 0, 0))
+        )
+        arguments.append(small)
+    out_spec = pl.BlockSpec((1, LINE, rows, D), lambda flip, places: (flip, 0, 0, 0))
+    return pl.pallas_call(
+        body,
+        out_shape=[out, out],
+        grid_spec=pltpu.PrefetchScalarGridSpec(
+            num_scalar_prefetch=1, grid=(4,), in_specs=in_specs, out_specs=[out_spec, out_spec]
+        ),
+        name="dense_grads",
+        compiler_params=pltpu.CompilerParams(vmem_limit_bytes=LIMIT),
+        cost_estimate=cost(9),
+    )(place_scalars(), *arguments)
 
 
 def swap_core(value):
@@ -101,15 +843,23 @@
     return lax.ppermute(value, "cp", pairs)
 
 
+def leap(value, distance):
+    pairs = [(i, i + 2 * distance) for i in range(2 * LINE) if 0 <= i + 2 * distance < 2 * LINE]
+    return lax.ppermute(value, "cp", pairs)
+
+
 def across(value, flip):
     return lax.ppermute(value, "dp", [(i, i ^ flip) for i in range(4)])
 
 
-def line_gather(value):
+def line_gather(value, *stages):
     place = lax.axis_index("cp") // 2
     rising, falling = value, value
     risen, fallen = [], []
     for step in range(1, LINE):
+        if step <= len(stages):
+            rising = after(rising, *stages[step - 1])
+            falling = after(falling, *stages[step - 1])
         rising = hop(rising, True, range(step - 1, LINE - 1))
         falling = hop(falling, False, range(1, LINE - step + 1))
         risen.insert(0, rising)
@@ -118,7 +868,13 @@
     return lax.dynamic_slice_in_dim(every, LINE - 1 - place, LINE, 0)
 
 
-def line_scatter(parts):
+def leap_gather(value):
+    place = lax.axis_index("cp") // 2
+    every = [leap(value, LINE - 1 - i) if i != LINE - 1 else value for i in range(2 * LINE - 1)]
+    return lax.dynamic_slice_in_dim(jnp.stack(every), LINE - 1 - place, LINE, 0)
+
+
+def line_scatter(parts, *stages):
     place = lax.axis_index("cp") // 2
 
     def pick(index):
@@ -131,93 +887,262 @@
         if step > 1:
             up = (up.astype(WIDE) + rising.astype(WIDE)).astype(LOW)
             down = (down.astype(WIDE) + falling.astype(WIDE)).astype(LOW)
+        if step <= len(stages):
+            up = after(up, *stages[step - 1])
+            down = after(down, *stages[step - 1])
         rising = hop(up, True, range(step))
         falling = hop(down, False, range(LINE - step, LINE))
     return pick(place).astype(WIDE) + rising.astype(WIDE) + falling.astype(WIDE)
 
 
-def square_gather(value):
-    half = value.shape[0] // 2
-    by_x = across(value, 1)
-    by_y = across(value, 2)
-    far = jnp.concatenate([across(by_x[:half], 2), across(by_y[half:], 1)], axis=0)
-    return (value, by_x, by_y, far)
-
-
-def square_scatter(piece):
-    far = piece(3)
-    half = far.shape[0] // 2
+def group_gather(value, *stages):
+    mine = line_gather(value, *stages[: LINE - 1])
+    for stage in stages[LINE - 1 :]:
+        mine = after(mine, *stage)
+    other = swap_core(mine)
+    return (mine.reshape(HALF, -1), other.reshape(HALF, -1))
+
+
+def group_scatter(own, other, first=(), *stages):
+    both = (own.astype(WIDE) + swap_core(after(other, *first)).astype(WIDE)).astype(LOW)
+    return line_scatter(both.reshape(LINE, ROWS, -1), *stages)
+
+
+def earlier_gather(value):
+    mine = jnp.stack([leap(value, 3), leap(value, 2), leap(value, 1), value])
+    other = swap_core(mine)
+    return (mine.reshape(HALF, -1), other.reshape(HALF, -1))
+
+
+def earlier_scatter(own, other):
+    both = (own.astype(WIDE) + swap_core(other).astype(WIDE)).astype(LOW).reshape(LINE, ROWS, -1)
+    total = both[LINE - 1].astype(WIDE)
+    for distance in range(1, LINE):
+        total = total + leap(both[LINE - 1 - distance], -distance).astype(WIDE)
+    return total
+
+
+def square_step(value):
+    return (across(value, 1), across(value, 2))
+
+
+def square_far(by_x, by_y):
+    half = by_x.shape[0] // 2
+    return (across(by_x[:half], 2), across(by_y[half:], 1))
+
+
+def dense_pieces(line, by_x, by_y, far):
+    held = [
+        (line, 0, 0, LINE),
+        (by_x, 1, 0, LINE),
+        (by_y, 2, 0, LINE),
+        (far[0], 3, 0, LINE // 2),
+        (far[1], 3, LINE // 2, LINE // 2),
+    ]
+    pieces = []
+    for array, flip, chip, chips in held:
+        pieces.append((array, None, flip, 0, chip, chips))
+        pieces.append((swap_core(array), None, flip, 1, chip, chips))
+    return pieces
+
+
+def dense_square_scatter(mine, received, *earlier):
+    def piece(flip):
+        return mine[flip].astype(WIDE) + received[flip].astype(WIDE)
+
+    half = LINE // 2
+    far = after(piece(3).astype(LOW), *earlier)
     from_x = across(far[:half], 1)
     from_y = across(far[half:], 2)
     to_x, to_y = piece(1), piece(2)
-    to_x = jnp.concatenate(
-        [to_x[:half], (to_x[half:].astype(WIDE) + from_y.astype(WIDE)).astype(LOW)], axis=0
-    )
-    to_y = jnp.concatenate(
-        [(to_y[:half].astype(WIDE) + from_x.astype(WIDE)).astype(LOW), to_y[half:]], axis=0
-    )
+    to_x = jnp.concatenate([to_x[:half], to_x[half:] + from_y.astype(WIDE)], axis=0).astype(LOW)
+    to_y = jnp.concatenate([to_y[:half] + from_x.astype(WIDE), to_y[half:]], axis=0).astype(LOW)
     got_x = across(to_x, 1)
     got_y = across(to_y, 2)
-    return piece(0).astype(WIDE) + got_x.astype(WIDE) + got_y.astype(WIDE)
-
-
-class SquareLine:
-    def order(self, rows):
-        core = lax.axis_index("cp") % 2
-        blocks = jnp.concatenate(
-            [2 * jnp.arange(LINE) + core, 2 * jnp.arange(LINE) + 1 - core]
-        ).astype(jnp.int32)
-        return (blocks[:, None] * rows + jnp.arange(rows, dtype=jnp.int32)[None, :]).reshape(-1)
-
-    def group_gather(self, value):
-        mine = line_gather(value)
-        other = swap_core(mine)
-        return jnp.concatenate([mine, other], axis=0).reshape(-1, *value.shape[1:])
-
-    def group_scatter(self, terms):
-        parts = terms.astype(LOW).reshape(2, LINE, -1, *terms.shape[1:])
-        other = swap_core(parts[1])
-        return line_scatter((parts[0].astype(WIDE) + other.astype(WIDE)).astype(LOW))
-
-    def expert_gather(self, block):
-        place = lax.axis_index("dp")
-        pieces = square_gather(block)
-        whole = jnp.zeros((block.shape[0], 4, *block.shape[1:]), block.dtype)
-        for flip, part in enumerate(pieces):
-            whole = lax.dynamic_update_slice_in_dim(whole, part[:, None], place ^ flip, 1)
-        return whole.reshape(block.shape[0], 4 * block.shape[1], *block.shape[2:])
-
-    def expert_scatter(self, terms):
-        place = lax.axis_index("dp")
-        parts = terms.reshape(terms.shape[0], 4, -1, *terms.shape[2:])
-        return square_scatter(
-            lambda flip: lax.dynamic_index_in_dim(parts, place ^ flip, 1, keepdims=False)
-        )
-
-    def dense_gather(self, block):
-        place = lax.axis_index("dp")
-        core = lax.axis_index("cp") % 2
-        rows = block.shape[0]
-        whole = jnp.zeros((4, LINE, 2, *block.shape), block.dtype)
-        for flip, part in enumerate(square_gather(line_gather(block))):
-            other = swap_core(part)
-            for held, side in ((part, core), (other, 1 - core)):
-                whole = lax.dynamic_update_slice(
-                    whole, held[None, :, None], (place ^ flip, 0, side, 0, 0)
-                )
-        return whole.reshape(8 * LINE * rows, *block.shape[1:])
-
-    def dense_scatter(self, terms):
-        place = lax.axis_index("dp")
-        core = lax.axis_index("cp") % 2
-        parts = terms.astype(LOW).reshape(4, LINE, 2, -1, *terms.shape[1:])
-        mine = lax.dynamic_index_in_dim(parts, core, 2, keepdims=False)
-        other = swap_core(lax.dynamic_index_in_dim(parts, 1 - core, 2, keepdims=False))
-        both = (mine.astype(WIDE) + other.astype(WIDE)).astype(LOW)
-        plane = square_scatter(
-            lambda flip: lax.dynamic_index_in_dim(both, place ^ flip, 0, keepdims=False)
-        )
-        return line_scatter(plane.astype(LOW))
+    plane = piece(0) + got_x.astype(WIDE) + got_y.astype(WIDE)
+    return ((from_x, from_y), (got_x, got_y), plane.astype(LOW))
+
+
+def square_line_shards(
+    tokens, cotangent, doc_lengths, routes, w_qkv, w_out, router, gains, w_gate_up, w_down
+):
+    dp_place = lax.axis_index("dp")
+    cp_place = lax.axis_index("cp")
+    core = cp_place % 2
+    chip = cp_place // 2
+    lengths_row = doc_lengths[0]
+    row_ids = jnp.arange(ROWS, dtype=jnp.int32)
+    my_index = cp_place * ROWS + row_ids
+    my_segment, my_position = doc_places(my_index, lengths_row)
+    query_meta = jnp.stack([my_index, my_segment], axis=1)
+    back = jnp.arange(LINE, dtype=jnp.int32) - (LINE - 1) + chip
+    blocks = jnp.concatenate([2 * back + core, 2 * back + 1 - core])
+    blocks = jnp.where(jnp.concatenate([back, back]) < 0, 4 * LINE, blocks)
+    key_index = (blocks[:, None] * ROWS + row_ids[None, :]).reshape(-1)
+    key_segment, unused_position = doc_places(key_index, lengths_row)
+    key_meta = jnp.stack([key_index, key_segment])
+    cosine, sine = rope_tables(my_position)
+    cosine, sine = cosine[:, 0], sine[:, 0]
+    tables = jnp.stack(
+        [jnp.concatenate([cosine, cosine], axis=1), jnp.concatenate([-sine, sine], axis=1)]
+    )
+
+    small_lines = LAYERS * (EXPERTS + 2)
+    own_rows = router.shape[1]
+    small = jnp.concatenate([router, gains], axis=2).transpose(0, 2, 1).reshape(-1)
+    small_size = small.shape[0]
+    small_rows = -(-small_size // D)
+    small = jnp.pad(small, (0, small_rows * D - small_size)).reshape(small_rows, D)
+    route_numbers = routes.reshape(-1).astype(LOW)
+    route_size = route_numbers.shape[0]
+    route_numbers = jnp.pad(route_numbers, (0, D - route_size)).reshape(1, D)
+    small = jnp.concatenate([small, route_numbers], axis=0)
+    small = jnp.pad(small, ((0, SMALL - small_rows - 1), (0, 0)))
+
+    gate_x, gate_y = square_step(w_gate_up[0, 0])
+    first = line_gather(jnp.concatenate([w_qkv[0], w_out[0], small], axis=0))
+    second = jnp.concatenate([w_qkv[1], w_out[1], cotangent], axis=0)
+    second = line_gather(after(second, first))
+    dense_rows = QROWS + OROWS
+    upstream_line = second[:, dense_rows:]
+    second = second[:, :dense_rows]
+    first_x, first_y = square_step(after(first, gate_x, gate_y))
+    first_far = square_far(first_x, first_y)
+    pieces = dense_pieces(first, first_x, first_y, first_far)
+    query, output = Dense(pieces, 0, QROWS), Dense(pieces, QROWS, OROWS)
+    small = small_call(Dense(pieces, dense_rows, SMALL))
+
+    def expert_weights(layer, first, more, down, far):
+        gate_ups = [w_gate_up[layer, 0], *first, far[0], w_gate_up[layer, 1], *more, far[1]]
+        return gate_ups + [w_down[layer], *down, far[2], far[3]]
+
+    def experts_far(first, more, down):
+        return (
+            across(after(first[0], *down), 2),
+            across(after(more[1], *down), 1),
+            across(down[0][0], 2),
+            across(down[1][1], 1),
+        )
+
+    gate_ups = [[(gate_x, gate_y)], []]
+    gate_ups[0].append(square_step(after(w_gate_up[0, 1], *first_far)))
+    downs = [square_step(after(w_down[0], *gate_ups[0][1]))]
+    fars = [experts_far(*gate_ups[0], downs[0])]
+    weights = [(query, output, expert_weights(0, *gate_ups[0], downs[0], fars[0]))]
+    second_near = square_step(after(second, *fars[0]))
+    second_far = square_far(*second_near)
+    pieces = dense_pieces(second, *second_near, second_far)
+    query, output = Dense(pieces, 0, QROWS), Dense(pieces, QROWS, OROWS)
+    gate_ups[1].append(square_step(after(w_gate_up[1, 0], *second_far)))
+    gate_ups[1].append(square_step(after(w_gate_up[1, 1], *gate_ups[1][0])))
+    downs.append(square_step(after(w_down[1], *gate_ups[1][1])))
+    fars.append(experts_far(*gate_ups[1], downs[1]))
+    weights.append((query, output, expert_weights(1, *gate_ups[1], downs[1], fars[1])))
+
+    shared = small.reshape(-1, SMALL, D)
+    lines = shared[:, :small_rows].reshape(-1, small_rows * D)[:, :small_size]
+    lines = lines.reshape(-1, small_lines, own_rows).transpose(1, 0, 2).reshape(small_lines, D)
+    lines = lines.reshape(LAYERS, EXPERTS + 2, D)
+    routers = lines[:, :EXPERTS]
+    gain_rows = lines[:, EXPERTS:].astype(WIDE)[:, :, None]
+    numbers = lax.dynamic_index_in_dim(small, dp_place, 0, keepdims=False)
+    numbers = numbers[:, :, small_rows, :route_size]
+    numbers = jnp.where(core == 0, numbers, numbers[:, ::-1]).astype(jnp.int32)
+    numbers = numbers.reshape(LINE, 2, LAYERS, ROWS, TOP).transpose(2, 1, 0, 3, 4)
+    group_routes = numbers.reshape(LAYERS, GROUP, TOP)
+
+    value = after(tokens, second).astype(WIDE)
+    stored = []
+    for layer in range(LAYERS):
+        query, output, pieces = weights[layer]
+        normed, heads, kv = project_call(value, gain_rows[layer, 0], query, tables)
+        keys_values = earlier_gather(kv)
+        if layer == 0:
+            keys_values = (after(keys_values[0], *gate_ups[0][1], routers, group_routes), keys_values[1])
+        low, probs, middle, mixed = attend_call(
+            value, heads, keys_values, query_meta, key_meta, output, gain_rows[layer, 1]
+        )
+        if layer == 0:
+            mixed = group_gather(mixed, (), downs[0])
+        else:
+            mixed = group_gather(mixed, gate_ups[1][1], (), downs[1])
+        own, other, gate_up, hidden, gates = experts_call(
+            mixed, group_routes[layer], routers[layer].T, pieces
+        )
+        stored.append((value, normed, heads, keys_values, low, probs, middle, mixed, gate_up, hidden, gates))
+        if layer == 0:
+            value = middle + group_scatter(own, other, second_near, (), second_far, ())
+            value = after(value, *gate_ups[1][0])
+    last_sums = (own, other)
+
+    upstream_group = (upstream_line.reshape(HALF, D), swap_core(upstream_line).reshape(HALF, D))
+    upstream = cotangent.astype(WIDE)
+    expert_grads = None
+    dense_grads, router_grads, gain_grads = ([None] * LAYERS for _ in range(3))
+    for layer in reversed(range(LAYERS)):
+        query, output, pieces = weights[layer]
+        value, normed, heads, keys_values, low, probs, middle, mixed, gate_up, hidden, gates = stored[layer]
+        own, other, grad_gate_up, grad_logits = experts_back_call(
+            upstream_group, gate_up, gates, routers[layer], pieces
+        )
+        router_grads[layer] = t_dot(grad_logits[:HALF], mixed[0]) + t_dot(grad_logits[HALF:], mixed[1])
+        terms = (mixed, grad_gate_up, hidden, upstream_group)
+        far = expert_grads_call((3,), *terms)
+        from_x = across(far[0], 1)
+        from_y = across(far[1], 2)
+        if layer < LAYERS - 1:
+            far = [after(part, *dense_sums[1]) for part in far]
+        grad_mixed = group_scatter(own, other, far)
+        to_x, to_y = expert_grads_call(
+            (1, 2), *terms, received=[(from_y, 0, 1), (from_x, 1, 0)]
+        )
+        grad_mixed = after(grad_mixed, to_x, to_y)
+        got_x = across(to_x, 1)
+        got_y = across(to_y, 2)
+        expert_sums = (got_x, got_y)
+        expert_grads = expert_grads_call(
+            (0,),
+            *terms,
+            received=[(got_x, 0, None), (got_y, 0, None)],
+            layer=layer,
+            results=expert_grads,
+        )
+        grad_middle, error, grad_heads, own, other, second_gain = attend_back_call(
+            grad_mixed, middle, gain_rows[layer, 1], upstream, output, low, probs, heads, keys_values
+        )
+        grad_kv = earlier_scatter(own, other)
+        joined, upstream, upstream_low, first_gain = project_back_call(
+            grad_heads, grad_kv, tables, query, value, gain_rows[layer, 0], grad_middle
+        )
+        gain_grads[layer] = jnp.concatenate([first_gain, second_gain], axis=0)
+        small = None
+        if layer == 0:
+            small = jnp.concatenate(
+                [jnp.concatenate([router_grads[l], gain_grads[l]], axis=0) for l in range(LAYERS)], axis=0
+            ).astype(LOW)
+            small = small.reshape(small_lines, -1, own_rows).transpose(1, 0, 2).reshape(-1, small_size)
+            small = jnp.pad(small, ((0, 0), (0, SMALL * D - small_size)))
+            small = small.reshape(4, LINE, 2, SMALL, D)
+        mine, other = dense_grads_call(joined, normed, low, error, small)
+        if layer > 0:
+            received = swap_core(other)
+            dense_sums = dense_square_scatter(mine, received, got_x, got_y)
+            upstream_group = group_gather(upstream_low, (mine, other), (), (got_x, got_y), dense_sums[0])
+            dense_grads[layer] = line_scatter(dense_sums[2])
+        else:
+            dense_grads[0] = line_scatter(dense_square_scatter(mine, swap_core(other))[2])
+    result = stored[-1][6] + group_scatter(after(last_sums[0], joined), last_sums[1])
+    small = dense_grads[0][QROWS + OROWS :].reshape(-1)[:small_size]
+    small = small.reshape(LAYERS, EXPERTS + 2, own_rows).transpose(0, 2, 1)
+    return (
+        result,
+        upstream,
+        jnp.stack([grads[:QROWS] for grads in dense_grads]),
+        jnp.stack([grads[QROWS : QROWS + OROWS] for grads in dense_grads]),
+        small[:, :, :EXPERTS],
+        small[:, :, EXPERTS:],
+        *expert_grads,
+    )
 
 
 class AnyMesh:
@@ -247,11 +1172,11 @@
         ).astype(WIDE)
 
 
-def shards(tokens, cotangent, doc_lengths, routes, w_qkv, w_out, router, gains, w_gate_up, w_down):
+def any_mesh_shards(tokens, cotangent, doc_lengths, routes, w_qkv, w_out, router, gains, w_gate_up, w_down):
     dp_size = lax.axis_size("dp")
     cp_size = lax.axis_size("cp")
     device_count = dp_size * cp_size
-    move = SquareLine() if (dp_size, cp_size) == (4, 2 * LINE) else AnyMesh()
+    move = AnyMesh()
     row_count = tokens.shape[0]
     group_rows = row_count * cp_size
     cycle_place = lax.axis_index("cp")
@@ -292,9 +1217,6 @@
         down_weight = move.expert_gather(w_down[layer])
         weights.append((query_weight, output_weight, gate_up_weight, down_weight))
     cotangent_group = move.group_gather(cotangent)
-
-    def norm_rows(values, gain):
-        return (values * inverse_rms(values) * gain).astype(LOW)
 
     def forward_layer(layer, layer_value):
         query_weight, output_weight, gate_up_weight, down_weight = weights[layer]
@@ -508,8 +1430,10 @@
 
 
 def solution(mesh):
+    sizes = dict(mesh.shape)
+    square_line = (sizes["dp"], sizes["cp"]) == (4, 2 * LINE)
     return jax.shard_map(
-        shards,
+        square_line_shards if square_line else any_mesh_shards,
         mesh=mesh,
         in_specs=(
             P(("dp", "cp"), None),

time: 1550 us -> 1170 us (0.75)
  Pallas kernels: 0 us -> 275 us
  matrix products: 184 us -> 1.34 us
  local copies, waits for them, and re-layouts: 231 us -> 67.7 us
  starting transfers between devices: 334 us -> 238 us
  other arithmetic: 150 us -> 62.7 us
  waiting for transfers between devices: 582 us -> 508 us
  blocking collectives: 53.5 us -> 0 us
    pallas_call x0 -> x21, Pallas kernels: none -> 275 us  [the longest x13 182 us: call(): pl.pallas_call(body, grid=grid, out_shape=outs, in_specs=in_specs, out_sp...]
    dot_general x34 -> x0, matrix products: 119 us -> none  [the longest x12 53.4 us: dot_t(): lax.dot_general(left, right, (((1,), (1,)), ((), ())), preferred_element_...]
    ppermute x120 -> x66, starting transfers between devices: 267 us -> 159 us  [hop(): return lax.ppermute(value, 'cp', pairs)]
    ppermute x64 -> x44, waiting for transfers between devices: 347 us -> 281 us  [across(): return lax.ppermute(value, 'dp', [(i, i ^ flip) for i in range(4)])]
    all_gather x2 -> x0, blocking collectives: 53.5 us -> none  [the longest x1 39.5 us: shards(): lax.all_gather(small, ('dp', 'cp'), axis=0, tiled=False)]
    dot_general x12 -> x4, matrix products: 51.5 us -> 1.34 us  [t_dot(): lax.dot_general(left, right, (((0,), (0,)), ((), ())), preferred_element_...]
    slice x61 -> x24, local copies, waits for them, and re-layouts: 62.3 us -> 18.7 us  [the longest x4 5.25 us: square_far(): return (across(by_x[:half], 2), across(by_y[half:], 1))]
    ppermute x120 -> x66, waiting for transfers between devices: 228 us -> 185 us  [hop(): return lax.ppermute(value, 'cp', pairs)]
  transfers between devices with their start and end apart: 216 -> 146, of which waited for: 91 -> 68; matrix products, arithmetic and copies ran while one was open for 30% -> 9% of each run, Pallas kernels for 0% -> 16%
where the time goes in v2:
time: 1170 us; the launch traced here: 1160 us
  waiting for transfers between devices  508 us (43%)
  Pallas kernels  275 us (24%)
  starting transfers between devices  238 us (20%)
  local copies, waits for them, and re-layouts  67.7 us (6%)
  other arithmetic  62.7 us (5%)
    ppermute x44, waiting for transfers between devices, across(): return lax.ppermute(value, 'dp', [(i, i ^ flip) for i in range(4)])  281 us
    ppermute x66, waiting for transfers between devices, hop(): return lax.ppermute(value, 'cp', pairs)  185 us
    pallas_call x13, Pallas kernels, call(): pl.pallas_call(body, grid=grid, out_shape=outs, in_specs=in_specs, out_sp...  182 us
    ppermute x66, starting transfers between devices, hop(): return lax.ppermute(value, 'cp', pairs)  159 us
    pallas_call x6, Pallas kernels, expert_grads_call(): pl.pallas_call(body, out_shape=outs, input_output_aliases={first_kept + i...  75.4 us
    ppermute x44, starting transfers between devices, across(): return lax.ppermute(value, 'dp', [(i, i ^ flip) for i in range(4)])  47.3 us
    ppermute x12, starting transfers between devices, leap(): return lax.ppermute(value, 'cp', pairs)  29.1 us
    ppermute x12, waiting for transfers between devices, leap(): return lax.ppermute(value, 'cp', pairs)  27.1 us
  transfers between devices with their start and end apart: 146, of which 68 were waited for; matrix products, arithmetic and copies ran while one was open for 9% of the time, Pallas kernels for 16%

profile of v2, /device:TPU:0, one launch (start us, length us, event | category | flops | bytes accessed | tf_op | source)
XLA Modules:
  0.0 1156.1 jit_solution(11315108544798300316)
XLA Ops:
  11.0 7.0 collective-permute-done
  38.1 11.2 collective-permute-done.5
  76.5 12.8 %collective-permute-done.10 = bf16[240,1536]{1,0:T(8,128)(2,1)S(1)} collective-permute-done((bf16[240,1536]{1,0:T(8,128)(2,1)}, bf16[240,1536]{1,0:T(8,128)(2,1)S(1)}, u32[]{:S(2)}, u32[]{:S(2)}) %collective-permute-start.10) | collective-permute-done | bytes 737312 | tf_op jit(solution)/shard_map/ppermute | solution.py:843
  99.2 10.2 collective-permute-done.11
  124.2 7.0 project.2
  131.3 7.0 collective-permute-start.25
  154.1 9.5 attend.2
  170.8 7.6 collective-permute-done.29
  187.7 7.4 collective-permute-done.35
  197.9 9.6 collective-permute-done.36
  207.8 15.8 %collective-permute-done.40.rest_11_ = bf16[192,1536]{1,0:T(8,128)(2,1)} collective-permute-done((bf16[192,1536]{1,0:T(8,128)(2,1)S(1)}, bf16[192,1536]{1,0:T(8,128)(2,1)}, u32[]{:S(2)}, u32[]{:S(2)}) %collective-permute-start.40) | collective-permute-done | bytes 589856 | tf_op jit(solution)/shard_map/ppermute | solution.py:852
  235.6 25.6 %experts.2 = (bf16[512,1536]{1,0:T(8,128)(2,1)}, bf16[512,1536]{1,0:T(8,128)(2,1)}, bf16[1024,3072]{1,0:T(8,128)(2,1)}, bf16[1024,1536]{1,0:T(8,128)(2,1)}, f32[1024,16]{1,0:T(8,128)}) custom-call(s32[4]{0:T(128)} %pad_add_fusion.2.places, bf16[512,1536]{1,0:T(8,128)(2,1)} %bitcast.370, bf16[512,1536]{1,0:T(8,128)(2,1)} %bitcast.382, s32[1024,4]{1,0:T(8,128)} %bitcast.429, ...), custom_call_target="tpu_custom_call" | custom-call | bytes 10400000 | tf_op jit(solution)/shard_map/experts/pallas_call | solution.py:129
  284.8 9.7 collective-permute-done.46.rest_6_
  311.4 16.7 %collective-permute-done.53.rest_1_ = bf16[384,1536]{1,0:T(8,128)(2,1)} collective-permute-done((bf16[384,1536]{1,0:T(8,128)(2,1)}, bf16[384,1536]{1,0:T(8,128)(2,1)}, u32[]{:S(2)}, u32[]{:S(2)}) %collective-permute-start.53) | collective-permute-done | bytes 1179680 | tf_op jit(solution)/shard_map/ppermute | solution.py:852
  346.0 7.0 project.3
  368.5 9.5 attend.3
  384.4 7.4 collective-permute-done.66
  412.1 8.7 collective-permute-done.73
  425.3 16.6 %collective-permute-done.77.rest_11_ = bf16[192,1536]{1,0:T(8,128)(2,1)} collective-permute-done((bf16[192,1536]{1,0:T(8,128)(2,1)S(1)}, bf16[192,1536]{1,0:T(8,128)(2,1)}, u32[]{:S(2)}, u32[]{:S(2)}) %collective-permute-start.77) | collective-permute-done | bytes 589856 | tf_op jit(solution)/shard_map/ppermute | solution.py:852
  444.7 18.2 %collective-permute-done.78.rest_12_ = bf16[192,1536]{1,0:T(8,128)(2,1)} collective-permute-done((bf16[192,1536]{1,0:T(8,128)(2,1)}, bf16[192,1536]{1,0:T(8,128)(2,1)}, u32[]{:S(2)}, u32[]{:S(2)}) %collective-permute-start.78) | collective-permute-done | bytes 589856 | tf_op jit(solution)/shard_map/ppermute | solution.py:852
  464.1 25.6 %experts.3 = (bf16[512,1536]{1,0:T(8,128)(2,1)}, bf16[512,1536]{1,0:T(8,128)(2,1)}, bf16[1024,3072]{1,0:T(8,128)(2,1)}, bf16[1024,1536]{1,0:T(8,128)(2,1)}, f32[1024,16]{1,0:T(8,128)}) custom-call(s32[4]{0:T(128)} %pad_add_fusion.2.places, bf16[512,1536]{1,0:T(8,128)(2,1)} %bitcast.364, bf16[512,1536]{1,0:T(8,128)(2,1)} %bitcast.376, s32[1024,4]{1,0:T(8,128)} %bitcast.428, ...), custom_call_target="tpu_custom_call" | custom-call | bytes 10400000 | tf_op jit(solution)/shard_map/experts/pallas_call | solution.py:129
  489.8 27.5 %experts_back.2 = (bf16[512,1536]{1,0:T(8,128)(2,1)}, bf16[512,1536]{1,0:T(8,128)(2,1)}, bf16[1024,3072]{1,0:T(8,128)(2,1)}, bf16[1024,16]{1,0:T(8,128)(2,1)}) custom-call(s32[4]{0:T(128)} %pad_add_fusion.2.places, bf16[512,1536]{1,0:T(8,128)(2,1)} %bitcast.98.up_own.rest_5_.rest_9_, bf16[512,1536]{1,0:T(8,128)(2,1)} %bitcast.99.up_other.rest_6_.rest_10_, ...), custom_call_target="tpu_custom_call" | custom-call | bytes 10400000 | tf_op jit(solution)/shard_map/experts_back/pallas_call | solution.py:129
  517.3 10.9 expert_grads.6
  537.0 7.9 collective-permute-done.81
  567.4 21.8 %collective-permute-done.87.rest_11_ = bf16[576,1536]{1,0:T(8,128)(2,1)S(1)} collective-permute-done((bf16[576,1536]{1,0:T(8,128)(2,1)S(1)}, bf16[576,1536]{1,0:T(8,128)(2,1)S(1)}, u32[]{:S(2)}, u32[]{:S(2)}) %collective-permute-start.87) | collective-permute-done | bytes 1769504 | tf_op jit(solution)/shard_map/ppermute | solution.py:852
  590.6 15.4 %expert_grads.7 = (bf16[2,576,1536]{2,1,0:T(8,128)(2,1)}, bf16[2,576,1536]{2,1,0:T(8,128)(2,1)}) custom-call(s32[4]{0:T(128)} %pad_add_fusion.2.places, bf16[512,1536]{1,0:T(8,128)(2,1)} %bitcast.366, bf16[512,1536]{1,0:T(8,128)(2,1)} %bitcast.378, bf16[512,1536]{1,0:T(8,128)(2,1)} %bitcast.367, bf16[512,1536]{1,0:T(8,128)(2,1)} %bitcast.379, ...), custom_call_target="tpu_custom_call" | custom-call | bytes 6000000 | tf_op jit(solution)/shard_map/expert_grads/pallas_call | solution.py:619
  607.0 12.4 %attend_back.2 = (f32[128,1536]{1,0:T(8,128)}, bf16[128,1536]{1,0:T(8,128)(2,1)}, f32[12,128,128]{2,1,0:T(8,128)}, bf16[512,512]{1,0:T(8,128)(2,1)}, bf16[512,512]{1,0:T(8,128)(2,1)}, /*index=5*/f32[1,1536]{1,0:T(1,128)}) custom-call(s32[4]{0:T(128)} %pad_add_fusion.2.places, f32[128,1536]{1,0:T(8,128)} %fusion.38.gm_ref, ...), custom_call_target="tpu_custom_call" | custom-call | bytes 4800000 | tf_op jit(solution)/shard_map/attend_back/pallas_call | solution.py:129
  645.5 8.8 dense_grads.2
  660.9 7.9 collective-permute-done.93
  674.1 24.6 %collective-permute-done.95.rest_7_ = bf16[2,576,1536]{2,1,0:T(8,128)(2,1)S(1)} collective-permute-done((bf16[2,576,1536]{2,1,0:T(8,128)(2,1)}, bf16[2,576,1536]{2,1,0:T(8,128)(2,1)S(1)}, u32[]{:S(2)}, u32[]{:S(2)}) %collective-permute-start.95) | collective-permute-done | bytes 3538976 | tf_op jit(solution)/shard_map/ppermute | solution.py:852
  701.8 7.7 convert_add_fusion.3
  712.7 13.7 %collective-permute-done.102 = bf16[2,112,1536]{2,1,0:T(8,128)(2,1)S(1)} collective-permute-done((bf16[2,112,1536]{2,1,0:T(8,128)(2,1)S(1)}, bf16[2,112,1536]{2,1,0:T(8,128)(2,1)S(1)}, u32[]{:S(2)}, u32[]{:S(2)}) %collective-permute-start.102) | collective-permute-done | bytes 688160 | tf_op jit(solution)/shard_map/ppermute | solution.py:852
  731.7 27.8 %experts_back.3 = (bf16[512,1536]{1,0:T(8,128)(2,1)}, bf16[512,1536]{1,0:T(8,128)(2,1)}, bf16[1024,3072]{1,0:T(8,128)(2,1)}, bf16[1024,16]{1,0:T(8,128)(2,1)}) custom-call(s32[4]{0:T(128)} %pad_add_fusion.2.places, bf16[512,1536]{1,0:T(8,128)(2,1)} %bitcast.388, bf16[512,1536]{1,0:T(8,128)(2,1)} %bitcast.392, bf16[1024,3072]{1,0:T(8,128)(2,1)} %get-tuple-element.170.gu_ref, ...), custom_call_target="tpu_custom_call" | custom-call | bytes 10400000 | tf_op jit(solution)/shard_map/experts_back/pallas_call | solution.py:129
  783.5 10.7 expert_grads.8
  805.5 28.5 %collective-permute-done.112.rest_11_ = bf16[576,1536]{1,0:T(8,128)(2,1)} collective-permute-done((bf16[576,1536]{1,0:T(8,128)(2,1)}, bf16[576,1536]{1,0:T(8,128)(2,1)}, u32[]{:S(2)}, u32[]{:S(2)}) %collective-permute-start.112) | collective-permute-done | bytes 1769504 | tf_op jit(solution)/shard_map/ppermute | solution.py:852
  835.0 15.4 %expert_grads.9 = (bf16[2,576,1536]{2,1,0:T(8,128)(2,1)}, bf16[2,576,1536]{2,1,0:T(8,128)(2,1)}) custom-call(s32[4]{0:T(128)} %pad_add_fusion.2.places, bf16[512,1536]{1,0:T(8,128)(2,1)} %bitcast.372, bf16[512,1536]{1,0:T(8,128)(2,1)} %bitcast.384, bf16[512,1536]{1,0:T(8,128)(2,1)} %bitcast.373, bf16[512,1536]{1,0:T(8,128)(2,1)} %bitcast.385, ...), custom_call_target="tpu_custom_call" | custom-call | bytes 6000000 | tf_op jit(solution)/shard_map/expert_grads/pallas_call | solution.py:619
  851.5 12.6 %attend_back.3 = (f32[128,1536]{1,0:T(8,128)}, bf16[128,1536]{1,0:T(8,128)(2,1)}, f32[12,128,128]{2,1,0:T(8,128)}, bf16[512,512]{1,0:T(8,128)(2,1)}, bf16[512,512]{1,0:T(8,128)(2,1)}, /*index=5*/f32[1,1536]{1,0:T(1,128)}) custom-call(s32[4]{0:T(128)} %pad_add_fusion.2.places, f32[128,1536]{1,0:T(8,128)} %fusion.33.gm_ref, ...), custom_call_target="tpu_custom_call" | custom-call | bytes 4800000 | tf_op jit(solution)/shard_map/attend_back/pallas_call | solution.py:129
  892.8 9.7 dense_grads.3
  903.8 31.7 %collective-permute-done.136 = bf16[4,112,1536]{2,1,0:T(8,128)(2,1)S(1)} collective-permute-done((bf16[4,112,1536]{2,1,0:T(8,128)(2,1)S(1)}, bf16[4,112,1536]{2,1,0:T(8,128)(2,1)S(1)}, u32[]{:S(2)}, u32[]{:S(2)}) %collective-permute-start.136) | collective-permute-done | bytes 1376288 | tf_op jit(solution)/shard_map/ppermute | solution.py:852
  969.3 11.5 expert_grads.10
  988.8 17.6 %collective-permute-done.128 = bf16[2,128,1536]{2,1,0:T(8,128)(2,1)S(1)} collective-permute-done((bf16[2,128,1536]{2,1,0:T(8,128)(2,1)S(1)}, bf16[2,128,1536]{2,1,0:T(8,128)(2,1)S(1)}, u32[]{:S(2)}, u32[]{:S(2)}) %collective-permute-start.128) | collective-permute-done | bytes 786464 | tf_op jit(solution)/shard_map/ppermute | solution.py:852
  1013.3 8.2 collective-permute-start.119
  1021.5 22.7 %collective-permute-done.129 = bf16[4,128,1536]{2,1,0:T(8,128)(2,1)S(1)} collective-permute-done((bf16[4,128,1536]{2,1,0:T(8,128)(2,1)S(1)}, bf16[4,128,1536]{2,1,0:T(8,128)(2,1)S(1)}, u32[]{:S(2)}, u32[]{:S(2)}) %collective-permute-start.129) | collective-permute-done | bytes 1572896 | tf_op jit(solution)/shard_map/ppermute | solution.py:852
  1048.5 8.2 collective-permute-start.130
  1058.1 8.1 collective-permute-done.130
  1087.7 32.4 %collective-permute-done.144.rest_7_ = bf16[2,576,1536]{2,1,0:T(8,128)(2,1)} collective-permute-done((bf16[2,576,1536]{2,1,0:T(8,128)(2,1)S(1)}, bf16[2,576,1536]{2,1,0:T(8,128)(2,1)}, u32[]{:S(2)}, u32[]{:S(2)}) %collective-permute-start.144) | collective-permute-done | bytes 3538976 | tf_op jit(solution)/shard_map/ppermute | solution.py:852
  1120.1 11.6 %expert_grads.11 = (f32[2,2,384,1536]{3,2,1,0:T(8,128)}, f32[2,2,192,1536]{3,2,1,0:T(8,128)}) custom-call(s32[4]{0:T(128)} %pad_add_fusion.2.places, bf16[512,1536]{1,0:T(8,128)(2,1)} %bitcast.374, bf16[512,1536]{1,0:T(8,128)(2,1)} %bitcast.386, ...), custom_call_target="tpu_custom_call", output_to_operand_aliasing={{0}: (10, {}), {1}: (11, {})} | custom-call | bytes 4400000 | tf_op jit(solution)/shard_map/expert_grads/pallas_call | solution.py:619
  1131.7 8.1 collective-permute-start.132
  (630 shorter events, 478.8 us)
Async XLA Ops:
  57.0 33.7 %collective-permute-start.15 = (bf16[4,128,1536]{2,1,0:T(8,128)(2,1)S(1)}, bf16[4,128,1536]{2,1,0:T(8,128)(2,1)S(1)}, u32[]{:S(2)}, u32[]{:S(2)}) collective-permute-start(bf16[4,128,1536]{2,1,0:T(8,128)(2,1)S(1)} %constant_dynamic-slice_fusion.5.rest_0_), channel_id=1, source_target_pairs={{0,8},{8,0},{16,24},{24,16},{1,9},{9,1},{17,25},{25,17},{2,10},{10... | collective-permute-start | bytes 4718600 | tf_op jit(solution)/shard_map/ppermute | solution.py:852
  57.5 34.9 %collective-permute-start.17 = (bf16[4,128,1536]{2,1,0:T(8,128)(2,1)S(1)}, bf16[4,128,1536]{2,1,0:T(8,128)(2,1)}, u32[]{:S(2)}, u32[]{:S(2)}) collective-permute-start(bf16[4,128,1536]{2,1,0:T(8,128)(2,1)S(1)} %constant_dynamic-slice_fusion.5.rest_0_), channel_id=1, source_target_pairs={{0,16},{8,24},{16,0},{24,8},{1,17},{9,25},{17,1},{25,9},{2,18},{10... | collective-permute-start | bytes 4718600 | tf_op jit(solution)/shard_map/ppermute | solution.py:852
  76.5 34.8 %collective-permute-start.12 = (bf16[4,128,1536]{2,1,0:T(8,128)(2,1)S(1)}, bf16[4,128,1536]{2,1,0:T(8,128)(2,1)S(1)}, u32[]{:S(2)}, u32[]{:S(2)}) collective-permute-start(bf16[4,128,1536]{2,1,0:T(8,128)(2,1)S(1)} %constant_dynamic-slice_fusion.5.rest_0_), channel_id=1, source_target_pairs={{0,1},{1,0},{2,3},{3,2},{4,5},{5,4},{6,7},{7,6},{8,9},{9,8},{10,11... | collective-permute-start | bytes 4718600 | tf_op jit(solution)/shard_map/ppermute | solution.py:837
  111.4 36.1 %collective-permute-start.26 = (bf16[384,1536]{1,0:T(8,128)(2,1)}, bf16[384,1536]{1,0:T(8,128)(2,1)}, u32[]{:S(2)}, u32[]{:S(2)}) collective-permute-start(bf16[384,1536]{1,0:T(8,128)(2,1)} %get-tuple-element.112.rest_4_), channel_id=1, source_target_pairs={{0,8},{8,0},{16,24},{24,16},{1,9},{9,1},{17,25},{25,17},{2,10},{10... | collective-permute-start | bytes 3538952 | tf_op jit(solution)/shard_map/ppermute | solution.py:852
  114.6 32.9 %collective-permute-start.27 = (bf16[384,1536]{1,0:T(8,128)(2,1)}, bf16[384,1536]{1,0:T(8,128)(2,1)S(1)}, u32[]{:S(2)}, u32[]{:S(2)}) collective-permute-start(bf16[384,1536]{1,0:T(8,128)(2,1)} %get-tuple-element.112.rest_4_), channel_id=1, source_target_pairs={{0,16},{8,24},{16,0},{24,8},{1,17},{9,25},{17,1},{25,9},{2,18},{10... | collective-permute-start | bytes 3538952 | tf_op jit(solution)/shard_map/ppermute | solution.py:852
  148.5 29.9 %collective-permute-start.30 = (bf16[2,192,1536]{2,1,0:T(8,128)(2,1)S(1)}, bf16[2,192,1536]{2,1,0:T(8,128)(2,1)S(1)}, u32[]{:S(2)}, u32[]{:S(2)}) collective-permute-start(bf16[2,192,1536]{2,1,0:T(8,128)(2,1)S(1)} %copy-done.23), channel_id=1, source_target_pairs={{0,8},{8,0},{16,24},{24,16},{1,9},{9,1},{17,25},{25,17},{2,10},{10... | collective-permute-start | bytes 3538952 | tf_op jit(solution)/shard_map/ppermute | solution.py:852
  149.5 28.9 %collective-permute-start.31 = (bf16[2,192,1536]{2,1,0:T(8,128)(2,1)S(1)}, bf16[2,192,1536]{2,1,0:T(8,128)(2,1)S(1)}, u32[]{:S(2)}, u32[]{:S(2)}) collective-permute-start(bf16[2,192,1536]{2,1,0:T(8,128)(2,1)S(1)} %copy-done.23), channel_id=1, source_target_pairs={{0,16},{8,24},{16,0},{24,8},{1,17},{9,25},{17,1},{25,9},{2,18},{10... | collective-permute-start | bytes 3538952 | tf_op jit(solution)/shard_map/ppermute | solution.py:852
  183.7 40.2 %collective-permute-start.38 = (bf16[384,1536]{1,0:T(8,128)(2,1)}, bf16[384,1536]{1,0:T(8,128)(2,1)}, u32[]{:S(2)}, u32[]{:S(2)}) collective-permute-start(bf16[384,1536]{1,0:T(8,128)(2,1)} %collective-permute-done.13.rest_1_), channel_id=1, source_target_pairs={{0,16},{8,24},{16,0},{24,8},{1,17},{9,25},{17,1},{25,9},{2,18},{10... | collective-permute-start | bytes 3538952 | tf_op jit(solution)/shard_map/ppermute | solution.py:852
  184.4 39.5 %collective-permute-start.39 = (bf16[384,1536]{1,0:T(8,128)(2,1)}, bf16[384,1536]{1,0:T(8,128)(2,1)}, u32[]{:S(2)}, u32[]{:S(2)}) collective-permute-start(bf16[384,1536]{1,0:T(8,128)(2,1)} %copy-done.36), channel_id=1, source_target_pairs={{0,8},{8,0},{16,24},{24,16},{1,9},{9,1},{17,25},{25,17},{2,10},{10... | collective-permute-start | bytes 3538952 | tf_op jit(solution)/shard_map/ppermute | solution.py:852
  185.9 37.7 %collective-permute-start.40 = (bf16[192,1536]{1,0:T(8,128)(2,1)S(1)}, bf16[192,1536]{1,0:T(8,128)(2,1)}, u32[]{:S(2)}, u32[]{:S(2)}) collective-permute-start(bf16[192,1536]{1,0:T(8,128)(2,1)S(1)} %slice_bitcast_fusion.13), channel_id=1, source_target_pairs={{0,16},{8,24},{16,0},{24,8},{1,17},{9,25},{17,1},{25,9},{2,18},{10... | collective-permute-start | bytes 1769480 | tf_op jit(solution)/shard_map/ppermute | solution.py:852
  195.1 28.9 %collective-permute-start.41 = (bf16[192,1536]{1,0:T(8,128)(2,1)S(1)}, bf16[192,1536]{1,0:T(8,128)(2,1)}, u32[]{:S(2)}, u32[]{:S(2)}) collective-permute-start(bf16[192,1536]{1,0:T(8,128)(2,1)S(1)} %slice_bitcast_fusion.12), channel_id=1, source_target_pairs={{0,8},{8,0},{16,24},{24,16},{1,9},{9,1},{17,25},{25,17},{2,10},{10... | collective-permute-start | bytes 1769480 | tf_op jit(solution)/shard_map/ppermute | solution.py:852
  224.0 37.2 %collective-permute-start.42 = (bf16[4,112,1536]{2,1,0:T(8,128)(2,1)}, bf16[4,112,1536]{2,1,0:T(8,128)(2,1)}, u32[]{:S(2)}, u32[]{:S(2)}) collective-permute-start(bf16[4,112,1536]{2,1,0:T(8,128)(2,1)} %constant_dynamic-slice_fusion.rest_0_), channel_id=1, source_target_pairs={{0,8},{8,0},{16,24},{24,16},{1,9},{9,1},{17,25},{25,17},{2,10},{10... | collective-permute-start | bytes 4128776 | tf_op jit(solution)/shard_map/ppermute | solution.py:852
  225.3 35.9 %collective-permute-start.43 = (bf16[4,112,1536]{2,1,0:T(8,128)(2,1)}, bf16[4,112,1536]{2,1,0:T(8,128)(2,1)}, u32[]{:S(2)}, u32[]{:S(2)}) collective-permute-start(bf16[4,112,1536]{2,1,0:T(8,128)(2,1)} %constant_dynamic-slice_fusion.rest_0_), channel_id=1, source_target_pairs={{0,16},{8,24},{16,0},{24,8},{1,17},{9,25},{17,1},{25,9},{2,18},{10... | collective-permute-start | bytes 4128776 | tf_op jit(solution)/shard_map/ppermute | solution.py:852
  299.3 32.7 %collective-permute-start.55 = (bf16[4,112,1536]{2,1,0:T(8,128)(2,1)}, bf16[4,112,1536]{2,1,0:T(8,128)(2,1)S(1)}, u32[]{:S(2)}, u32[]{:S(2)}) collective-permute-start(bf16[4,112,1536]{2,1,0:T(8,128)(2,1)} %constant_dynamic-slice_fusion.rest_0_), channel_id=1, source_target_pairs={{0,1},{1,0},{2,3},{3,2},{4,5},{5,4},{6,7},{7,6},{8,9},{9,8},{10,11... | collective-permute-start | bytes 4128776 | tf_op jit(solution)/shard_map/ppermute | solution.py:837
  299.3 33.5 %collective-permute-start.56 = (bf16[4,112,1536]{2,1,0:T(8,128)(2,1)}, bf16[4,112,1536]{2,1,0:T(8,128)(2,1)S(1)}, u32[]{:S(2)}, u32[]{:S(2)}) collective-permute-start(bf16[4,112,1536]{2,1,0:T(8,128)(2,1)} %collective-permute-done.42.rest_2_), channel_id=1, source_target_pairs={{0,1},{1,0},{2,3},{3,2},{4,5},{5,4},{6,7},{7,6},{8,9},{9,8},{10,11... | collective-permute-start | bytes 4128776 | tf_op jit(solution)/shard_map/ppermute | solution.py:837
  300.5 30.2 %collective-permute-start.54 = (bf16[384,1536]{1,0:T(8,128)(2,1)}, bf16[384,1536]{1,0:T(8,128)(2,1)}, u32[]{:S(2)}, u32[]{:S(2)}) collective-permute-start(bf16[384,1536]{1,0:T(8,128)(2,1)} %get-tuple-element.127.rest_0_), channel_id=1, source_target_pairs={{0,16},{8,24},{16,0},{24,8},{1,17},{9,25},{17,1},{25,9},{2,18},{10... | collective-permute-start | bytes 3538952 | tf_op jit(solution)/shard_map/ppermute | solution.py:852
  310.1 35.8 %collective-permute-start.57 = (bf16[4,112,1536]{2,1,0:T(8,128)(2,1)}, bf16[4,112,1536]{2,1,0:T(8,128)(2,1)}, u32[]{:S(2)}, u32[]{:S(2)}) collective-permute-start(bf16[4,112,1536]{2,1,0:T(8,128)(2,1)} %collective-permute-done.43.rest_4_), channel_id=1, source_target_pairs={{0,1},{1,0},{2,3},{3,2},{4,5},{5,4},{6,7},{7,6},{8,9},{9,8},{10,11... | collective-permute-start | bytes 4128776 | tf_op jit(solution)/shard_map/ppermute | solution.py:837
  332.0 33.6 %collective-permute-start.64 = (bf16[384,1536]{1,0:T(8,128)(2,1)}, bf16[384,1536]{1,0:T(8,128)(2,1)}, u32[]{:S(2)}, u32[]{:S(2)}) collective-permute-start(bf16[384,1536]{1,0:T(8,128)(2,1)} %get-tuple-element.133.rest_4_), channel_id=1, source_target_pairs={{0,8},{8,0},{16,24},{24,16},{1,9},{9,1},{17,25},{25,17},{2,10},{10... | collective-permute-start | bytes 3538952 | tf_op jit(solution)/shard_map/ppermute | solution.py:852
  332.8 32.8 %collective-permute-start.65 = (bf16[384,1536]{1,0:T(8,128)(2,1)}, bf16[384,1536]{1,0:T(8,128)(2,1)}, u32[]{:S(2)}, u32[]{:S(2)}) collective-permute-start(bf16[384,1536]{1,0:T(8,128)(2,1)} %get-tuple-element.133.rest_4_), channel_id=1, source_target_pairs={{0,16},{8,24},{16,0},{24,8},{1,17},{9,25},{17,1},{25,9},{2,18},{10... | collective-permute-start | bytes 3538952 | tf_op jit(solution)/shard_map/ppermute | solution.py:852
  365.6 31.5 %collective-permute-start.68 = (bf16[2,192,1536]{2,1,0:T(8,128)(2,1)S(1)}, bf16[2,192,1536]{2,1,0:T(8,128)(2,1)S(1)}, u32[]{:S(2)}, u32[]{:S(2)}) collective-permute-start(bf16[2,192,1536]{2,1,0:T(8,128)(2,1)S(1)} %copy-done.24), channel_id=1, source_target_pairs={{0,8},{8,0},{16,24},{24,16},{1,9},{9,1},{17,25},{25,17},{2,10},{10... | collective-permute-start | bytes 3538952 | tf_op jit(solution)/shard_map/ppermute | solution.py:852
  366.4 30.8 %collective-permute-start.69 = (bf16[2,192,1536]{2,1,0:T(8,128)(2,1)S(1)}, bf16[2,192,1536]{2,1,0:T(8,128)(2,1)S(1)}, u32[]{:S(2)}, u32[]{:S(2)}) collective-permute-start(bf16[2,192,1536]{2,1,0:T(8,128)(2,1)S(1)} %copy-done.24), channel_id=1, source_target_pairs={{0,16},{8,24},{16,0},{24,8},{1,17},{9,25},{17,1},{25,9},{2,18},{10... | collective-permute-start | bytes 3538952 | tf_op jit(solution)/shard_map/ppermute | solution.py:852
  400.6 89.1 %collective-permute-start.79 = (bf16[4,128,1536]{2,1,0:T(8,128)(2,1)}, bf16[4,128,1536]{2,1,0:T(8,128)(2,1)}, u32[]{:S(2)}, u32[]{:S(2)}) collective-permute-start(bf16[4,128,1536]{2,1,0:T(8,128)(2,1)} %constant_dynamic-slice_fusion.4), channel_id=1, source_target_pairs={{0,1},{1,0},{2,3},{3,2},{4,5},{5,4},{6,7},{7,6},{8,9},{9,8},{10,11... | collective-permute-start | bytes 4718600 | tf_op jit(solution)/shard_map/ppermute | solution.py:837
  400.6 62.3 %collective-permute-start.75 = (bf16[384,1536]{1,0:T(8,128)(2,1)}, bf16[384,1536]{1,0:T(8,128)(2,1)}, u32[]{:S(2)}, u32[]{:S(2)}) collective-permute-start(bf16[384,1536]{1,0:T(8,128)(2,1)} %collective-permute-done.53.rest_1_), channel_id=1, source_target_pairs={{0,16},{8,24},{16,0},{24,8},{1,17},{9,25},{17,1},{25,9},{2,18},{10... | collective-permute-start | bytes 3538952 | tf_op jit(solution)/shard_map/ppermute | solution.py:852
  420.9 42.0 %collective-permute-start.74 = (bf16[4,128,1536]{2,1,0:T(8,128)(2,1)S(1)}, bf16[4,128,1536]{2,1,0:T(8,128)(2,1)S(1)}, u32[]{:S(2)}, u32[]{:S(2)}) collective-permute-start(bf16[4,128,1536]{2,1,0:T(8,128)(2,1)S(1)} %constant_dynamic-slice_fusion.2), channel_id=1, source_target_pairs={{0,1},{1,0},{2,3},{3,2},{4,5},{5,4},{6,7},{7,6},{8,9},{9,8},{10,11... | collective-permute-start | bytes 4718600 | tf_op jit(solution)/shard_map/ppermute | solution.py:837
  423.4 39.5 %collective-permute-start.76 = (bf16[384,1536]{1,0:T(8,128)(2,1)}, bf16[384,1536]{1,0:T(8,128)(2,1)}, u32[]{:S(2)}, u32[]{:S(2)}) collective-permute-start(bf16[384,1536]{1,0:T(8,128)(2,1)} %collective-permute-done.65.rest_6_), channel_id=1, source_target_pairs={{0,8},{8,0},{16,24},{24,16},{1,9},{9,1},{17,25},{25,17},{2,10},{10... | collective-permute-start | bytes 3538952 | tf_op jit(solution)/shard_map/ppermute | solution.py:852
  549.6 39.6 %collective-permute-start.87 = (bf16[576,1536]{1,0:T(8,128)(2,1)S(1)}, bf16[576,1536]{1,0:T(8,128)(2,1)S(1)}, u32[]{:S(2)}, u32[]{:S(2)}) collective-permute-start(bf16[576,1536]{1,0:T(8,128)(2,1)S(1)} %copy-done.78), channel_id=1, source_target_pairs={{0,16},{8,24},{16,0},{24,8},{1,17},{9,25},{17,1},{25,9},{2,18},{10... | collective-permute-start | bytes 5308424 | tf_op jit(solution)/shard_map/ppermute | solution.py:852
  551.0 39.4 %collective-permute-start.88 = (bf16[576,1536]{1,0:T(8,128)(2,1)S(1)}, bf16[576,1536]{1,0:T(8,128)(2,1)}, u32[]{:S(2)}, u32[]{:S(2)}) collective-permute-start(bf16[576,1536]{1,0:T(8,128)(2,1)S(1)} %copy-done.77), channel_id=1, source_target_pairs={{0,8},{8,0},{16,24},{24,16},{1,9},{9,1},{17,25},{25,17},{2,10},{10... | collective-permute-start | bytes 5308424 | tf_op jit(solution)/shard_map/ppermute | solution.py:852
  559.0 46.9 %collective-permute-start.83 = (bf16[128,1536]{1,0:T(8,128)(2,1)}, bf16[128,1536]{1,0:T(8,128)(2,1)S(1)}, u32[]{:S(2)}, u32[]{:S(2)}) collective-permute-start(bf16[128,1536]{1,0:T(8,128)(2,1)} %get-tuple-element.232), channel_id=1, source_target_pairs={{0,2},{1,3},{2,4},{3,5},{4,6},{5,7},{8,10},{9,11},{10,12},{11,13},... | collective-permute-start | bytes 1179656 | tf_op jit(solution)/shard_map/ppermute | solution.py:843
  565.1 40.8 %collective-permute-start.86 = (bf16[128,1536]{1,0:T(8,128)(2,1)}, bf16[128,1536]{1,0:T(8,128)(2,1)S(1)}, u32[]{:S(2)}, u32[]{:S(2)}) collective-permute-start(bf16[128,1536]{1,0:T(8,128)(2,1)} %fusion.35), channel_id=1, source_target_pairs={{2,0},{3,1},{4,2},{5,3},{6,4},{7,5},{10,8},{11,9},{12,10},{13,11},... | collective-permute-start | bytes 1179656 | tf_op jit(solution)/shard_map/ppermute | solution.py:843
  619.5 79.2 %collective-permute-start.95 = (bf16[2,576,1536]{2,1,0:T(8,128)(2,1)}, bf16[2,576,1536]{2,1,0:T(8,128)(2,1)S(1)}, u32[]{:S(2)}, u32[]{:S(2)}) collective-permute-start(bf16[2,576,1536]{2,1,0:T(8,128)(2,1)} %get-tuple-element.150), channel_id=1, source_target_pairs={{0,8},{8,0},{16,24},{24,16},{1,9},{9,1},{17,25},{25,17},{2,10},{10... | collective-permute-start | bytes 10616840 | tf_op jit(solution)/shard_map/ppermute | solution.py:852
  620.6 78.9 %collective-permute-start.96 = (bf16[2,576,1536]{2,1,0:T(8,128)(2,1)}, bf16[2,576,1536]{2,1,0:T(8,128)(2,1)}, u32[]{:S(2)}, u32[]{:S(2)}) collective-permute-start(bf16[2,576,1536]{2,1,0:T(8,128)(2,1)} %get-tuple-element.151), channel_id=1, source_target_pairs={{0,16},{8,24},{16,0},{24,8},{1,17},{9,25},{17,1},{25,9},{2,18},{10... | collective-permute-start | bytes 10616840 | tf_op jit(solution)/shard_map/ppermute | solution.py:852
  654.2 47.6 %collective-permute-start.101 = (bf16[4,4,112,1536]{3,2,1,0:T(8,128)(2,1)}, bf16[4,4,112,1536]{3,2,1,0:T(8,128)(2,1)S(1)}, u32[]{:S(2)}, u32[]{:S(2)}) collective-permute-start(bf16[4,4,112,1536]{3,2,1,0:T(8,128)(2,1)} %get-tuple-element.164), channel_id=1, source_target_pairs={{0,1},{1,0},{2,3},{3,2},{4,5},{5,4},{6,7},{7,6},{8,9},{9,8},{10,11... | collective-permute-start | bytes 16515080 | tf_op jit(solution)/shard_map/ppermute | solution.py:837
  794.2 39.9 %collective-permute-start.112 = (bf16[576,1536]{1,0:T(8,128)(2,1)}, bf16[576,1536]{1,0:T(8,128)(2,1)}, u32[]{:S(2)}, u32[]{:S(2)}) collective-permute-start(bf16[576,1536]{1,0:T(8,128)(2,1)} %get-tuple-element.176), channel_id=1, source_target_pairs={{0,16},{8,24},{16,0},{24,8},{1,17},{9,25},{17,1},{25,9},{2,18},{10... | collective-permute-start | bytes 5308424 | tf_op jit(solution)/shard_map/ppermute | solution.py:852
  795.5 39.6 %collective-permute-start.113 = (bf16[576,1536]{1,0:T(8,128)(2,1)}, bf16[576,1536]{1,0:T(8,128)(2,1)}, u32[]{:S(2)}, u32[]{:S(2)}) collective-permute-start(bf16[576,1536]{1,0:T(8,128)(2,1)} %get-tuple-element.177), channel_id=1, source_target_pairs={{0,8},{8,0},{16,24},{24,16},{1,9},{9,1},{17,25},{25,17},{2,10},{10... | collective-permute-start | bytes 5308424 | tf_op jit(solution)/shard_map/ppermute | solution.py:852
  800.6 49.9 %collective-permute-start.108 = (bf16[128,1536]{1,0:T(8,128)(2,1)}, bf16[128,1536]{1,0:T(8,128)(2,1)S(1)}, u32[]{:S(2)}, u32[]{:S(2)}) collective-permute-start(bf16[128,1536]{1,0:T(8,128)(2,1)} %get-tuple-element.228), channel_id=1, source_target_pairs={{0,2},{1,3},{2,4},{3,5},{4,6},{5,7},{8,10},{9,11},{10,12},{11,13},... | collective-permute-start | bytes 1179656 | tf_op jit(solution)/shard_map/ppermute | solution.py:843
  803.2 47.2 %collective-permute-start.111 = (bf16[128,1536]{1,0:T(8,128)(2,1)}, bf16[128,1536]{1,0:T(8,128)(2,1)S(1)}, u32[]{:S(2)}, u32[]{:S(2)}) collective-permute-start(bf16[128,1536]{1,0:T(8,128)(2,1)} %fusion.30), channel_id=1, source_target_pairs={{2,0},{3,1},{4,2},{5,3},{6,4},{7,5},{10,8},{11,9},{12,10},{13,11},... | collective-permute-start | bytes 1179656 | tf_op jit(solution)/shard_map/ppermute | solution.py:843
  865.4 38.4 %collective-permute-start.137 = (bf16[4,112,1536]{2,1,0:T(8,128)(2,1)}, bf16[4,112,1536]{2,1,0:T(8,128)(2,1)}, u32[]{:S(2)}, u32[]{:S(2)}) collective-permute-start(bf16[4,112,1536]{2,1,0:T(8,128)(2,1)} %pad_maximum_fusion.3), channel_id=1, source_target_pairs={{0,16},{8,24},{16,0},{24,8},{1,17},{9,25},{17,1},{25,9},{2,18},{10... | collective-permute-start | bytes 4128776 | tf_op jit(solution)/shard_map/ppermute | solution.py:852
  902.5 79.5 %collective-permute-start.125 = (bf16[4,4,128,1536]{3,2,1,0:T(8,128)(2,1)}, bf16[4,4,128,1536]{3,2,1,0:T(8,128)(2,1)}, u32[]{:S(2)}, u32[]{:S(2)}) collective-permute-start(bf16[4,4,128,1536]{3,2,1,0:T(8,128)(2,1)} %get-tuple-element.201), channel_id=1, source_target_pairs={{0,1},{1,0},{2,3},{3,2},{4,5},{5,4},{6,7},{7,6},{8,9},{9,8},{10,11... | collective-permute-start | bytes 18874376 | tf_op jit(solution)/shard_map/ppermute | solution.py:837
  902.8 32.6 %collective-permute-start.136 = (bf16[4,112,1536]{2,1,0:T(8,128)(2,1)S(1)}, bf16[4,112,1536]{2,1,0:T(8,128)(2,1)S(1)}, u32[]{:S(2)}, u32[]{:S(2)}) collective-permute-start(bf16[4,112,1536]{2,1,0:T(8,128)(2,1)S(1)} %pad_maximum_fusion.2), channel_id=1, source_target_pairs={{0,8},{8,0},{16,24},{24,16},{1,9},{9,1},{17,25},{25,17},{2,10},{10... | collective-permute-start | bytes 4128776 | tf_op jit(solution)/shard_map/ppermute | solution.py:852
  969.2 43.6 %collective-permute-start.118 = (bf16[512,1536]{1,0:T(8,128)(2,1)}, bf16[512,1536]{1,0:T(8,128)(2,1)S(1)}, u32[]{:S(2)}, u32[]{:S(2)}) collective-permute-start(bf16[512,1536]{1,0:T(8,128)(2,1)} %get-tuple-element.190), channel_id=1, source_target_pairs={{0,1},{1,0},{2,3},{3,2},{4,5},{5,4},{6,7},{7,6},{8,9},{9,8},{10,11... | collective-permute-start | bytes 4718600 | tf_op jit(solution)/shard_map/ppermute | solution.py:837
  1006.8 37.4 %collective-permute-start.129 = (bf16[4,128,1536]{2,1,0:T(8,128)(2,1)S(1)}, bf16[4,128,1536]{2,1,0:T(8,128)(2,1)S(1)}, u32[]{:S(2)}, u32[]{:S(2)}) collective-permute-start(bf16[4,128,1536]{2,1,0:T(8,128)(2,1)S(1)} %pad_maximum_fusion.1), channel_id=1, source_target_pairs={{0,16},{8,24},{16,0},{24,8},{1,17},{9,25},{17,1},{25,9},{2,18},{10... | collective-permute-start | bytes 4718600 | tf_op jit(solution)/shard_map/ppermute | solution.py:852
  1008.4 37.4 %collective-permute-start.127 = (bf16[4,128,1536]{2,1,0:T(8,128)(2,1)S(1)}, bf16[4,128,1536]{2,1,0:T(8,128)(2,1)S(1)}, u32[]{:S(2)}, u32[]{:S(2)}) collective-permute-start(bf16[4,128,1536]{2,1,0:T(8,128)(2,1)S(1)} %pad_maximum_fusion), channel_id=1, source_target_pairs={{0,8},{8,0},{16,24},{24,16},{1,9},{9,1},{17,25},{25,17},{2,10},{10... | collective-permute-start | bytes 4718600 | tf_op jit(solution)/shard_map/ppermute | solution.py:852
  1010.9 109.3 %collective-permute-start.144 = (bf16[2,576,1536]{2,1,0:T(8,128)(2,1)S(1)}, bf16[2,576,1536]{2,1,0:T(8,128)(2,1)}, u32[]{:S(2)}, u32[]{:S(2)}) collective-permute-start(bf16[2,576,1536]{2,1,0:T(8,128)(2,1)S(1)} %copy-done.76), channel_id=1, source_target_pairs={{0,8},{8,0},{16,24},{24,16},{1,9},{9,1},{17,25},{25,17},{2,10},{10... | collective-permute-start | bytes 10616840 | tf_op jit(solution)/shard_map/ppermute | solution.py:852
  1012.0 108.1 %collective-permute-start.145 = (bf16[2,576,1536]{2,1,0:T(8,128)(2,1)S(1)}, bf16[2,576,1536]{2,1,0:T(8,128)(2,1)}, u32[]{:S(2)}, u32[]{:S(2)}) collective-permute-start(bf16[2,576,1536]{2,1,0:T(8,128)(2,1)S(1)} %copy-done.75), channel_id=1, source_target_pairs={{0,16},{8,24},{16,0},{24,8},{1,17},{9,25},{17,1},{25,9},{2,18},{10... | collective-permute-start | bytes 10616840 | tf_op jit(solution)/shard_map/ppermute | solution.py:852
  1013.3 43.4 %collective-permute-start.119 = (bf16[128,1536]{1,0:T(8,128)(2,1)S(1)}, bf16[128,1536]{1,0:T(8,128)(2,1)S(1)}, u32[]{:S(2)}, u32[]{:S(2)}) collective-permute-start(bf16[128,1536]{1,0:T(8,128)(2,1)S(1)} %get-tuple-element.226), channel_id=1, source_target_pairs={{0,2},{1,3},{8,10},{9,11},{16,18},{17,19},{24,26},{25,27}} | collective-permute-start | bytes 1179656 | tf_op jit(solution)/shard_map/ppermute | solution.py:843
  1076.3 66.0 %collective-permute-start.121 = (bf16[128,1536]{1,0:T(8,128)(2,1)}, bf16[128,1536]{1,0:T(8,128)(2,1)}, u32[]{:S(2)}, u32[]{:S(2)}) collective-permute-start(bf16[128,1536]{1,0:T(8,128)(2,1)} %get-tuple-element.224), channel_id=1, source_target_pairs={{0,2},{1,3},{2,4},{3,5},{4,6},{5,7},{8,10},{9,11},{10,12},{11,13},... | collective-permute-start | bytes 1179656 | tf_op jit(solution)/shard_map/ppermute | solution.py:843
  1084.1 55.7 %collective-permute-start.134 = (bf16[128,1536]{1,0:T(8,128)(2,1)}, bf16[128,1536]{1,0:T(8,128)(2,1)}, u32[]{:S(2)}, u32[]{:S(2)}) collective-permute-start(bf16[128,1536]{1,0:T(8,128)(2,1)} %get-tuple-element.219), channel_id=1, source_target_pairs={{4,2},{5,3},{6,4},{7,5},{12,10},{13,11},{14,12},{15,13},{20,18},{2... | collective-permute-start | bytes 1179656 | tf_op jit(solution)/shard_map/ppermute | solution.py:843
  1086.4 55.9 %collective-permute-start.124 = (bf16[128,1536]{1,0:T(8,128)(2,1)}, bf16[128,1536]{1,0:T(8,128)(2,1)}, u32[]{:S(2)}, u32[]{:S(2)}) collective-permute-start(bf16[128,1536]{1,0:T(8,128)(2,1)} %fusion.24), channel_id=1, source_target_pairs={{2,0},{3,1},{4,2},{5,3},{6,4},{7,5},{10,8},{11,9},{12,10},{13,11},... | collective-permute-start | bytes 1179656 | tf_op jit(solution)/shard_map/ppermute | solution.py:843
  (180 other events, 2108.4 us)

commit v3 on v2

--- a/solution.py
+++ b/solution.py
@@ -86,10 +86,6 @@
     return lax.dot_general(left, right, (((0,), (0,)), ((), ())), preferred_element_type=WIDE)
 
 
-def after(value, *earlier):
-    return lax.optimization_barrier((value, *earlier))[0]
-
-
 ROWS = 128
 LINE = 4
 GROUP = 2 * LINE * ROWS
@@ -103,11 +99,15 @@
 
 
 def cost(microseconds):
-    return pl.CostEstimate(flops=0, bytes_accessed=int(microseconds * 0.4e6), transcendentals=0)
+    return pl.CostEstimate(flops=0, bytes_accessed=int(microseconds * 3.7e6), transcendentals=0)
 
 
 LIMIT = 60 * 1024 * 1024
 SCALE = HEAD**-0.5
+
+
+def shape(dims, dtype):
+    return jax.ShapeDtypeStruct(dims, dtype)
 
 
 def spec(shape, index=None):
@@ -120,14 +120,36 @@
 SCALARS = pl.BlockSpec(memory_space=pltpu.SMEM)
 
 
+def after(values, *earlier):
+    several = isinstance(values, (tuple, list))
+    group = list(values) if several else [values]
+    result = pl.pallas_call(
+        lambda *refs: None,
+        out_shape=[shape(v.shape, v.dtype) for v in group],
+        in_specs=[ANYWHERE] * (len(group) + len(earlier)),
+        out_specs=[ANYWHERE] * len(group),
+        input_output_aliases={i: i for i in range(len(group))},
+        name="after",
+        cost_estimate=cost(0),
+    )(*group, *earlier)
+    return result if several else result[0]
+
+
 def place_scalars():
     dp, cp = lax.axis_index("dp"), lax.axis_index("cp")
     return jnp.stack([dp, cp % 2, cp, cp // 2]).astype(jnp.int32)
 
 
-def call(body, name, grid, arguments, in_specs, outs, out_specs, scratch, microseconds):
+def call(body, name, grid, arguments, in_specs, outs, out_specs, scratch, microseconds, earlier=()):
+    count = len(arguments)
+    arguments = [*arguments, *earlier]
+    in_specs = [*in_specs, *[ANYWHERE] * len(earlier)]
+
+    def whole(*refs):
+        body(*refs[:count], *refs[len(arguments) :])
+
     return pl.pallas_call(
-        body,
+        whole,
         grid=grid,
         out_shape=outs,
         in_specs=in_specs,
@@ -139,10 +161,6 @@
     )(*arguments)
 
 
-def shape(dims, dtype):
-    return jax.ShapeDtypeStruct(dims, dtype)
-
-
 class Dense:
     def __init__(self, pieces, first_row, rows):
         self.pieces = pieces
@@ -174,11 +192,12 @@
     for expert in range(EXP_DEV):
         for flip in range(4):
             part = places[0] ^ flip
+            far = refs[9 + expert]
             first = pl.multiple_of(part * GROWS, GROWS)
-            target = gate_up.at[expert, pl.ds(first, GROWS)]
-            made.append((refs[4 * expert + flip], target))
-            source = refs[8 + flip].at[expert] if flip < 3 else refs[11 + expert]
+            source = refs[3 * expert + flip] if flip < 3 else far.at[pl.ds(0, GROWS)]
+            made.append((source, gate_up.at[expert, pl.ds(first, GROWS)]))
             first = pl.multiple_of(part * FROWS, FROWS)
+            source = refs[6 + flip].at[expert] if flip < 3 else far.at[pl.ds(GROWS, FROWS)]
             made.append((source, down.at[expert, pl.ds(first, FROWS)]))
     return [
         pltpu.make_async_copy(source, target, sems.at[number])
@@ -226,11 +245,11 @@
         out,
         spec(out.shape),
         [pltpu.SemaphoreType.DMA((count,))],
-        3,
-    )
-
-
-def project_call(value, gain, query, tables):
+        0,
+    )
+
+
+def project_call(value, gain, query, tables, earlier=()):
     count = len(query.pieces)
 
     def body(places, value_ref, gain_ref, tables_ref, *rest):
@@ -266,11 +285,12 @@
         outs,
         [spec(o.shape) for o in outs],
         [*query.scratch(), pltpu.VMEM((4, ROWS, 8 * QROWS), WIDE)],
-        7,
-    )
-
-
-def attend_call(value, heads, keys_values, query_meta, key_meta, output, gain):
+        0,
+        earlier,
+    )
+
+
+def attend_call(value, heads, keys_values, query_meta, key_meta, output, gain, earlier=()):
     count = len(output.pieces)
 
     def body(places, value_ref, heads_ref, kv_own, kv_other, qmeta, kmeta, gain_ref, *rest):
@@ -337,7 +357,8 @@
         outs,
         [spec(o.shape) for o in outs],
         [*output.scratch(), pltpu.VMEM((ROWS, HQ), LOW), pltpu.VMEM((GROUP, 2 * KVW), LOW)],
-        9,
+        0,
+        earlier,
     )
 
 
@@ -361,14 +382,16 @@
     return jnp.where(step < STEPS // 2, own_ref[...], other_ref[...])
 
 
-def put_halves(step, own_ref, other_ref, values):
+def put_halves(step, own_ref, other_refs, values):
     @pl.when(step < STEPS // 2)
     def own():
         own_ref[...] = values
 
-    @pl.when(step >= STEPS // 2)
-    def other():
-        other_ref[...] = values
+    for number, ref in enumerate(other_refs):
+
+        @pl.when(step == STEPS // 2 + number)
+        def other():
+            ref[...] = values
 
 
 def own_gate(gates, places, expert):
@@ -378,11 +401,11 @@
     )
 
 
-def experts_call(mixed, routes, router, pieces):
+def experts_call(mixed, routes, router, pieces, earlier=()):
     def body(places, mixed_own, mixed_other, routes_ref, router_ref, *rest):
-        refs, (own_ref, other_ref, gu_ref, hidden_ref, gates_ref, gate_up, down, sems) = (
-            rest[:13],
-            rest[13:],
+        refs, (own_ref, *other_refs, gu_ref, hidden_ref, gates_ref, gate_up, down, sems) = (
+            rest[:11],
+            rest[11:],
         )
         step = pl.program_id(0)
         copies = expert_copies(refs, places, gate_up, down, sems)
@@ -415,11 +438,12 @@
             hidden_ref[:, pl.ds(expert * FF, FF)] = hidden
             product = dot(hidden, down[expert])
             terms = product if terms is None else terms + product
-        put_halves(step, own_ref, other_ref, terms.astype(LOW))
+        put_halves(step, own_ref, other_refs, terms.astype(LOW))
 
     outs = [
         shape((HALF, D), LOW),
-        shape((HALF, D), LOW),
+        shape((BLOCK, D), LOW),
+        shape((BLOCK, D), LOW),
         shape((GROUP, EXP_DEV * 2 * FF), LOW),
         shape((GROUP, EXP_DEV * FF), LOW),
         shape((GROUP, EXPERTS), WIDE),
@@ -436,25 +460,27 @@
             spec((BLOCK, TOP), rows_at),
             spec((D, EXPERTS)),
         ]
-        + [ANYWHERE] * 13,
+        + [ANYWHERE] * 11,
         outs,
         [
             spec((BLOCK, D), own_half),
-            spec((BLOCK, D), other_half),
+            spec((BLOCK, D)),
+            spec((BLOCK, D)),
             spec((BLOCK, EXP_DEV * 2 * FF), rows_at),
             spec((BLOCK, EXP_DEV * FF), rows_at),
             spec((BLOCK, EXPERTS), rows_at),
         ],
         EXPERT_SCRATCH,
-        26,
-    )
-
-
-def experts_back_call(upstream, gate_up_kept, gates, router, pieces):
+        8,
+        earlier,
+    )
+
+
+def experts_back_call(upstream, gate_up_kept, gates, router, pieces, earlier=()):
     def body(places, up_own, up_other, gu_ref, gates_ref, router_ref, *rest):
-        refs, (own_ref, other_ref, grad_ref, logits_ref, gate_up, down, sems) = (
-            rest[:13],
-            rest[13:],
+        refs, (own_ref, *other_refs, grad_ref, logits_ref, gate_up, down, sems) = (
+            rest[:11],
+            rest[11:],
         )
         step = pl.program_id(0)
         copies = expert_copies(refs, places, gate_up, down, sems)
@@ -492,12 +518,13 @@
             terms = product if terms is None else terms + product
         grad_logits = grad_logits.astype(LOW)
         terms = terms + dot(grad_logits, router_ref[...])
-        put_halves(step, own_ref, other_ref, terms.astype(LOW))
+        put_halves(step, own_ref, other_refs, terms.astype(LOW))
         logits_ref[...] = grad_logits
 
     outs = [
         shape((HALF, D), LOW),
-        shape((HALF, D), LOW),
+        shape((BLOCK, D), LOW),
+        shape((BLOCK, D), LOW),
         shape((GROUP, EXP_DEV * 2 * FF), LOW),
         shape((GROUP, EXPERTS), LOW),
     ]
@@ -514,24 +541,25 @@
             spec((BLOCK, EXPERTS), rows_at),
             spec((EXPERTS, D)),
         ]
-        + [ANYWHERE] * 13,
+        + [ANYWHERE] * 11,
         outs,
         [
             spec((BLOCK, D), own_half),
-            spec((BLOCK, D), other_half),
+            spec((BLOCK, D)),
+            spec((BLOCK, D)),
             spec((BLOCK, EXP_DEV * 2 * FF), rows_at),
             spec((BLOCK, EXPERTS), rows_at),
         ],
         EXPERT_SCRATCH,
-        26,
+        8,
+        earlier,
     )
 
 
 def expert_grads_call(
-    flips, mixed, grad_gate_up, hidden, upstream, received=(), layer=None, results=None
+    flips, mixed, grad_gate_up, hidden, upstream, received=(), layer=None, results=None, earlier=()
 ):
     last = layer is not None
-    apart = len(flips) == 1 and not last
     kept = () if results is None else tuple(results)
     count = len(flips)
 
@@ -539,7 +567,7 @@
         mixed_refs, rest = rest[: 2 * count], rest[2 * count :]
         hidden_refs, rest = rest[: 2 * count], rest[2 * count :]
         grad_ref, up_own, up_other = rest[:3]
-        sums, outs = rest[3 : 3 + len(received)], rest[3 + len(received) + len(kept) :]
+        sums, outs = rest[3 : 3 + len(received)], rest[3 + len(received) + len(kept) + len(earlier) :]
         expert = pl.program_id(0)
         for number, flip in enumerate(flips):
             gate_up = t_dot(mixed_refs[2 * number][...], grad_ref[pl.ds(0, HALF)])
@@ -551,9 +579,7 @@
             for ref, (unused, whose, only) in zip(sums, received):
                 if whose != number:
                     continue
-                held = (ref[...] if only is not None else ref[0]).astype(WIDE)
-                if only is not None:
-                    held = jnp.where(expert == only, held, 0.0)
+                held = jnp.where(expert == only, ref[...].astype(WIDE), 0.0)
                 gate_up = gate_up + held[:GROWS]
                 down = down + held[GROWS:]
             if last:
@@ -562,19 +588,13 @@
                 continue
             gate_up = gate_up.astype(LOW)
             down = down.astype(LOW)
-            if apart:
-                for own in range(EXP_DEV):
-
-                    @pl.when(expert == own)
-                    def put():
-                        outs[own][pl.ds(0, GROWS)] = gate_up
-                        outs[own][pl.ds(GROWS, FROWS)] = down
-
-            else:
-                outs[number][0, pl.ds(0, GROWS)] = gate_up
-                outs[number][0, pl.ds(GROWS, FROWS)] = down
-
-    each = lambda e, places: (e, 0, 0)
+            for own in range(EXP_DEV):
+
+                @pl.when(expert == own)
+                def put():
+                    outs[EXP_DEV * number + own][pl.ds(0, GROWS)] = gate_up
+                    outs[EXP_DEV * number + own][pl.ds(GROWS, FROWS)] = down
+
     whole = lambda e, places: (0, 0)
     if last:
         at_layer = lambda e, places: (layer, e, 0, 0)
@@ -583,12 +603,9 @@
             pl.BlockSpec((1, 1, GROWS, D), at_layer),
             pl.BlockSpec((1, 1, FROWS, D), at_layer),
         ]
-    elif apart:
-        outs = [shape((GROWS + FROWS, D), LOW)] * EXP_DEV
-        out_specs = [pl.BlockSpec((GROWS + FROWS, D), whole)] * EXP_DEV
     else:
-        outs = [shape((EXP_DEV, GROWS + FROWS, D), LOW)] * count
-        out_specs = [pl.BlockSpec((1, GROWS + FROWS, D), each)] * count
+        outs = [shape((GROWS + FROWS, D), LOW)] * (count * EXP_DEV)
+        out_specs = [pl.BlockSpec((GROWS + FROWS, D), whole)] * (count * EXP_DEV)
     in_specs = []
     for flip in flips:
         in_specs += [pl.BlockSpec((HALF, GROWS), lambda e, places, flip=flip: (0, places[0] ^ flip))] * 2
@@ -608,13 +625,8 @@
         pl.BlockSpec((HALF, D), whole),
         pl.BlockSpec((HALF, D), whole),
     ]
-    for unused, whose, only in received:
-        in_specs.append(
-            pl.BlockSpec((1, GROWS + FROWS, D), each)
-            if only is None
-            else pl.BlockSpec((GROWS + FROWS, D), whole)
-        )
-    in_specs += [ANYWHERE] * len(kept)
+    in_specs += [pl.BlockSpec((GROWS + FROWS, D), whole)] * len(received)
+    in_specs += [ANYWHERE] * (len(kept) + len(earlier))
     first_kept = 1 + 4 * count + 3 + len(received)
     return pl.pallas_call(
         body,
@@ -625,7 +637,7 @@
         ),
         name="expert_grads",
         compiler_params=pltpu.CompilerParams(vmem_limit_bytes=LIMIT),
-        cost_estimate=cost(15 if count > 1 else 11),
+        cost_estimate=cost(4 if last else 0),
     )(
         place_scalars(),
         *(list(mixed) * count),
@@ -634,6 +646,7 @@
         *upstream,
         *(array for array, unused, only in received),
         *kept,
+        *earlier,
     )
 
 
@@ -645,7 +658,9 @@
     return (grads, jnp.sum(values * scale_rows * upstream, axis=0, keepdims=True))
 
 
-def attend_back_call(grad_mixed, middle, gain, upstream, output, low, probs, heads, keys_values):
+def attend_back_call(
+    grad_mixed, middle, gain, upstream, output, low, probs, heads, keys_values, earlier=()
+):
     count = len(output.pieces)
 
     def body(
@@ -723,11 +738,12 @@
         outs,
         [spec(o.shape) for o in outs],
         [*output.scratch(), pltpu.VMEM((GROUP, 2 * KVW), WIDE), pltpu.VMEM((GROUP, 2 * KVW), LOW)],
-        12,
-    )
-
-
-def project_back_call(grad_heads, grad_kv, tables, query, value, gain, grad_middle):
+        0,
+        earlier,
+    )
+
+
+def project_back_call(grad_heads, grad_kv, tables, query, value, gain, grad_middle, earlier=()):
     count = len(query.pieces)
 
     def body(places, gq_ref, gkv_ref, tables_ref, value_ref, gain_ref, gm_ref, *rest):
@@ -778,34 +794,39 @@
         outs,
         [spec(o.shape) for o in outs],
         query.scratch(),
-        7,
-    )
-
-
-def dense_grads_call(joined, normed, low, error, small):
+        0,
+        earlier,
+    )
+
+
+def dense_grads_call(joined, normed, low, error, small, earlier=()):
     rows = QROWS + OROWS + (SMALL if small is not None else 0)
 
     def body(places, joined_ref, normed_ref, low_ref, error_ref, *rest):
-        mine_ref, other_ref = rest[-2:]
+        mine_refs, other_refs = rest[-8:-4], rest[-4:]
+        flip = pl.program_id(0)
         query = t_dot(joined_ref[...], normed_ref[...]).astype(LOW).reshape(LINE, 2, QROWS, D)
         outs = t_dot(low_ref[...], error_ref[...]).astype(LOW).reshape(LINE, 2, OROWS, D)
         for core in range(2):
 
             def put(ref):
-                ref[0, :, pl.ds(0, QROWS)] = query[:, core]
-                ref[0, :, pl.ds(QROWS, OROWS)] = outs[:, core]
+                ref[:, pl.ds(0, QROWS)] = query[:, core]
+                ref[:, pl.ds(QROWS, OROWS)] = outs[:, core]
                 if small is not None:
-                    ref[0, :, pl.ds(QROWS + OROWS, SMALL)] = rest[0][0, :, core]
-
-            @pl.when(places[1] == core)
-            def mine():
-                put(mine_ref)
-
-            @pl.when(places[1] != core)
-            def other():
-                put(other_ref)
-
-    out = shape((4, LINE, rows, D), LOW)
+                    ref[:, pl.ds(QROWS + OROWS, SMALL)] = rest[0][0, :, core]
+
+            for at in range(4):
+
+                @pl.when((flip == at) & (places[1] == core))
+                def mine():
+                    put(mine_refs[at])
+
+                @pl.when((flip == at) & (places[1] != core))
+                def other():
+                    put(other_refs[at])
+
+    out = shape((LINE, rows, D), LOW)
+    count = len(earlier)
     part = lambda flip, places: (0, places[0] ^ flip)
     whole = lambda flip, places: (0, 0)
     in_specs = [
@@ -820,17 +841,19 @@
             pl.BlockSpec((1, LINE, 2, SMALL, D), lambda flip, places: (places[0] ^ flip, 0, 0, 0, 0))
         )
         arguments.append(small)
-    out_spec = pl.BlockSpec((1, LINE, rows, D), lambda flip, places: (flip, 0, 0, 0))
-    return pl.pallas_call(
+    in_specs += [ANYWHERE] * count
+    out_spec = pl.BlockSpec((LINE, rows, D), lambda flip, places: (0, 0, 0))
+    grads = pl.pallas_call(
         body,
-        out_shape=[out, out],
+        out_shape=[out] * 8,
         grid_spec=pltpu.PrefetchScalarGridSpec(
-            num_scalar_prefetch=1, grid=(4,), in_specs=in_specs, out_specs=[out_spec, out_spec]
+            num_scalar_prefetch=1, grid=(4,), in_specs=in_specs, out_specs=[out_spec] * 8
         ),
         name="dense_grads",
         compiler_params=pltpu.CompilerParams(vmem_limit_bytes=LIMIT),
-        cost_estimate=cost(9),
-    )(place_scalars(), *arguments)
+        cost_estimate=cost(0),
+    )(place_scalars(), *arguments, *earlier)
+    return (grads[:4], grads[4:])
 
 
 def swap_core(value):
@@ -852,14 +875,11 @@
     return lax.ppermute(value, "dp", [(i, i ^ flip) for i in range(4)])
 
 
-def line_gather(value, *stages):
+def line_gather(value):
     place = lax.axis_index("cp") // 2
     rising, falling = value, value
     risen, fallen = [], []
     for step in range(1, LINE):
-        if step <= len(stages):
-            rising = after(rising, *stages[step - 1])
-            falling = after(falling, *stages[step - 1])
         rising = hop(rising, True, range(step - 1, LINE - 1))
         falling = hop(falling, False, range(1, LINE - step + 1))
         risen.insert(0, rising)
@@ -887,25 +907,25 @@
         if step > 1:
             up = (up.astype(WIDE) + rising.astype(WIDE)).astype(LOW)
             down = (down.astype(WIDE) + falling.astype(WIDE)).astype(LOW)
-        if step <= len(stages):
-            up = after(up, *stages[step - 1])
-            down = after(down, *stages[step - 1])
+        if step <= len(stages) and stages[step - 1]:
+            up, down = after((up, down), *stages[step - 1])
         rising = hop(up, True, range(step))
         falling = hop(down, False, range(LINE - step, LINE))
     return pick(place).astype(WIDE) + rising.astype(WIDE) + falling.astype(WIDE)
 
 
-def group_gather(value, *stages):
-    mine = line_gather(value, *stages[: LINE - 1])
-    for stage in stages[LINE - 1 :]:
-        mine = after(mine, *stage)
+def group_gather(value):
+    mine = line_gather(value)
     other = swap_core(mine)
     return (mine.reshape(HALF, -1), other.reshape(HALF, -1))
 
 
-def group_scatter(own, other, first=(), *stages):
-    both = (own.astype(WIDE) + swap_core(after(other, *first)).astype(WIDE)).astype(LOW)
-    return line_scatter(both.reshape(LINE, ROWS, -1), *stages)
+def group_scatter(own, others, *stages):
+    if stages and stages[0]:
+        others = after(others, *stages[0])
+    other = jnp.concatenate([swap_core(part) for part in others], axis=0)
+    both = (own.astype(WIDE) + other.astype(WIDE)).astype(LOW)
+    return line_scatter(both.reshape(LINE, ROWS, -1), *stages[1:])
 
 
 def earlier_gather(value):
@@ -946,7 +966,9 @@
     return pieces
 
 
-def dense_square_scatter(mine, received, *earlier):
+def dense_square_scatter(mine, others, *earlier):
+    received = [swap_core(other) for other in others]
+
     def piece(flip):
         return mine[flip].astype(WIDE) + received[flip].astype(WIDE)
 
@@ -960,7 +982,16 @@
     got_x = across(to_x, 1)
     got_y = across(to_y, 2)
     plane = piece(0) + got_x.astype(WIDE) + got_y.astype(WIDE)
-    return ((from_x, from_y), (got_x, got_y), plane.astype(LOW))
+    return ((from_x, from_y), (to_x, to_y), (got_x, got_y), plane.astype(LOW))
+
+
+def in_order(own, other):
+    own, other = (rows.reshape(LINE, 1, ROWS, -1) for rows in (own, other))
+    first = lax.axis_index("cp") % 2 == 0
+    rows = jnp.where(
+        first, jnp.concatenate([own, other], axis=1), jnp.concatenate([other, own], axis=1)
+    )
+    return rows.reshape(GROUP, -1)
 
 
 def square_line_shards(
@@ -999,43 +1030,48 @@
     small = jnp.concatenate([small, route_numbers], axis=0)
     small = jnp.pad(small, ((0, SMALL - small_rows - 1), (0, 0)))
 
-    gate_x, gate_y = square_step(w_gate_up[0, 0])
+    own_gate_ups = [[w_gate_up[l, e] for e in range(EXP_DEV)] for l in range(LAYERS)]
+    own_downs = [w_down[l] for l in range(LAYERS)]
+    gate_ups = [[square_step(own_gate_ups[0][0])], []]
     first = line_gather(jnp.concatenate([w_qkv[0], w_out[0], small], axis=0))
-    second = jnp.concatenate([w_qkv[1], w_out[1], cotangent], axis=0)
-    second = line_gather(after(second, first))
+    second = line_gather(after(jnp.concatenate([w_qkv[1], w_out[1], cotangent], axis=0), first))
+    first = after(first, *gate_ups[0][0])
     dense_rows = QROWS + OROWS
     upstream_line = second[:, dense_rows:]
     second = second[:, :dense_rows]
-    first_x, first_y = square_step(after(first, gate_x, gate_y))
-    first_far = square_far(first_x, first_y)
-    pieces = dense_pieces(first, first_x, first_y, first_far)
+    first_near = square_step(first)
+    first_far = square_far(*first_near)
+    pieces = dense_pieces(first, *first_near, first_far)
     query, output = Dense(pieces, 0, QROWS), Dense(pieces, QROWS, OROWS)
     small = small_call(Dense(pieces, dense_rows, SMALL))
 
     def expert_weights(layer, first, more, down, far):
-        gate_ups = [w_gate_up[layer, 0], *first, far[0], w_gate_up[layer, 1], *more, far[1]]
-        return gate_ups + [w_down[layer], *down, far[2], far[3]]
+        own = own_gate_ups[layer]
+        return [own[0], *first, own[1], *more, own_downs[layer], *down, *far]
 
     def experts_far(first, more, down):
-        return (
-            across(after(first[0], *down), 2),
-            across(after(more[1], *down), 1),
-            across(down[0][0], 2),
-            across(down[1][1], 1),
-        )
-
-    gate_ups = [[(gate_x, gate_y)], []]
-    gate_ups[0].append(square_step(after(w_gate_up[0, 1], *first_far)))
-    downs = [square_step(after(w_down[0], *gate_ups[0][1]))]
+        by_x = jnp.concatenate([first[0], down[0][0]], axis=0)
+        by_y = jnp.concatenate([more[1], down[1][1]], axis=0)
+        by_x, by_y = after((by_x, by_y), *more, *down)
+        return (across(by_x, 2), across(by_y, 1))
+
+    own_gate_ups[0][1] = after(own_gate_ups[0][1], *first_far)
+    gate_ups[0].append(square_step(own_gate_ups[0][1]))
+    own_downs[0] = after(own_downs[0], *first_far)
+    downs = [square_step(own_downs[0])]
     fars = [experts_far(*gate_ups[0], downs[0])]
     weights = [(query, output, expert_weights(0, *gate_ups[0], downs[0], fars[0]))]
-    second_near = square_step(after(second, *fars[0]))
+    second = after(second, *fars[0])
+    second_near = square_step(second)
     second_far = square_far(*second_near)
     pieces = dense_pieces(second, *second_near, second_far)
     query, output = Dense(pieces, 0, QROWS), Dense(pieces, QROWS, OROWS)
-    gate_ups[1].append(square_step(after(w_gate_up[1, 0], *second_far)))
-    gate_ups[1].append(square_step(after(w_gate_up[1, 1], *gate_ups[1][0])))
-    downs.append(square_step(after(w_down[1], *gate_ups[1][1])))
+    own_gate_ups[1][0] = after(own_gate_ups[1][0], *second_far)
+    gate_ups[1].append(square_step(own_gate_ups[1][0]))
+    own_gate_ups[1][1] = after(own_gate_ups[1][1], *gate_ups[1][0])
+    gate_ups[1].append(square_step(own_gate_ups[1][1]))
+    own_downs[1] = after(own_downs[1], *gate_ups[1][0])
+    downs.append(square_step(own_downs[1]))
     fars.append(experts_far(*gate_ups[1], downs[1]))
     weights.append((query, output, expert_weights(1, *gate_ups[1], downs[1], fars[1])))
 
@@ -1051,64 +1087,75 @@
     numbers = numbers.reshape(LINE, 2, LAYERS, ROWS, TOP).transpose(2, 1, 0, 3, 4)
     group_routes = numbers.reshape(LAYERS, GROUP, TOP)
 
-    value = after(tokens, second).astype(WIDE)
+    value = tokens.astype(WIDE)
+    before_project = [(), gate_ups[1][0]]
+    before_attend = [(upstream_line, routers, group_routes), ()]
     stored = []
     for layer in range(LAYERS):
         query, output, pieces = weights[layer]
-        normed, heads, kv = project_call(value, gain_rows[layer, 0], query, tables)
+        normed, heads, kv = project_call(
+            value, gain_rows[layer, 0], query, tables, before_project[layer]
+        )
         keys_values = earlier_gather(kv)
-        if layer == 0:
-            keys_values = (after(keys_values[0], *gate_ups[0][1], routers, group_routes), keys_values[1])
         low, probs, middle, mixed = attend_call(
-            value, heads, keys_values, query_meta, key_meta, output, gain_rows[layer, 1]
-        )
-        if layer == 0:
-            mixed = group_gather(mixed, (), downs[0])
-        else:
-            mixed = group_gather(mixed, gate_ups[1][1], (), downs[1])
-        own, other, gate_up, hidden, gates = experts_call(
+            value,
+            heads,
+            keys_values,
+            query_meta,
+            key_meta,
+            output,
+            gain_rows[layer, 1],
+            before_attend[layer],
+        )
+        mixed = group_gather(mixed)
+        own, *others, gate_up, hidden, gates = experts_call(
             mixed, group_routes[layer], routers[layer].T, pieces
         )
         stored.append((value, normed, heads, keys_values, low, probs, middle, mixed, gate_up, hidden, gates))
         if layer == 0:
-            value = middle + group_scatter(own, other, second_near, (), second_far, ())
-            value = after(value, *gate_ups[1][0])
-    last_sums = (own, other)
+            value = middle + group_scatter(own, others, second_near, (), second_far)
+    last_sums = (own, others)
 
     upstream_group = (upstream_line.reshape(HALF, D), swap_core(upstream_line).reshape(HALF, D))
     upstream = cotangent.astype(WIDE)
-    expert_grads = None
-    dense_grads, router_grads, gain_grads = ([None] * LAYERS for _ in range(3))
+    router_grads, gain_grads = ([None] * LAYERS for _ in range(2))
+    before_back = before_scatter = ()
     for layer in reversed(range(LAYERS)):
         query, output, pieces = weights[layer]
         value, normed, heads, keys_values, low, probs, middle, mixed, gate_up, hidden, gates = stored[layer]
-        own, other, grad_gate_up, grad_logits = experts_back_call(
-            upstream_group, gate_up, gates, routers[layer], pieces
+        own, *others, grad_gate_up, grad_logits = experts_back_call(
+            upstream_group, gate_up, gates, routers[layer], pieces, before_back
         )
         router_grads[layer] = t_dot(grad_logits[:HALF], mixed[0]) + t_dot(grad_logits[HALF:], mixed[1])
         terms = (mixed, grad_gate_up, hidden, upstream_group)
         far = expert_grads_call((3,), *terms)
         from_x = across(far[0], 1)
         from_y = across(far[1], 2)
-        if layer < LAYERS - 1:
-            far = [after(part, *dense_sums[1]) for part in far]
-        grad_mixed = group_scatter(own, other, far)
-        to_x, to_y = expert_grads_call(
+        grad_mixed = group_scatter(own, others, before_scatter, far, (), (from_x, from_y))
+        to_x0, to_x1, to_y0, to_y1 = expert_grads_call(
             (1, 2), *terms, received=[(from_y, 0, 1), (from_x, 1, 0)]
         )
-        grad_mixed = after(grad_mixed, to_x, to_y)
-        got_x = across(to_x, 1)
-        got_y = across(to_y, 2)
-        expert_sums = (got_x, got_y)
-        expert_grads = expert_grads_call(
-            (0,),
-            *terms,
-            received=[(got_x, 0, None), (got_y, 0, None)],
+        got = [(across(to_x0, 1), across(to_y0, 2)), (across(to_x1, 1), across(to_y1, 2))]
+        last_part = dict(
+            flips=(0,),
+            mixed=mixed,
+            grad_gate_up=grad_gate_up,
+            hidden=hidden,
+            upstream=upstream_group,
+            received=[(got[e][k], 0, e) for e in range(EXP_DEV) for k in range(2)],
             layer=layer,
-            results=expert_grads,
         )
         grad_middle, error, grad_heads, own, other, second_gain = attend_back_call(
-            grad_mixed, middle, gain_rows[layer, 1], upstream, output, low, probs, heads, keys_values
+            grad_mixed,
+            middle,
+            gain_rows[layer, 1],
+            upstream,
+            output,
+            low,
+            probs,
+            heads,
+            keys_values,
+            (to_x0, to_x1, to_y0, to_y1),
         )
         grad_kv = earlier_scatter(own, other)
         joined, upstream, upstream_low, first_gain = project_back_call(
@@ -1123,15 +1170,22 @@
             small = small.reshape(small_lines, -1, own_rows).transpose(1, 0, 2).reshape(-1, small_size)
             small = jnp.pad(small, ((0, 0), (0, SMALL * D - small_size)))
             small = small.reshape(4, LINE, 2, SMALL, D)
-        mine, other = dense_grads_call(joined, normed, low, error, small)
+        mine, others = dense_grads_call(joined, normed, low, error, small, got[0])
         if layer > 0:
-            received = swap_core(other)
-            dense_sums = dense_square_scatter(mine, received, got_x, got_y)
-            upstream_group = group_gather(upstream_low, (mine, other), (), (got_x, got_y), dense_sums[0])
-            dense_grads[layer] = line_scatter(dense_sums[2])
-        else:
-            dense_grads[0] = line_scatter(dense_square_scatter(mine, swap_core(other))[2])
-    result = stored[-1][6] + group_scatter(after(last_sums[0], joined), last_sums[1])
+            sums = dense_square_scatter(mine, others)
+            upstream_group = group_gather(upstream_low)
+            before_back = got[1]
+            before_scatter = sums[2]
+            dense_sums = sums
+            second_part = last_part
+    expert_grads = expert_grads_call(**second_part, earlier=mine)
+    sums = dense_square_scatter(mine, others, *got[1], *expert_grads)
+    expert_grads = expert_grads_call(**last_part, results=expert_grads, earlier=sums[1])
+    dense_grads = [line_scatter(sums[3]), line_scatter(after(dense_sums[3], *mine))]
+    last_sums = in_order(last_sums[0], jnp.concatenate(last_sums[1], axis=0))
+    result = stored[-1][6] + lax.psum_scatter(
+        last_sums, "cp", scatter_dimension=0, tiled=True
+    ).astype(WIDE)
     small = dense_grads[0][QROWS + OROWS :].reshape(-1)[:small_size]
     small = small.reshape(LAYERS, EXPERTS + 2, own_rows).transpose(0, 2, 1)
     return (

time: 1170 us -> 1110 us (0.949)
  waiting for transfers between devices: 508 us -> 318 us
  local copies, waits for them, and re-layouts: 67.7 us -> 112 us
  starting transfers between devices: 238 us -> 267 us
  other arithmetic: 62.7 us -> 86.9 us
  Pallas kernels: 275 us -> 289 us
  between operations: 3.52 us -> 16.4 us
    ppermute x44, waiting for transfers between devices: 281 us -> 130 us  [across(): return lax.ppermute(value, 'dp', [(i, i ^ flip) for i in range(4)])]
    ppermute x66 -> x60, waiting for transfers between devices: 185 us -> 158 us  [hop(): return lax.ppermute(value, 'cp', pairs)]
    unnamed x196 -> x204, local copies, waits for them, and re-layouts: 23.7 us -> 48.9 us
    ppermute x66 -> x60, starting transfers between devices: 159 us -> 182 us  [hop(): return lax.ppermute(value, 'cp', pairs)]
    ppermute x24 -> x32, waiting for transfers between devices: 14.6 us -> 1.18 us  [swap_core(): return lax.ppermute(value, 'cp', [(i, i ^ 1) for i in range(2 * LINE)])]
    pallas_call x15 -> x35, Pallas kernels: 200 us -> 205 us  [the longest x13 182 us: call(): pl.pallas_call(whole, grid=grid, out_shape=outs, in_specs=in_specs, out_s...]
  transfers between devices with their start and end apart: 146 -> 149, of which waited for: 68 -> 62; matrix products, arithmetic and copies ran while one was open for 9% -> 15% of each run, Pallas kernels for 16% -> 23%
where the time goes in v3:
time: 1110 us; the launch traced here: 1090 us
  waiting for transfers between devices  318 us (29%)
  Pallas kernels  289 us (26%)
  starting transfers between devices  267 us (24%)
  local copies, waits for them, and re-layouts  112 us (10%)
  other arithmetic  86.9 us (8%)
  between operations  16.4 us (1%)
    ppermute x60, starting transfers between devices, hop(): return lax.ppermute(value, 'cp', pairs)  182 us
    pallas_call x13, Pallas kernels, call(): pl.pallas_call(whole, grid=grid, out_shape=outs, in_specs=in_specs, out_s...  182 us
    ppermute x60, waiting for transfers between devices, hop(): return lax.ppermute(value, 'cp', pairs)  158 us
    ppermute x44, waiting for transfers between devices, across(): return lax.ppermute(value, 'dp', [(i, i ^ flip) for i in range(4)])  130 us
    pallas_call x6, Pallas kernels, expert_grads_call(): pl.pallas_call(body, out_shape=outs, input_output_aliases={first_kept + i...  83.4 us
    ppermute x44, starting transfers between devices, across(): return lax.ppermute(value, 'dp', [(i, i ^ flip) for i in range(4)])  49.4 us
    unnamed x204, local copies, waits for them, and re-layouts  48.9 us
    ppermute x12, starting transfers between devices, leap(): return lax.ppermute(value, 'cp', pairs)  30.6 us
  transfers between devices with their start and end apart: 149, of which 62 were waited for; matrix products, arithmetic and copies ran while one was open for 15% of the time, Pallas kernels for 23%

profile of v3, /device:TPU:0, one launch (start us, length us, event | category | flops | bytes accessed | tf_op | source)
XLA Modules:
  0.0 1092.1 jit_solution(7306396239803628161)
XLA Ops:
  37.9 7.3 collective-permute-done.4
  84.2 11.7 %collective-permute-done.24 = bf16[240,1536]{1,0:T(8,128)(2,1)} collective-permute-done((bf16[240,1536]{1,0:T(8,128)(2,1)}, bf16[240,1536]{1,0:T(8,128)(2,1)}, u32[]{:S(2)}, u32[]{:S(2)}) %collective-permute-start.24) | collective-permute-done | bytes 737312 | tf_op jit(solution)/shard_map/ppermute | solution.py:866
  107.1 13.1 %collective-permute-done.25 = bf16[240,1536]{1,0:T(8,128)(2,1)S(1)} collective-permute-done((bf16[240,1536]{1,0:T(8,128)(2,1)}, bf16[240,1536]{1,0:T(8,128)(2,1)S(1)}, u32[]{:S(2)}, u32[]{:S(2)}) %collective-permute-start.25) | collective-permute-done | bytes 737312 | tf_op jit(solution)/shard_map/ppermute | solution.py:866
  135.7 7.0 project.2
  142.7 8.3 collective-permute-start.19
  179.8 9.5 attend.2
  196.1 7.4 collective-permute-done.27
  235.8 17.3 %collective-permute-done.38.refs_14_.refs_1_.refs_15_ = bf16[576,1536]{1,0:T(8,128)(2,1)} collective-permute-done((bf16[576,1536]{1,0:T(8,128)(2,1)}, bf16[576,1536]{1,0:T(8,128)(2,1)}, u32[]{:S(2)}, u32[]{:S(2)}) %collective-permute-start.38) | collective-permute-done | bytes 1769504 | tf_op jit(solution)/shard_map/ppermute | solution.py:875
  262.1 25.9 %experts.2 = (bf16[512,1536]{1,0:T(8,128)(2,1)}, bf16[256,1536]{1,0:T(8,128)(2,1)}, bf16[256,1536]{1,0:T(8,128)(2,1)}, bf16[1024,3072]{1,0:T(8,128)(2,1)}, bf16[...) custom-call(s32[4]{0:T(128)} %pad_add_fusion.2.refs_0_.places, bf16[512,1536]{1,0:T(8,128)(2,1)} %bitcast.300, ...), custom_call_target="tpu_custom_call" | custom-call | bytes 29600000 | tf_op jit(solution)/shard_map/experts/pallas_call | solution.py:151
  300.1 9.9 collective-permute-start.44
  339.6 8.3 collective-permute-start.49
  361.5 7.0 project.3
  385.2 9.5 attend.3
  394.7 6.9 collective-permute-start.63
  420.6 16.6 %collective-permute-done.71.refs_3_.refs_10_.refs_11_ = bf16[384,1536]{1,0:T(8,128)(2,1)S(1)} collective-permute-done((bf16[384,1536]{1,0:T(8,128)(2,1)}, bf16[384,1536]{1,0:T(8,128)(2,1)S(1)}, u32[]{:S(2)}, u32[]{:S(2)}) %collective-permute-start.71) | collective-permute-done | bytes 1179680 | tf_op jit(solution)/shard_map/ppermute | solution.py:875
  446.0 6.8 collective-permute-done.68
  456.7 21.4 %collective-permute-done.74.refs_14_.refs_15_ = bf16[576,1536]{1,0:T(8,128)(2,1)} collective-permute-done((bf16[576,1536]{1,0:T(8,128)(2,1)}, bf16[576,1536]{1,0:T(8,128)(2,1)}, u32[]{:S(2)}, u32[]{:S(2)}) %collective-permute-start.74) | collective-permute-done | bytes 1769504 | tf_op jit(solution)/shard_map/ppermute | solution.py:875
  478.5 25.9 %experts.3 = (bf16[512,1536]{1,0:T(8,128)(2,1)}, bf16[256,1536]{1,0:T(8,128)(2,1)}, bf16[256,1536]{1,0:T(8,128)(2,1)}, bf16[1024,3072]{1,0:T(8,128)(2,1)}, bf16[...) custom-call(s32[4]{0:T(128)} %pad_add_fusion.2.refs_0_.places, bf16[512,1536]{1,0:T(8,128)(2,1)} %bitcast.306, ...), custom_call_target="tpu_custom_call" | custom-call | bytes 29600000 | tf_op jit(solution)/shard_map/experts/pallas_call | solution.py:151
  504.4 27.6 %experts_back.2 = (bf16[512,1536]{1,0:T(8,128)(2,1)}, bf16[256,1536]{1,0:T(8,128)(2,1)}, bf16[256,1536]{1,0:T(8,128)(2,1)}, bf16[1024,3072]{1,0:T(8,128)(2,1)}, bf16[1024,16]{1,0:T(8,128)(2,1)}) custom-call(s32[4]{0:T(128)} %pad_add_fusion.2.refs_0_.places, bf16[512,1536]{1,0:T(8,128)(2,1)} %bitcast.318, ...), custom_call_target="tpu_custom_call" | custom-call | bytes 29600000 | tf_op jit(solution)/shard_map/experts_back/pallas_call | solution.py:151
  532.6 10.8 expert_grads.6
  557.3 7.5 collective-permute-done.79
  565.8 14.5 %collective-permute-start.80 = (bf16[128,1536]{1,0:T(8,128)(2,1)S(1)}, bf16[128,1536]{1,0:T(8,128)(2,1)S(1)}, u32[]{:S(2)}, u32[]{:S(2)}) collective-permute-start(bf16[128,1536]{1,0:T(8,128)(2,1)S(1)} %get-tuple-element.235), channel_id=1, source_target_pairs={{0,2},{1,3},{2,4},{3,5},{8,10},{9,11},{10,12},{11,13},{16,18},{17,... | collective-permute-start | bytes 1179656 | tf_op jit(solution)/shard_map/ppermute | solution.py:866
  580.3 7.7 collective-permute-done.80
  592.0 6.9 collective-permute-start.85
  600.8 18.1 %expert_grads.7 = (bf16[576,1536]{1,0:T(8,128)(2,1)}, bf16[576,1536]{1,0:T(8,128)(2,1)}, bf16[576,1536]{1,0:T(8,128)(2,1)}, bf16[576,1536]{1,0:T(8,128)(2,1)}) custom-call(s32[4]{0:T(128)} %pad_add_fusion.2.refs_0_.places, bf16[512,1536]{1,0:T(8,128)(2,1)} %bitcast.308, bf16[512,1536]{1,0:T(8,128)(2,1)} %bitcast.91.refs_2_.rest_1_.rest_3_, ...), custom_call_target="tpu_custom_call" | custom-call | tf_op jit(solution)/shard_map/expert_grads/pallas_call | solution.py:631
  620.0 12.5 %attend_back.2 = (f32[128,1536]{1,0:T(8,128)}, bf16[128,1536]{1,0:T(8,128)(2,1)}, f32[12,128,128]{2,1,0:T(8,128)}, bf16[512,512]{1,0:T(8,128)(2,1)}, bf16[512,512]{1,0:T(8,128)(2,1)}, /*index=5*/f32[1,1536]{1,0:T(1,128)}) custom-call(s32[4]{0:T(128)} %pad_add_fusion.2.refs_0_.places, f32[128,1536]{1,0:T(8,128)} %fusion.20.refs_1_, ...), custom_call_target="tpu_custom_call" | custom-call | tf_op jit(solution)/shard_map/attend_back/pallas_call | solution.py:151
  639.8 6.2 collective-permute-done.90
  651.6 6.8 project_back.2
  664.9 7.5 collective-permute-done.91
  682.7 11.2 %dense_grads.2 = (bf16[4,112,1536]{2,1,0:T(8,128)(2,1)}, bf16[4,112,1536]{2,1,0:T(8,128)(2,1)}, bf16[4,112,1536]{2,1,0:T(8,128)(2,1)}, bf16[4,112,1536]{2,1,0:T(...) custom-call(s32[4]{0:T(128)} %pad_add_fusion.2.refs_0_.places, ...), custom_call_target="tpu_custom_call" | custom-call | tf_op jit(solution)/shard_map/dense_grads/pallas_call | solution.py:846
  699.0 13.4 %collective-permute-done.96 = bf16[128,1536]{1,0:T(8,128)(2,1)S(1)} collective-permute-done((bf16[128,1536]{1,0:T(8,128)(2,1)}, bf16[128,1536]{1,0:T(8,128)(2,1)S(1)}, u32[]{:S(2)}, u32[]{:S(2)}) %collective-permute-start.96) | collective-permute-done | bytes 393248 | tf_op jit(solution)/shard_map/ppermute | solution.py:866
  724.3 10.9 collective-permute-done.104
  745.2 27.6 %experts_back.3 = (bf16[512,1536]{1,0:T(8,128)(2,1)}, bf16[256,1536]{1,0:T(8,128)(2,1)}, bf16[256,1536]{1,0:T(8,128)(2,1)}, bf16[1024,3072]{1,0:T(8,128)(2,1)}, bf16[1024,16]{1,0:T(8,128)(2,1)}) custom-call(s32[4]{0:T(128)} %pad_add_fusion.2.refs_0_.places, bf16[512,1536]{1,0:T(8,128)(2,1)} %bitcast.322, bf16[512,1536]{1,0:T(8,128)(2,1)} %bitcast.326, ...), custom_call_target="tpu_custom_call" | custom-call | bytes 29600000 | tf_op jit(solution)/shard_map/experts_back/pallas_call | solution.py:151
  774.6 10.8 expert_grads.8
  796.4 7.5 collective-permute-done.111
  804.8 17.0 %collective-permute-start.112 = (bf16[128,1536]{1,0:T(8,128)(2,1)S(1)}, bf16[128,1536]{1,0:T(8,128)(2,1)S(1)}, u32[]{:S(2)}, u32[]{:S(2)}) collective-permute-start(bf16[128,1536]{1,0:T(8,128)(2,1)S(1)} %get-tuple-element.231), channel_id=1, source_target_pairs={{0,2},{1,3},{2,4},{3,5},{8,10},{9,11},{10,12},{11,13},{16,18},{17,... | collective-permute-start | bytes 1179656 | tf_op jit(solution)/shard_map/ppermute | solution.py:866
  844.0 18.2 %expert_grads.9 = (bf16[576,1536]{1,0:T(8,128)(2,1)}, bf16[576,1536]{1,0:T(8,128)(2,1)}, bf16[576,1536]{1,0:T(8,128)(2,1)}, bf16[576,1536]{1,0:T(8,128)(2,1)}) custom-call(s32[4]{0:T(128)} %pad_add_fusion.2.refs_0_.places, bf16[512,1536]{1,0:T(8,128)(2,1)} %bitcast.302, bf16[512,1536]{1,0:T(8,128)(2,1)} %bitcast.314, bf16[512,1536]{1,0:T(8,128)(2,1)} %bitcast.303, ...), custom_call_target="tpu_custom_call" | custom-call | tf_op jit(solution)/shard_map/expert_grads/pallas_call | solution.py:631
  863.1 12.7 %attend_back.3 = (f32[128,1536]{1,0:T(8,128)}, bf16[128,1536]{1,0:T(8,128)(2,1)}, f32[12,128,128]{2,1,0:T(8,128)}, bf16[512,512]{1,0:T(8,128)(2,1)}, bf16[512,512]{1,0:T(8,128)(2,1)}, /*index=5*/f32[1,1536]{1,0:T(1,128)}) custom-call(s32[4]{0:T(128)} %pad_add_fusion.2.refs_0_.places, f32[128,1536]{1,0:T(8,128)} %fusion.15.refs_1_, ...), custom_call_target="tpu_custom_call" | custom-call | tf_op jit(solution)/shard_map/attend_back/pallas_call | solution.py:151
  888.0 6.7 collective-permute-done.122
  904.7 6.8 project_back.3
  920.3 12.1 %dense_grads.3 = (bf16[4,128,1536]{2,1,0:T(8,128)(2,1)}, bf16[4,128,1536]{2,1,0:T(8,128)(2,1)}, bf16[4,128,1536]{2,1,0:T(8,128)(2,1)}, bf16[4,128,1536]{2,1,0:T(...) custom-call(s32[4]{0:T(128)} %pad_add_fusion.2.refs_0_.places, ...), custom_call_target="tpu_custom_call" | custom-call | tf_op jit(solution)/shard_map/dense_grads/pallas_call | solution.py:846
  940.8 6.2 collective-permute-start.142
  947.0 12.7 %expert_grads.10 = (f32[2,2,384,1536]{3,2,1,0:T(8,128)}, f32[2,2,192,1536]{3,2,1,0:T(8,128)}) custom-call(s32[4]{0:T(128)} %pad_add_fusion.2.refs_0_.places, bf16[512,1536]{1,0:T(8,128)(2,1)} %bitcast.310, bf16[512,1536]{1,0:T(8,128)(2,1)} %bitcast.91.refs_2_.rest_1_.rest_3_, ...), custom_call_target="tpu_custom_call" | custom-call | bytes 14800000 | tf_op jit(solution)/shard_map/expert_grads/pallas_call | solution.py:631
  963.0 10.6 collective-permute-done.128.refs_1_.rest_9_
  982.8 12.9 %collective-permute-done.133 = bf16[2,128,1536]{2,1,0:T(8,128)(2,1)S(1)} collective-permute-done((bf16[2,128,1536]{2,1,0:T(8,128)(2,1)S(1)}, bf16[2,128,1536]{2,1,0:T(8,128)(2,1)S(1)}, u32[]{:S(2)}, u32[]{:S(2)}) %collective-permute-start.133) | collective-permute-done | bytes 786464 | tf_op jit(solution)/shard_map/ppermute | solution.py:875
  1003.5 6.5 collective-permute-start.143
  1022.6 10.1 collective-permute-done.134
  1067.2 12.8 %expert_grads.11 = (f32[2,2,384,1536]{3,2,1,0:T(8,128)}, f32[2,2,192,1536]{3,2,1,0:T(8,128)}) custom-call(s32[4]{0:T(128)} %pad_add_fusion.2.refs_0_.places, bf16[512,1536]{1,0:T(8,128)(2,1)} %bitcast.304, bf16[512,1536]{1,0:T(8,128)(2,1)} %bitcast.316, ...), custom_call_target="tpu_custom_call", output_to_operand_aliasing={{0}: (12, {}), {1}: (13, {})} | custom-call | bytes 14800000 | tf_op jit(solution)/shard_map/expert_grads/pallas_call | solution.py:631
  (672 shorter events, 503.0 us)
Async XLA Ops:
  7.2 1002.9 %reduce-scatter.2.cloned.1.call-start = ((), (), s32[]{:S(2)}) async-start(), calls=%async_computation.1 | async-start | bytes 3538944 | tf_op jit(solution)/shard_map/reduce_scatter | solution.py:1186
  24.6 37.4 %collective-permute-start.6 = (bf16[384,1536]{1,0:T(8,128)(2,1)S(1)}, bf16[384,1536]{1,0:T(8,128)(2,1)S(1)}, u32[]{:S(2)}, u32[]{:S(2)}) collective-permute-start(bf16[384,1536]{1,0:T(8,128)(2,1)S(1)} %get-tuple-element.220.refs_5_.refs_6_), channel_id=1, source_target_pairs={{0,8},{8,0},{16,24},{24,16},{1,9},{9,1},{17,25},{25,17},{2,10},{10... | collective-permute-start | bytes 3538952 | tf_op jit(solution)/shard_map/ppermute | solution.py:875
  26.1 35.9 %collective-permute-start.7 = (bf16[384,1536]{1,0:T(8,128)(2,1)S(1)}, bf16[384,1536]{1,0:T(8,128)(2,1)S(1)}, u32[]{:S(2)}, u32[]{:S(2)}) collective-permute-start(bf16[384,1536]{1,0:T(8,128)(2,1)S(1)} %get-tuple-element.220.refs_5_.refs_6_), channel_id=1, source_target_pairs={{0,16},{8,24},{16,0},{24,8},{1,17},{9,25},{17,1},{25,9},{2,18},{10... | collective-permute-start | bytes 3538952 | tf_op jit(solution)/shard_map/ppermute | solution.py:875
  64.1 33.4 %collective-permute-start.9 = (bf16[4,128,1536]{2,1,0:T(8,128)(2,1)}, bf16[4,128,1536]{2,1,0:T(8,128)(2,1)S(1)}, u32[]{:S(2)}, u32[]{:S(2)}) collective-permute-start(bf16[4,128,1536]{2,1,0:T(8,128)(2,1)} %after.20.refs_1_.refs_4_.refs_8_.refs_10_.refs_7_), channel_id=1, source_target_pairs={{0,8},{8,0},{16,24},{24,16},{1,9},{9,1},{17,25},{25,17},{2,10},{10... | collective-permute-start | bytes 4718600 | tf_op jit(solution)/shard_map/ppermute | solution.py:875
  65.9 35.8 %collective-permute-start.11 = (bf16[4,128,1536]{2,1,0:T(8,128)(2,1)}, bf16[4,128,1536]{2,1,0:T(8,128)(2,1)}, u32[]{:S(2)}, u32[]{:S(2)}) collective-permute-start(bf16[4,128,1536]{2,1,0:T(8,128)(2,1)} %after.20.refs_1_.refs_4_.refs_8_.refs_10_.refs_7_), channel_id=1, source_target_pairs={{0,16},{8,24},{16,0},{24,8},{1,17},{9,25},{17,1},{25,9},{2,18},{10... | collective-permute-start | bytes 4718600 | tf_op jit(solution)/shard_map/ppermute | solution.py:875
  84.2 42.6 %collective-permute-start.8 = (bf16[4,128,1536]{2,1,0:T(8,128)(2,1)S(1)}, bf16[4,128,1536]{2,1,0:T(8,128)(2,1)}, u32[]{:S(2)}, u32[]{:S(2)}) collective-permute-start(bf16[4,128,1536]{2,1,0:T(8,128)(2,1)S(1)} %copy-done), channel_id=1, source_target_pairs={{0,1},{1,0},{2,3},{3,2},{4,5},{5,4},{6,7},{7,6},{8,9},{9,8},{10,11... | collective-permute-start | bytes 4718600 | tf_op jit(solution)/shard_map/ppermute | solution.py:860
  126.9 28.3 %collective-permute-start.26 = (bf16[240,1536]{1,0:T(8,128)(2,1)}, bf16[240,1536]{1,0:T(8,128)(2,1)}, u32[]{:S(2)}, u32[]{:S(2)}) collective-permute-start(bf16[240,1536]{1,0:T(8,128)(2,1)} %copy-done.65), channel_id=1, source_target_pairs={{2,0},{3,1},{10,8},{11,9},{18,16},{19,17},{26,24},{27,25}} | collective-permute-start | bytes 2211848 | tf_op jit(solution)/shard_map/ppermute | solution.py:866
  128.2 66.5 %collective-permute-start.36 = (bf16[2,192,1536]{2,1,0:T(8,128)(2,1)}, bf16[2,192,1536]{2,1,0:T(8,128)(2,1)S(1)}, u32[]{:S(2)}, u32[]{:S(2)}) collective-permute-start(bf16[2,192,1536]{2,1,0:T(8,128)(2,1)} %after.23.refs_11_.refs_12_), channel_id=1, source_target_pairs={{0,8},{8,0},{16,24},{24,16},{1,9},{9,1},{17,25},{25,17},{2,10},{10... | collective-permute-start | bytes 3538952 | tf_op jit(solution)/shard_map/ppermute | solution.py:875
  157.2 47.7 %collective-permute-start.37 = (bf16[2,192,1536]{2,1,0:T(8,128)(2,1)S(1)}, bf16[2,192,1536]{2,1,0:T(8,128)(2,1)}, u32[]{:S(2)}, u32[]{:S(2)}) collective-permute-start(bf16[2,192,1536]{2,1,0:T(8,128)(2,1)S(1)} %copy-done.22), channel_id=1, source_target_pairs={{0,16},{8,24},{16,0},{24,8},{1,17},{9,25},{17,1},{25,9},{2,18},{10... | collective-permute-start | bytes 3538952 | tf_op jit(solution)/shard_map/ppermute | solution.py:875
  164.4 48.8 %collective-permute-start.34 = (bf16[384,1536]{1,0:T(8,128)(2,1)}, bf16[384,1536]{1,0:T(8,128)(2,1)}, u32[]{:S(2)}, u32[]{:S(2)}) collective-permute-start(bf16[384,1536]{1,0:T(8,128)(2,1)} %after.22.refs_8_.refs_9_), channel_id=1, source_target_pairs={{0,8},{8,0},{16,24},{24,16},{1,9},{9,1},{17,25},{25,17},{2,10},{10... | collective-permute-start | bytes 3538952 | tf_op jit(solution)/shard_map/ppermute | solution.py:875
  165.2 46.6 %collective-permute-start.35 = (bf16[384,1536]{1,0:T(8,128)(2,1)}, bf16[384,1536]{1,0:T(8,128)(2,1)S(1)}, u32[]{:S(2)}, u32[]{:S(2)}) collective-permute-start(bf16[384,1536]{1,0:T(8,128)(2,1)} %after.22.refs_8_.refs_9_), channel_id=1, source_target_pairs={{0,16},{8,24},{16,0},{24,8},{1,17},{9,25},{17,1},{25,9},{2,18},{10... | collective-permute-start | bytes 3538952 | tf_op jit(solution)/shard_map/ppermute | solution.py:875
  213.4 39.6 %collective-permute-start.38 = (bf16[576,1536]{1,0:T(8,128)(2,1)}, bf16[576,1536]{1,0:T(8,128)(2,1)}, u32[]{:S(2)}, u32[]{:S(2)}) collective-permute-start(bf16[576,1536]{1,0:T(8,128)(2,1)} %get-tuple-element.117), channel_id=1, source_target_pairs={{0,16},{8,24},{16,0},{24,8},{1,17},{9,25},{17,1},{25,9},{2,18},{10... | collective-permute-start | bytes 5308424 | tf_op jit(solution)/shard_map/ppermute | solution.py:875
  214.8 39.3 %collective-permute-start.39 = (bf16[576,1536]{1,0:T(8,128)(2,1)}, bf16[576,1536]{1,0:T(8,128)(2,1)}, u32[]{:S(2)}, u32[]{:S(2)}) collective-permute-start(bf16[576,1536]{1,0:T(8,128)(2,1)} %get-tuple-element.118), channel_id=1, source_target_pairs={{0,8},{8,0},{16,24},{24,16},{1,9},{9,1},{17,25},{25,17},{2,10},{10... | collective-permute-start | bytes 5308424 | tf_op jit(solution)/shard_map/ppermute | solution.py:875
  254.1 33.9 %collective-permute-start.40 = (bf16[4,112,1536]{2,1,0:T(8,128)(2,1)}, bf16[4,112,1536]{2,1,0:T(8,128)(2,1)}, u32[]{:S(2)}, u32[]{:S(2)}) collective-permute-start(bf16[4,112,1536]{2,1,0:T(8,128)(2,1)} %after.25.refs_4_.refs_8_.refs_10_.refs_7_), channel_id=1, source_target_pairs={{0,8},{8,0},{16,24},{24,16},{1,9},{9,1},{17,25},{25,17},{2,10},{10... | collective-permute-start | bytes 4128776 | tf_op jit(solution)/shard_map/ppermute | solution.py:875
  255.6 32.4 %collective-permute-start.41 = (bf16[4,112,1536]{2,1,0:T(8,128)(2,1)}, bf16[4,112,1536]{2,1,0:T(8,128)(2,1)}, u32[]{:S(2)}, u32[]{:S(2)}) collective-permute-start(bf16[4,112,1536]{2,1,0:T(8,128)(2,1)} %after.25.refs_4_.refs_8_.refs_10_.refs_7_), channel_id=1, source_target_pairs={{0,16},{8,24},{16,0},{24,8},{1,17},{9,25},{17,1},{25,9},{2,18},{10... | collective-permute-start | bytes 4128776 | tf_op jit(solution)/shard_map/ppermute | solution.py:875
  311.0 28.6 %collective-permute-start.57 = (bf16[384,1536]{1,0:T(8,128)(2,1)}, bf16[384,1536]{1,0:T(8,128)(2,1)S(1)}, u32[]{:S(2)}, u32[]{:S(2)}) collective-permute-start(bf16[384,1536]{1,0:T(8,128)(2,1)} %after.28.refs_5_.refs_6_), channel_id=1, source_target_pairs={{0,8},{8,0},{16,24},{24,16},{1,9},{9,1},{17,25},{25,17},{2,10},{10... | collective-permute-start | bytes 3538952 | tf_op jit(solution)/shard_map/ppermute | solution.py:875
  332.1 28.4 %collective-permute-start.53 = (bf16[4,112,1536]{2,1,0:T(8,128)(2,1)}, bf16[4,112,1536]{2,1,0:T(8,128)(2,1)}, u32[]{:S(2)}, u32[]{:S(2)}) collective-permute-start(bf16[4,112,1536]{2,1,0:T(8,128)(2,1)} %collective-permute-done.40.refs_2_.refs_6_.refs_10_.refs_12_.refs_9_), channel_id=1, source_target_pairs={{0,1},{1,0},{2,3},{3,2},{4,5},{5,4},{6,7},{7,6},{8,9},{9,8},{10,11... | collective-permute-start | bytes 4128776 | tf_op jit(solution)/shard_map/ppermute | solution.py:860
  332.1 28.4 %collective-permute-start.54 = (bf16[4,112,1536]{2,1,0:T(8,128)(2,1)}, bf16[4,112,1536]{2,1,0:T(8,128)(2,1)}, u32[]{:S(2)}, u32[]{:S(2)}) collective-permute-start(bf16[4,112,1536]{2,1,0:T(8,128)(2,1)} %collective-permute-done.41.refs_3_.refs_8_.refs_12_.refs_14_.refs_11_), channel_id=1, source_target_pairs={{0,1},{1,0},{2,3},{3,2},{4,5},{5,4},{6,7},{7,6},{8,9},{9,8},{10,11... | collective-permute-start | bytes 4128776 | tf_op jit(solution)/shard_map/ppermute | solution.py:860
  356.5 59.6 %collective-permute-start.72 = (bf16[2,192,1536]{2,1,0:T(8,128)(2,1)}, bf16[2,192,1536]{2,1,0:T(8,128)(2,1)S(1)}, u32[]{:S(2)}, u32[]{:S(2)}) collective-permute-start(bf16[2,192,1536]{2,1,0:T(8,128)(2,1)} %after.30.refs_11_.refs_12_), channel_id=1, source_target_pairs={{0,8},{8,0},{16,24},{24,16},{1,9},{9,1},{17,25},{25,17},{2,10},{10... | collective-permute-start | bytes 3538952 | tf_op jit(solution)/shard_map/ppermute | solution.py:875
  382.5 34.9 %collective-permute-start.73 = (bf16[2,192,1536]{2,1,0:T(8,128)(2,1)S(1)}, bf16[2,192,1536]{2,1,0:T(8,128)(2,1)}, u32[]{:S(2)}, u32[]{:S(2)}) collective-permute-start(bf16[2,192,1536]{2,1,0:T(8,128)(2,1)S(1)} %copy-done.18), channel_id=1, source_target_pairs={{0,16},{8,24},{16,0},{24,8},{1,17},{9,25},{17,1},{25,9},{2,18},{10... | collective-permute-start | bytes 3538952 | tf_op jit(solution)/shard_map/ppermute | solution.py:875
  402.9 35.9 %collective-permute-start.70 = (bf16[384,1536]{1,0:T(8,128)(2,1)}, bf16[384,1536]{1,0:T(8,128)(2,1)}, u32[]{:S(2)}, u32[]{:S(2)}) collective-permute-start(bf16[384,1536]{1,0:T(8,128)(2,1)} %after.29.refs_8_.refs_9_), channel_id=1, source_target_pairs={{0,8},{8,0},{16,24},{24,16},{1,9},{9,1},{17,25},{25,17},{2,10},{10... | collective-permute-start | bytes 3538952 | tf_op jit(solution)/shard_map/ppermute | solution.py:875
  438.8 39.2 %collective-permute-start.74 = (bf16[576,1536]{1,0:T(8,128)(2,1)}, bf16[576,1536]{1,0:T(8,128)(2,1)}, u32[]{:S(2)}, u32[]{:S(2)}) collective-permute-start(bf16[576,1536]{1,0:T(8,128)(2,1)} %get-tuple-element.130), channel_id=1, source_target_pairs={{0,16},{8,24},{16,0},{24,8},{1,17},{9,25},{17,1},{25,9},{2,18},{10... | collective-permute-start | bytes 5308424 | tf_op jit(solution)/shard_map/ppermute | solution.py:875
  439.5 38.9 %collective-permute-start.75 = (bf16[576,1536]{1,0:T(8,128)(2,1)}, bf16[576,1536]{1,0:T(8,128)(2,1)}, u32[]{:S(2)}, u32[]{:S(2)}) collective-permute-start(bf16[576,1536]{1,0:T(8,128)(2,1)} %get-tuple-element.131), channel_id=1, source_target_pairs={{0,8},{8,0},{16,24},{24,16},{1,9},{9,1},{17,25},{25,17},{2,10},{10... | collective-permute-start | bytes 5308424 | tf_op jit(solution)/shard_map/ppermute | solution.py:875
  454.8 49.6 %collective-permute-start.76 = (bf16[4,128,1536]{2,1,0:T(8,128)(2,1)S(1)}, bf16[4,128,1536]{2,1,0:T(8,128)(2,1)}, u32[]{:S(2)}, u32[]{:S(2)}) collective-permute-start(bf16[4,128,1536]{2,1,0:T(8,128)(2,1)S(1)} %copy-done.7), channel_id=1, source_target_pairs={{0,1},{1,0},{2,3},{3,2},{4,5},{5,4},{6,7},{7,6},{8,9},{9,8},{10,11... | collective-permute-start | bytes 4718600 | tf_op jit(solution)/shard_map/ppermute | solution.py:860
  548.6 40.9 %collective-permute-start.83 = (bf16[576,1536]{1,0:T(8,128)(2,1)}, bf16[576,1536]{1,0:T(8,128)(2,1)S(1)}, u32[]{:S(2)}, u32[]{:S(2)}) collective-permute-start(bf16[576,1536]{1,0:T(8,128)(2,1)} %get-tuple-element.142.refs_2_), channel_id=1, source_target_pairs={{0,8},{8,0},{16,24},{24,16},{1,9},{9,1},{17,25},{25,17},{2,10},{10... | collective-permute-start | bytes 5308424 | tf_op jit(solution)/shard_map/ppermute | solution.py:875
  549.4 40.6 %collective-permute-start.84 = (bf16[576,1536]{1,0:T(8,128)(2,1)}, bf16[576,1536]{1,0:T(8,128)(2,1)}, u32[]{:S(2)}, u32[]{:S(2)}) collective-permute-start(bf16[576,1536]{1,0:T(8,128)(2,1)} %get-tuple-element.143.refs_3_), channel_id=1, source_target_pairs={{0,16},{8,24},{16,0},{24,8},{1,17},{9,25},{17,1},{25,9},{2,18},{10... | collective-permute-start | bytes 5308424 | tf_op jit(solution)/shard_map/ppermute | solution.py:875
  632.6 47.9 %collective-permute-start.100 = (bf16[576,1536]{1,0:T(8,128)(2,1)}, bf16[576,1536]{1,0:T(8,128)(2,1)S(1)}, u32[]{:S(2)}, u32[]{:S(2)}) collective-permute-start(bf16[576,1536]{1,0:T(8,128)(2,1)} %get-tuple-element.150.refs_20_), channel_id=1, source_target_pairs={{0,8},{8,0},{16,24},{24,16},{1,9},{9,1},{17,25},{25,17},{2,10},{10... | collective-permute-start | bytes 5308424 | tf_op jit(solution)/shard_map/ppermute | solution.py:875
  633.4 48.1 %collective-permute-start.101 = (bf16[576,1536]{1,0:T(8,128)(2,1)}, bf16[576,1536]{1,0:T(8,128)(2,1)S(1)}, u32[]{:S(2)}, u32[]{:S(2)}) collective-permute-start(bf16[576,1536]{1,0:T(8,128)(2,1)} %get-tuple-element.152.refs_22_), channel_id=1, source_target_pairs={{0,16},{8,24},{16,0},{24,8},{1,17},{9,25},{17,1},{25,9},{2,18},{10... | collective-permute-start | bytes 5308424 | tf_op jit(solution)/shard_map/ppermute | solution.py:875
  679.4 64.6 %collective-permute-start.98 = (bf16[576,1536]{1,0:T(8,128)(2,1)}, bf16[576,1536]{1,0:T(8,128)(2,1)}, u32[]{:S(2)}, u32[]{:S(2)}) collective-permute-start(bf16[576,1536]{1,0:T(8,128)(2,1)} %get-tuple-element.151.refs_21_), channel_id=1, source_target_pairs={{0,8},{8,0},{16,24},{24,16},{1,9},{9,1},{17,25},{25,17},{2,10},{10... | collective-permute-start | bytes 5308424 | tf_op jit(solution)/shard_map/ppermute | solution.py:875
  680.4 63.6 %collective-permute-start.99 = (bf16[576,1536]{1,0:T(8,128)(2,1)}, bf16[576,1536]{1,0:T(8,128)(2,1)}, u32[]{:S(2)}, u32[]{:S(2)}) collective-permute-start(bf16[576,1536]{1,0:T(8,128)(2,1)} %get-tuple-element.153.refs_23_), channel_id=1, source_target_pairs={{0,16},{8,24},{16,0},{24,8},{1,17},{9,25},{17,1},{25,9},{2,18},{10... | collective-permute-start | bytes 5308424 | tf_op jit(solution)/shard_map/ppermute | solution.py:875
  712.6 31.4 %collective-permute-start.97 = (bf16[4,128,1536]{2,1,0:T(8,128)(2,1)S(1)}, bf16[4,128,1536]{2,1,0:T(8,128)(2,1)S(1)}, u32[]{:S(2)}, u32[]{:S(2)}) collective-permute-start(bf16[4,128,1536]{2,1,0:T(8,128)(2,1)S(1)} %constant_dynamic-slice_fusion.1), channel_id=1, source_target_pairs={{0,1},{1,0},{2,3},{3,2},{4,5},{5,4},{6,7},{7,6},{8,9},{9,8},{10,11... | collective-permute-start | bytes 4718600 | tf_op jit(solution)/shard_map/ppermute | solution.py:860
  736.6 36.2 %collective-permute-start.105 = (bf16[4,112,1536]{2,1,0:T(8,128)(2,1)}, bf16[4,112,1536]{2,1,0:T(8,128)(2,1)}, u32[]{:S(2)}, u32[]{:S(2)}) collective-permute-start(bf16[4,112,1536]{2,1,0:T(8,128)(2,1)} %pad_maximum_fusion.7), channel_id=1, source_target_pairs={{0,8},{8,0},{16,24},{24,16},{1,9},{9,1},{17,25},{25,17},{2,10},{10... | collective-permute-start | bytes 4128776 | tf_op jit(solution)/shard_map/ppermute | solution.py:875
  743.0 31.1 %collective-permute-start.108 = (bf16[4,112,1536]{2,1,0:T(8,128)(2,1)}, bf16[4,112,1536]{2,1,0:T(8,128)(2,1)}, u32[]{:S(2)}, u32[]{:S(2)}) collective-permute-start(bf16[4,112,1536]{2,1,0:T(8,128)(2,1)} %pad_maximum_fusion.8), channel_id=1, source_target_pairs={{0,16},{8,24},{16,0},{24,8},{1,17},{9,25},{17,1},{25,9},{2,18},{10... | collective-permute-start | bytes 4128776 | tf_op jit(solution)/shard_map/ppermute | solution.py:875
  790.6 40.8 %collective-permute-start.115 = (bf16[576,1536]{1,0:T(8,128)(2,1)}, bf16[576,1536]{1,0:T(8,128)(2,1)S(1)}, u32[]{:S(2)}, u32[]{:S(2)}) collective-permute-start(bf16[576,1536]{1,0:T(8,128)(2,1)} %get-tuple-element.177.refs_2_), channel_id=1, source_target_pairs={{0,8},{8,0},{16,24},{24,16},{1,9},{9,1},{17,25},{25,17},{2,10},{10... | collective-permute-start | bytes 5308424 | tf_op jit(solution)/shard_map/ppermute | solution.py:875
  791.7 40.6 %collective-permute-start.116 = (bf16[576,1536]{1,0:T(8,128)(2,1)}, bf16[576,1536]{1,0:T(8,128)(2,1)}, u32[]{:S(2)}, u32[]{:S(2)}) collective-permute-start(bf16[576,1536]{1,0:T(8,128)(2,1)} %get-tuple-element.178.refs_3_), channel_id=1, source_target_pairs={{0,16},{8,24},{16,0},{24,8},{1,17},{9,25},{17,1},{25,9},{2,18},{10... | collective-permute-start | bytes 5308424 | tf_op jit(solution)/shard_map/ppermute | solution.py:875
  832.6 29.5 %collective-permute-start.118 = (bf16[128,1536]{1,0:T(8,128)(2,1)}, bf16[128,1536]{1,0:T(8,128)(2,1)S(1)}, u32[]{:S(2)}, u32[]{:S(2)}) collective-permute-start(bf16[128,1536]{1,0:T(8,128)(2,1)} %get-tuple-element.182), channel_id=1, source_target_pairs={{2,0},{3,1},{4,2},{5,3},{6,4},{7,5},{10,8},{11,9},{12,10},{13,11},... | collective-permute-start | bytes 1179656 | tf_op jit(solution)/shard_map/ppermute | solution.py:866
  833.9 28.2 %collective-permute-start.117 = (bf16[128,1536]{1,0:T(8,128)(2,1)}, bf16[128,1536]{1,0:T(8,128)(2,1)S(1)}, u32[]{:S(2)}, u32[]{:S(2)}) collective-permute-start(bf16[128,1536]{1,0:T(8,128)(2,1)} %get-tuple-element.181), channel_id=1, source_target_pairs={{0,2},{1,3},{2,4},{3,5},{4,6},{5,7},{8,10},{9,11},{10,12},{11,13},... | collective-permute-start | bytes 1179656 | tf_op jit(solution)/shard_map/ppermute | solution.py:866
  877.9 41.2 %collective-permute-start.123 = (bf16[576,1536]{1,0:T(8,128)(2,1)}, bf16[576,1536]{1,0:T(8,128)(2,1)S(1)}, u32[]{:S(2)}, u32[]{:S(2)}) collective-permute-start(bf16[576,1536]{1,0:T(8,128)(2,1)} %get-tuple-element.186.refs_20_), channel_id=1, source_target_pairs={{0,8},{8,0},{16,24},{24,16},{1,9},{9,1},{17,25},{25,17},{2,10},{10... | collective-permute-start | bytes 5308424 | tf_op jit(solution)/shard_map/ppermute | solution.py:875
  878.9 41.0 %collective-permute-start.124 = (bf16[576,1536]{1,0:T(8,128)(2,1)}, bf16[576,1536]{1,0:T(8,128)(2,1)}, u32[]{:S(2)}, u32[]{:S(2)}) collective-permute-start(bf16[576,1536]{1,0:T(8,128)(2,1)} %get-tuple-element.188.refs_22_), channel_id=1, source_target_pairs={{0,16},{8,24},{16,0},{24,8},{1,17},{9,25},{17,1},{25,9},{2,18},{10... | collective-permute-start | bytes 5308424 | tf_op jit(solution)/shard_map/ppermute | solution.py:875
  882.6 52.2 %collective-permute-start.141 = (bf16[4,112,1536]{2,1,0:T(8,128)(2,1)}, bf16[4,112,1536]{2,1,0:T(8,128)(2,1)}, u32[]{:S(2)}, u32[]{:S(2)}) collective-permute-start(bf16[4,112,1536]{2,1,0:T(8,128)(2,1)} %get-tuple-element.215), channel_id=1, source_target_pairs={{0,1},{1,0},{2,3},{3,2},{4,5},{5,4},{6,7},{7,6},{8,9},{9,8},{10,11... | collective-permute-start | bytes 4128776 | tf_op jit(solution)/shard_map/ppermute | solution.py:860
  932.4 41.2 %collective-permute-start.128 = (bf16[576,1536]{1,0:T(8,128)(2,1)}, bf16[576,1536]{1,0:T(8,128)(2,1)S(1)}, u32[]{:S(2)}, u32[]{:S(2)}) collective-permute-start(bf16[576,1536]{1,0:T(8,128)(2,1)} %get-tuple-element.187.refs_21_), channel_id=1, source_target_pairs={{0,8},{8,0},{16,24},{24,16},{1,9},{9,1},{17,25},{25,17},{2,10},{10... | collective-permute-start | bytes 5308424 | tf_op jit(solution)/shard_map/ppermute | solution.py:875
  933.4 41.0 %collective-permute-start.129 = (bf16[576,1536]{1,0:T(8,128)(2,1)}, bf16[576,1536]{1,0:T(8,128)(2,1)}, u32[]{:S(2)}, u32[]{:S(2)}) collective-permute-start(bf16[576,1536]{1,0:T(8,128)(2,1)} %get-tuple-element.189.refs_23_), channel_id=1, source_target_pairs={{0,16},{8,24},{16,0},{24,8},{1,17},{9,25},{17,1},{25,9},{2,18},{10... | collective-permute-start | bytes 5308424 | tf_op jit(solution)/shard_map/ppermute | solution.py:875
  934.8 42.7 %collective-permute-start.132 = (bf16[4,128,1536]{2,1,0:T(8,128)(2,1)}, bf16[4,128,1536]{2,1,0:T(8,128)(2,1)}, u32[]{:S(2)}, u32[]{:S(2)}) collective-permute-start(bf16[4,128,1536]{2,1,0:T(8,128)(2,1)} %get-tuple-element.213), channel_id=1, source_target_pairs={{0,1},{1,0},{2,3},{3,2},{4,5},{5,4},{6,7},{7,6},{8,9},{9,8},{10,11... | collective-permute-start | bytes 4718600 | tf_op jit(solution)/shard_map/ppermute | solution.py:860
  940.8 60.9 %collective-permute-start.142 = (bf16[112,1536]{1,0:T(8,128)(2,1)}, bf16[112,1536]{1,0:T(8,128)(2,1)}, u32[]{:S(2)}, u32[]{:S(2)}) collective-permute-start(bf16[112,1536]{1,0:T(8,128)(2,1)} %get-tuple-element.246), channel_id=1, source_target_pairs={{0,2},{1,3},{8,10},{9,11},{16,18},{17,19},{24,26},{25,27}} | collective-permute-start | bytes 1032200 | tf_op jit(solution)/shard_map/ppermute | solution.py:866
  973.6 48.9 %collective-permute-start.125 = (bf16[4,128,1536]{2,1,0:T(8,128)(2,1)}, bf16[4,128,1536]{2,1,0:T(8,128)(2,1)}, u32[]{:S(2)}, u32[]{:S(2)}) collective-permute-start(bf16[4,128,1536]{2,1,0:T(8,128)(2,1)} %get-tuple-element.205), channel_id=1, source_target_pairs={{0,1},{1,0},{2,3},{3,2},{4,5},{5,4},{6,7},{7,6},{8,9},{9,8},{10,11... | collective-permute-start | bytes 4718600 | tf_op jit(solution)/shard_map/ppermute | solution.py:860
  997.2 35.5 %collective-permute-start.134 = (bf16[4,128,1536]{2,1,0:T(8,128)(2,1)}, bf16[4,128,1536]{2,1,0:T(8,128)(2,1)}, u32[]{:S(2)}, u32[]{:S(2)}) collective-permute-start(bf16[4,128,1536]{2,1,0:T(8,128)(2,1)} %pad_maximum_fusion.6.rest_14_), channel_id=1, source_target_pairs={{0,16},{8,24},{16,0},{24,8},{1,17},{9,25},{17,1},{25,9},{2,18},{10... | collective-permute-start | bytes 4718600 | tf_op jit(solution)/shard_map/ppermute | solution.py:875
  999.9 35.2 %collective-permute-start.131 = (bf16[4,128,1536]{2,1,0:T(8,128)(2,1)}, bf16[4,128,1536]{2,1,0:T(8,128)(2,1)}, u32[]{:S(2)}, u32[]{:S(2)}) collective-permute-start(bf16[4,128,1536]{2,1,0:T(8,128)(2,1)} %pad_maximum_fusion.5.rest_13_), channel_id=1, source_target_pairs={{0,8},{8,0},{16,24},{24,16},{1,9},{9,1},{17,25},{25,17},{2,10},{10... | collective-permute-start | bytes 4718600 | tf_op jit(solution)/shard_map/ppermute | solution.py:875
  1017.2 37.3 %collective-permute-start.144 = (bf16[112,1536]{1,0:T(8,128)(2,1)S(1)}, bf16[112,1536]{1,0:T(8,128)(2,1)S(1)}, u32[]{:S(2)}, u32[]{:S(2)}) collective-permute-start(bf16[112,1536]{1,0:T(8,128)(2,1)S(1)} %get-tuple-element.244), channel_id=1, source_target_pairs={{0,2},{1,3},{2,4},{3,5},{4,6},{5,7},{8,10},{9,11},{10,12},{11,13},... | collective-permute-start | bytes 1032200 | tf_op jit(solution)/shard_map/ppermute | solution.py:866
  (187 other events, 2168.6 us)
Sparse Core Ops, SparseCore 0:
  844.1 42.0 reduce-scatter.1

commit v4 on v3

--- a/solution.py
+++ b/solution.py
@@ -875,11 +875,13 @@
     return lax.ppermute(value, "dp", [(i, i ^ flip) for i in range(4)])
 
 
-def line_gather(value):
+def line_gather(value, *earlier):
     place = lax.axis_index("cp") // 2
     rising, falling = value, value
     risen, fallen = [], []
     for step in range(1, LINE):
+        if earlier and step == LINE - 1:
+            rising, falling = after((rising, falling), *earlier)
         rising = hop(rising, True, range(step - 1, LINE - 1))
         falling = hop(falling, False, range(1, LINE - step + 1))
         risen.insert(0, rising)
@@ -914,8 +916,8 @@
     return pick(place).astype(WIDE) + rising.astype(WIDE) + falling.astype(WIDE)
 
 
-def group_gather(value):
-    mine = line_gather(value)
+def group_gather(value, *earlier):
+    mine = line_gather(value, *earlier)
     other = swap_core(mine)
     return (mine.reshape(HALF, -1), other.reshape(HALF, -1))
 
@@ -1107,7 +1109,7 @@
             gain_rows[layer, 1],
             before_attend[layer],
         )
-        mixed = group_gather(mixed)
+        mixed = group_gather(mixed, *(fars[0] if layer == 0 else ()))
         own, *others, gate_up, hidden, gates = experts_call(
             mixed, group_routes[layer], routers[layer].T, pieces
         )
@@ -1178,10 +1180,14 @@
             before_scatter = sums[2]
             dense_sums = sums
             second_part = last_part
-    expert_grads = expert_grads_call(**second_part, earlier=mine)
-    sums = dense_square_scatter(mine, others, *got[1], *expert_grads)
-    expert_grads = expert_grads_call(**last_part, results=expert_grads, earlier=sums[1])
-    dense_grads = [line_scatter(sums[3]), line_scatter(after(dense_sums[3], *mine))]
+    sums = dense_square_scatter(mine, others)
+    expert_grads = expert_grads_call(**second_part, earlier=sums[1])
+    late_x, late_y = after((to_x1, to_y1), *sums[2])
+    got = (across(late_x, 1), across(late_y, 2))
+    last_part["received"] = last_part["received"][:2] + [(part, 0, 1) for part in got]
+    plane = after(sums[3], *expert_grads)
+    expert_grads = expert_grads_call(**last_part, results=expert_grads)
+    dense_grads = [line_scatter(plane, (), (), got), line_scatter(after(dense_sums[3], *mine))]
     last_sums = in_order(last_sums[0], jnp.concatenate(last_sums[1], axis=0))
     result = stored[-1][6] + lax.psum_scatter(
         last_sums, "cp", scatter_dimension=0, tiled=True

time: 1110 us -> 1100 us (level)
  starting transfers between devices: 267 us -> 254 us
    ppermute x60, starting transfers between devices: 182 us -> 166 us  [hop(): return lax.ppermute(value, 'cp', pairs)]
    unnamed x204 -> x218, local copies, waits for them, and re-layouts: 48.9 us -> 49.1 us
  transfers between devices with their start and end apart: 149 -> 149, of which waited for: 62 -> 56; matrix products, arithmetic and copies ran while one was open for 15% -> 16% of each run, Pallas kernels for 23% -> 23%
where the time goes in v4:
time: 1100 us; the launch traced here: 1090 us
  waiting for transfers between devices  318 us (29%)
  Pallas kernels  289 us (26%)
  starting transfers between devices  254 us (23%)
  local copies, waits for them, and re-layouts  116 us (11%)
  other arithmetic  93.5 us (8%)
  between operations  16.4 us (1%)
    pallas_call x13, Pallas kernels, call(): pl.pallas_call(whole, grid=grid, out_shape=outs, in_specs=in_specs, out_s...  182 us
    ppermute x60, starting transfers between devices, hop(): return lax.ppermute(value, 'cp', pairs)  166 us
    ppermute x60, waiting for transfers between devices, hop(): return lax.ppermute(value, 'cp', pairs)  153 us
    ppermute x44, waiting for transfers between devices, across(): return lax.ppermute(value, 'dp', [(i, i ^ flip) for i in range(4)])  138 us
    pallas_call x6, Pallas kernels, expert_grads_call(): pl.pallas_call(body, out_shape=outs, input_output_aliases={first_kept + i...  83.4 us
    unnamed x218, local copies, waits for them, and re-layouts  49.1 us
    ppermute x44, starting transfers between devices, across(): return lax.ppermute(value, 'dp', [(i, i ^ flip) for i in range(4)])  44.9 us
    ppermute x12, starting transfers between devices, leap(): return lax.ppermute(value, 'cp', pairs)  37.7 us
  transfers between devices with their start and end apart: 149, of which 56 were waited for; matrix products, arithmetic and copies ran while one was open for 16% of the time, Pallas kernels for 23%

profile of v4, /device:TPU:0, one launch (start us, length us, event | category | flops | bytes accessed | tf_op | source)
XLA Modules:
  0.0 1089.3 jit_solution(8959486281088843355)
XLA Ops:
  37.9 7.2 collective-permute-done.4
  84.2 11.8 %collective-permute-done.24 = bf16[240,1536]{1,0:T(8,128)(2,1)} collective-permute-done((bf16[240,1536]{1,0:T(8,128)(2,1)}, bf16[240,1536]{1,0:T(8,128)(2,1)}, u32[]{:S(2)}, u32[]{:S(2)}) %collective-permute-start.24) | collective-permute-done | bytes 737312 | tf_op jit(solution)/shard_map/ppermute | solution.py:866
  107.1 13.3 %collective-permute-done.25 = bf16[240,1536]{1,0:T(8,128)(2,1)} collective-permute-done((bf16[240,1536]{1,0:T(8,128)(2,1)}, bf16[240,1536]{1,0:T(8,128)(2,1)}, u32[]{:S(2)}, u32[]{:S(2)}) %collective-permute-start.25) | collective-permute-done | bytes 737312 | tf_op jit(solution)/shard_map/ppermute | solution.py:866
  139.7 6.9 project.2
  146.6 8.4 collective-permute-done.31.refs_4_.refs_12_.refs_13_
  155.0 8.2 collective-permute-start.19
  171.3 12.8 %collective-permute-done.32.refs_3_.refs_10_.refs_11_ = bf16[384,1536]{1,0:T(8,128)(2,1)S(1)} collective-permute-done((bf16[384,1536]{1,0:T(8,128)(2,1)}, bf16[384,1536]{1,0:T(8,128)(2,1)S(1)}, u32[]{:S(2)}, u32[]{:S(2)}) %collective-permute-start.32) | collective-permute-done | bytes 1179680 | tf_op jit(solution)/shard_map/ppermute | solution.py:875
  184.1 8.1 collective-permute-start.17
  213.8 9.5 attend.2
  227.4 8.0 collective-permute-done.27
  241.5 10.2 collective-permute-done.30
  258.8 8.7 collective-permute-done.38
  279.5 25.9 %experts.2 = (bf16[512,1536]{1,0:T(8,128)(2,1)}, bf16[256,1536]{1,0:T(8,128)(2,1)}, bf16[256,1536]{1,0:T(8,128)(2,1)}, bf16[1024,3072]{1,0:T(8,128)(2,1)}, bf16[...) custom-call(s32[4]{0:T(128)} %pad_add_fusion.2.refs_0_.places, bf16[512,1536]{1,0:T(8,128)(2,1)} %bitcast.300, ...), custom_call_target="tpu_custom_call" | custom-call | bytes 29600000 | tf_op jit(solution)/shard_map/experts/pallas_call | solution.py:151
  345.2 9.1 collective-permute-done.57.refs_14_.refs_1_.refs_6_.refs_7_
  368.0 7.0 project.3
  391.2 9.5 attend.3
  407.3 7.6 collective-permute-done.63
  423.2 11.5 %collective-permute-done.71.refs_3_.refs_10_.refs_11_ = bf16[384,1536]{1,0:T(8,128)(2,1)S(1)} collective-permute-done((bf16[384,1536]{1,0:T(8,128)(2,1)}, bf16[384,1536]{1,0:T(8,128)(2,1)S(1)}, u32[]{:S(2)}, u32[]{:S(2)}) %collective-permute-start.71) | collective-permute-done | bytes 1179680 | tf_op jit(solution)/shard_map/ppermute | solution.py:875
  452.0 21.7 %collective-permute-done.74.refs_14_.refs_15_ = bf16[576,1536]{1,0:T(8,128)(2,1)} collective-permute-done((bf16[576,1536]{1,0:T(8,128)(2,1)}, bf16[576,1536]{1,0:T(8,128)(2,1)}, u32[]{:S(2)}, u32[]{:S(2)}) %collective-permute-start.74) | collective-permute-done | bytes 1769504 | tf_op jit(solution)/shard_map/ppermute | solution.py:875
  475.1 25.9 %experts.3 = (bf16[512,1536]{1,0:T(8,128)(2,1)}, bf16[256,1536]{1,0:T(8,128)(2,1)}, bf16[256,1536]{1,0:T(8,128)(2,1)}, bf16[1024,3072]{1,0:T(8,128)(2,1)}, bf16[...) custom-call(s32[4]{0:T(128)} %pad_add_fusion.2.refs_0_.places, bf16[512,1536]{1,0:T(8,128)(2,1)} %bitcast.306, ...), custom_call_target="tpu_custom_call" | custom-call | bytes 29600000 | tf_op jit(solution)/shard_map/experts/pallas_call | solution.py:151
  501.1 27.7 %experts_back.2 = (bf16[512,1536]{1,0:T(8,128)(2,1)}, bf16[256,1536]{1,0:T(8,128)(2,1)}, bf16[256,1536]{1,0:T(8,128)(2,1)}, bf16[1024,3072]{1,0:T(8,128)(2,1)}, bf16[1024,16]{1,0:T(8,128)(2,1)}) custom-call(s32[4]{0:T(128)} %pad_add_fusion.2.refs_0_.places, bf16[512,1536]{1,0:T(8,128)(2,1)} %bitcast.318, ...), custom_call_target="tpu_custom_call" | custom-call | bytes 29600000 | tf_op jit(solution)/shard_map/experts_back/pallas_call | solution.py:151
  529.3 10.8 expert_grads.6
  548.7 7.6 collective-permute-done.79
  557.2 18.6 %collective-permute-start.80 = (bf16[128,1536]{1,0:T(8,128)(2,1)S(1)}, bf16[128,1536]{1,0:T(8,128)(2,1)S(1)}, u32[]{:S(2)}, u32[]{:S(2)}) collective-permute-start(bf16[128,1536]{1,0:T(8,128)(2,1)S(1)} %get-tuple-element.247), channel_id=1, source_target_pairs={{0,2},{1,3},{2,4},{3,5},{8,10},{9,11},{10,12},{11,13},{16,18},{17,... | collective-permute-start | bytes 1179656 | tf_op jit(solution)/shard_map/ppermute | solution.py:866
  575.8 7.3 collective-permute-done.80
  595.6 18.1 %expert_grads.7 = (bf16[576,1536]{1,0:T(8,128)(2,1)}, bf16[576,1536]{1,0:T(8,128)(2,1)}, bf16[576,1536]{1,0:T(8,128)(2,1)}, bf16[576,1536]{1,0:T(8,128)(2,1)}) custom-call(s32[4]{0:T(128)} %pad_add_fusion.2.refs_0_.places, bf16[512,1536]{1,0:T(8,128)(2,1)} %bitcast.308, bf16[512,1536]{1,0:T(8,128)(2,1)} %bitcast.91.refs_2_.rest_1_.rest_3_, ...), custom_call_target="tpu_custom_call" | custom-call | tf_op jit(solution)/shard_map/expert_grads/pallas_call | solution.py:631
  614.8 12.6 %attend_back.2 = (f32[128,1536]{1,0:T(8,128)}, bf16[128,1536]{1,0:T(8,128)(2,1)}, f32[12,128,128]{2,1,0:T(8,128)}, bf16[512,512]{1,0:T(8,128)(2,1)}, bf16[512,512]{1,0:T(8,128)(2,1)}, /*index=5*/f32[1,1536]{1,0:T(1,128)}) custom-call(s32[4]{0:T(128)} %pad_add_fusion.2.refs_0_.places, f32[128,1536]{1,0:T(8,128)} %fusion.20.refs_1_, ...), custom_call_target="tpu_custom_call" | custom-call | tf_op jit(solution)/shard_map/attend_back/pallas_call | solution.py:151
  634.7 6.0 collective-permute-done.90
  646.5 6.8 project_back.2
  659.9 7.6 collective-permute-done.91
  677.3 11.3 %dense_grads.2 = (bf16[4,112,1536]{2,1,0:T(8,128)(2,1)}, bf16[4,112,1536]{2,1,0:T(8,128)(2,1)}, bf16[4,112,1536]{2,1,0:T(8,128)(2,1)}, bf16[4,112,1536]{2,1,0:T(...) custom-call(s32[4]{0:T(128)} %pad_add_fusion.2.refs_0_.places, ...), custom_call_target="tpu_custom_call" | custom-call | tf_op jit(solution)/shard_map/dense_grads/pallas_call | solution.py:846
  693.7 13.4 %collective-permute-done.96 = bf16[128,1536]{1,0:T(8,128)(2,1)S(1)} collective-permute-done((bf16[128,1536]{1,0:T(8,128)(2,1)}, bf16[128,1536]{1,0:T(8,128)(2,1)S(1)}, u32[]{:S(2)}, u32[]{:S(2)}) %collective-permute-start.96) | collective-permute-done | bytes 393248 | tf_op jit(solution)/shard_map/ppermute | solution.py:866
  719.4 10.6 collective-permute-done.104
  739.8 27.6 %experts_back.3 = (bf16[512,1536]{1,0:T(8,128)(2,1)}, bf16[256,1536]{1,0:T(8,128)(2,1)}, bf16[256,1536]{1,0:T(8,128)(2,1)}, bf16[1024,3072]{1,0:T(8,128)(2,1)}, bf16[1024,16]{1,0:T(8,128)(2,1)}) custom-call(s32[4]{0:T(128)} %pad_add_fusion.2.refs_0_.places, bf16[512,1536]{1,0:T(8,128)(2,1)} %bitcast.322, bf16[512,1536]{1,0:T(8,128)(2,1)} %bitcast.326, ...), custom_call_target="tpu_custom_call" | custom-call | bytes 29600000 | tf_op jit(solution)/shard_map/experts_back/pallas_call | solution.py:151
  769.2 10.8 expert_grads.8
  791.1 7.5 collective-permute-done.111
  799.6 16.6 %collective-permute-start.112 = (bf16[128,1536]{1,0:T(8,128)(2,1)S(1)}, bf16[128,1536]{1,0:T(8,128)(2,1)S(1)}, u32[]{:S(2)}, u32[]{:S(2)}) collective-permute-start(bf16[128,1536]{1,0:T(8,128)(2,1)S(1)} %get-tuple-element.243), channel_id=1, source_target_pairs={{0,2},{1,3},{2,4},{3,5},{8,10},{9,11},{10,12},{11,13},{16,18},{17,... | collective-permute-start | bytes 1179656 | tf_op jit(solution)/shard_map/ppermute | solution.py:866
  838.7 18.1 %expert_grads.9 = (bf16[576,1536]{1,0:T(8,128)(2,1)}, bf16[576,1536]{1,0:T(8,128)(2,1)}, bf16[576,1536]{1,0:T(8,128)(2,1)}, bf16[576,1536]{1,0:T(8,128)(2,1)}) custom-call(s32[4]{0:T(128)} %pad_add_fusion.2.refs_0_.places, bf16[512,1536]{1,0:T(8,128)(2,1)} %bitcast.302, bf16[512,1536]{1,0:T(8,128)(2,1)} %bitcast.314, bf16[512,1536]{1,0:T(8,128)(2,1)} %bitcast.303, ...), custom_call_target="tpu_custom_call" | custom-call | tf_op jit(solution)/shard_map/expert_grads/pallas_call | solution.py:631
  857.8 12.7 %attend_back.3 = (f32[128,1536]{1,0:T(8,128)}, bf16[128,1536]{1,0:T(8,128)(2,1)}, f32[12,128,128]{2,1,0:T(8,128)}, bf16[512,512]{1,0:T(8,128)(2,1)}, bf16[512,512]{1,0:T(8,128)(2,1)}, /*index=5*/f32[1,1536]{1,0:T(1,128)}) custom-call(s32[4]{0:T(128)} %pad_add_fusion.2.refs_0_.places, f32[128,1536]{1,0:T(8,128)} %fusion.15.refs_1_, ...), custom_call_target="tpu_custom_call" | custom-call | tf_op jit(solution)/shard_map/attend_back/pallas_call | solution.py:151
  882.2 6.7 collective-permute-done.122
  899.0 6.8 project_back.3
  914.9 12.1 %dense_grads.3 = (bf16[4,128,1536]{2,1,0:T(8,128)(2,1)}, bf16[4,128,1536]{2,1,0:T(8,128)(2,1)}, bf16[4,128,1536]{2,1,0:T(8,128)(2,1)}, bf16[4,128,1536]{2,1,0:T(...) custom-call(s32[4]{0:T(128)} %pad_add_fusion.2.refs_0_.places, ...), custom_call_target="tpu_custom_call" | custom-call | tf_op jit(solution)/shard_map/dense_grads/pallas_call | solution.py:846
  933.6 6.4 collective-permute-start.142
  949.9 14.6 %collective-permute-done.131 = bf16[2,128,1536]{2,1,0:T(8,128)(2,1)S(1)} collective-permute-done((bf16[2,128,1536]{2,1,0:T(8,128)(2,1)S(1)}, bf16[2,128,1536]{2,1,0:T(8,128)(2,1)S(1)}, u32[]{:S(2)}, u32[]{:S(2)}) %collective-permute-start.131) | collective-permute-done | bytes 786464 | tf_op jit(solution)/shard_map/ppermute | solution.py:875
  988.6 12.7 %expert_grads.10 = (f32[2,2,384,1536]{3,2,1,0:T(8,128)}, f32[2,2,192,1536]{3,2,1,0:T(8,128)}) custom-call(s32[4]{0:T(128)} %pad_add_fusion.2.refs_0_.places, bf16[512,1536]{1,0:T(8,128)(2,1)} %bitcast.310, bf16[512,1536]{1,0:T(8,128)(2,1)} %bitcast.91.refs_2_.rest_1_.rest_3_, ...), custom_call_target="tpu_custom_call" | custom-call | bytes 14800000 | tf_op jit(solution)/shard_map/expert_grads/pallas_call | solution.py:631
  1028.0 12.6 %collective-permute-start.134 = (bf16[128,1536]{1,0:T(8,128)(2,1)S(1)}, bf16[128,1536]{1,0:T(8,128)(2,1)S(1)}, u32[]{:S(2)}, u32[]{:S(2)}) collective-permute-start(bf16[128,1536]{1,0:T(8,128)(2,1)S(1)} %get-tuple-element.237), channel_id=1, source_target_pairs={{0,2},{1,3},{2,4},{3,5},{8,10},{9,11},{10,12},{11,13},{16,18},{17,... | collective-permute-start | bytes 1179656 | tf_op jit(solution)/shard_map/ppermute | solution.py:866
  1046.7 12.1 %collective-permute-done.137.refs_2_.rest_9_ = bf16[576,1536]{1,0:T(8,128)(2,1)} collective-permute-done((bf16[576,1536]{1,0:T(8,128)(2,1)}, bf16[576,1536]{1,0:T(8,128)(2,1)}, u32[]{:S(2)}, u32[]{:S(2)}) %collective-permute-start.137) | collective-permute-done | bytes 1769504 | tf_op jit(solution)/shard_map/ppermute | solution.py:875
  1066.0 12.8 %expert_grads.11 = (f32[2,2,384,1536]{3,2,1,0:T(8,128)}, f32[2,2,192,1536]{3,2,1,0:T(8,128)}) custom-call(s32[4]{0:T(128)} %pad_add_fusion.2.refs_0_.places, bf16[512,1536]{1,0:T(8,128)(2,1)} %bitcast.304, bf16[512,1536]{1,0:T(8,128)(2,1)} %bitcast.316, ...), custom_call_target="tpu_custom_call", output_to_operand_aliasing={{0}: (12, {}), {1}: (13, {})} | custom-call | bytes 14800000 | tf_op jit(solution)/shard_map/expert_grads/pallas_call | solution.py:631
  (690 shorter events, 493.1 us)
Async XLA Ops:
  7.2 966.9 %reduce-scatter.2.cloned.1.call-start = ((), (), s32[]{:S(2)}) async-start(), calls=%async_computation.1 | async-start | bytes 3538944 | tf_op jit(solution)/shard_map/reduce_scatter | solution.py:1192
  24.6 37.3 %collective-permute-start.6 = (bf16[384,1536]{1,0:T(8,128)(2,1)S(1)}, bf16[384,1536]{1,0:T(8,128)(2,1)S(1)}, u32[]{:S(2)}, u32[]{:S(2)}) collective-permute-start(bf16[384,1536]{1,0:T(8,128)(2,1)S(1)} %get-tuple-element.232.refs_5_.refs_6_), channel_id=1, source_target_pairs={{0,8},{8,0},{16,24},{24,16},{1,9},{9,1},{17,25},{25,17},{2,10},{10... | collective-permute-start | bytes 3538952 | tf_op jit(solution)/shard_map/ppermute | solution.py:875
  26.1 35.8 %collective-permute-start.7 = (bf16[384,1536]{1,0:T(8,128)(2,1)S(1)}, bf16[384,1536]{1,0:T(8,128)(2,1)S(1)}, u32[]{:S(2)}, u32[]{:S(2)}) collective-permute-start(bf16[384,1536]{1,0:T(8,128)(2,1)S(1)} %get-tuple-element.232.refs_5_.refs_6_), channel_id=1, source_target_pairs={{0,16},{8,24},{16,0},{24,8},{1,17},{9,25},{17,1},{25,9},{2,18},{10... | collective-permute-start | bytes 3538952 | tf_op jit(solution)/shard_map/ppermute | solution.py:875
  64.0 33.4 %collective-permute-start.9 = (bf16[4,128,1536]{2,1,0:T(8,128)(2,1)}, bf16[4,128,1536]{2,1,0:T(8,128)(2,1)S(1)}, u32[]{:S(2)}, u32[]{:S(2)}) collective-permute-start(bf16[4,128,1536]{2,1,0:T(8,128)(2,1)} %after.24.refs_1_.refs_4_.refs_8_.refs_10_.refs_7_), channel_id=1, source_target_pairs={{0,8},{8,0},{16,24},{24,16},{1,9},{9,1},{17,25},{25,17},{2,10},{10... | collective-permute-start | bytes 4718600 | tf_op jit(solution)/shard_map/ppermute | solution.py:875
  65.8 35.8 %collective-permute-start.11 = (bf16[4,128,1536]{2,1,0:T(8,128)(2,1)}, bf16[4,128,1536]{2,1,0:T(8,128)(2,1)}, u32[]{:S(2)}, u32[]{:S(2)}) collective-permute-start(bf16[4,128,1536]{2,1,0:T(8,128)(2,1)} %after.24.refs_1_.refs_4_.refs_8_.refs_10_.refs_7_), channel_id=1, source_target_pairs={{0,16},{8,24},{16,0},{24,8},{1,17},{9,25},{17,1},{25,9},{2,18},{10... | collective-permute-start | bytes 4718600 | tf_op jit(solution)/shard_map/ppermute | solution.py:875
  84.2 41.7 %collective-permute-start.8 = (bf16[4,128,1536]{2,1,0:T(8,128)(2,1)S(1)}, bf16[4,128,1536]{2,1,0:T(8,128)(2,1)}, u32[]{:S(2)}, u32[]{:S(2)}) collective-permute-start(bf16[4,128,1536]{2,1,0:T(8,128)(2,1)S(1)} %copy-done), channel_id=1, source_target_pairs={{0,1},{1,0},{2,3},{3,2},{4,5},{5,4},{6,7},{7,6},{8,9},{9,8},{10,11... | collective-permute-start | bytes 4718600 | tf_op jit(solution)/shard_map/ppermute | solution.py:860
  125.9 29.1 %collective-permute-start.31 = (bf16[2,192,1536]{2,1,0:T(8,128)(2,1)}, bf16[2,192,1536]{2,1,0:T(8,128)(2,1)}, u32[]{:S(2)}, u32[]{:S(2)}) collective-permute-start(bf16[2,192,1536]{2,1,0:T(8,128)(2,1)} %after.26.refs_11_.refs_12_), channel_id=1, source_target_pairs={{0,8},{8,0},{16,24},{24,16},{1,9},{9,1},{17,25},{25,17},{2,10},{10... | collective-permute-start | bytes 3538952 | tf_op jit(solution)/shard_map/ppermute | solution.py:875
  129.2 65.0 %collective-permute-start.26 = (bf16[240,1536]{1,0:T(8,128)(2,1)}, bf16[240,1536]{1,0:T(8,128)(2,1)}, u32[]{:S(2)}, u32[]{:S(2)}) collective-permute-start(bf16[240,1536]{1,0:T(8,128)(2,1)} %collective-permute-done.25), channel_id=1, source_target_pairs={{2,0},{3,1},{10,8},{11,9},{18,16},{19,17},{26,24},{27,25}} | collective-permute-start | bytes 2211848 | tf_op jit(solution)/shard_map/ppermute | solution.py:866
  130.7 35.0 %collective-permute-start.33 = (bf16[2,192,1536]{2,1,0:T(8,128)(2,1)S(1)}, bf16[2,192,1536]{2,1,0:T(8,128)(2,1)}, u32[]{:S(2)}, u32[]{:S(2)}) collective-permute-start(bf16[2,192,1536]{2,1,0:T(8,128)(2,1)S(1)} %copy-done.25), channel_id=1, source_target_pairs={{0,16},{8,24},{16,0},{24,8},{1,17},{9,25},{17,1},{25,9},{2,18},{10... | collective-permute-start | bytes 3538952 | tf_op jit(solution)/shard_map/ppermute | solution.py:875
  132.5 51.6 %collective-permute-start.32 = (bf16[384,1536]{1,0:T(8,128)(2,1)}, bf16[384,1536]{1,0:T(8,128)(2,1)S(1)}, u32[]{:S(2)}, u32[]{:S(2)}) collective-permute-start(bf16[384,1536]{1,0:T(8,128)(2,1)} %after.27.refs_8_.refs_9_), channel_id=1, source_target_pairs={{0,16},{8,24},{16,0},{24,8},{1,17},{9,25},{17,1},{25,9},{2,18},{10... | collective-permute-start | bytes 3538952 | tf_op jit(solution)/shard_map/ppermute | solution.py:875
  132.8 60.7 %collective-permute-start.34 = (bf16[384,1536]{1,0:T(8,128)(2,1)}, bf16[384,1536]{1,0:T(8,128)(2,1)}, u32[]{:S(2)}, u32[]{:S(2)}) collective-permute-start(bf16[384,1536]{1,0:T(8,128)(2,1)} %after.27.refs_8_.refs_9_), channel_id=1, source_target_pairs={{0,8},{8,0},{16,24},{24,16},{1,9},{9,1},{17,25},{25,17},{2,10},{10... | collective-permute-start | bytes 3538952 | tf_op jit(solution)/shard_map/ppermute | solution.py:875
  155.0 41.7 %collective-permute-start.19 = (bf16[128,512]{1,0:T(8,128)(2,1)}, bf16[128,512]{1,0:T(8,128)(2,1)}, u32[]{:S(2)}, u32[]{:S(2)}) collective-permute-start(bf16[128,512]{1,0:T(8,128)(2,1)} %get-tuple-element.120), channel_id=1, source_target_pairs={{0,2},{1,3},{2,4},{3,5},{4,6},{5,7},{8,10},{9,11},{10,12},{11,13},... | collective-permute-start | bytes 393224 | tf_op jit(solution)/shard_map/ppermute | solution.py:871
  165.7 31.0 %collective-permute-start.18 = (bf16[128,512]{1,0:T(8,128)(2,1)}, bf16[128,512]{1,0:T(8,128)(2,1)}, u32[]{:S(2)}, u32[]{:S(2)}) collective-permute-start(bf16[128,512]{1,0:T(8,128)(2,1)} %get-tuple-element.120), channel_id=1, source_target_pairs={{0,4},{1,5},{2,6},{3,7},{8,12},{9,13},{10,14},{11,15},{16,20},{17,... | collective-permute-start | bytes 393224 | tf_op jit(solution)/shard_map/ppermute | solution.py:871
  193.5 59.0 %collective-permute-start.35 = (bf16[576,1536]{1,0:T(8,128)(2,1)}, bf16[576,1536]{1,0:T(8,128)(2,1)S(1)}, u32[]{:S(2)}, u32[]{:S(2)}) collective-permute-start(bf16[576,1536]{1,0:T(8,128)(2,1)} %get-tuple-element.123), channel_id=1, source_target_pairs={{0,16},{8,24},{16,0},{24,8},{1,17},{9,25},{17,1},{25,9},{2,18},{10... | collective-permute-start | bytes 5308424 | tf_op jit(solution)/shard_map/ppermute | solution.py:875
  194.2 58.4 %collective-permute-start.36 = (bf16[576,1536]{1,0:T(8,128)(2,1)}, bf16[576,1536]{1,0:T(8,128)(2,1)S(1)}, u32[]{:S(2)}, u32[]{:S(2)}) collective-permute-start(bf16[576,1536]{1,0:T(8,128)(2,1)} %get-tuple-element.124), channel_id=1, source_target_pairs={{0,8},{8,0},{16,24},{24,16},{1,9},{9,1},{17,25},{25,17},{2,10},{10... | collective-permute-start | bytes 5308424 | tf_op jit(solution)/shard_map/ppermute | solution.py:875
  270.8 34.5 %collective-permute-start.40 = (bf16[4,112,1536]{2,1,0:T(8,128)(2,1)}, bf16[4,112,1536]{2,1,0:T(8,128)(2,1)}, u32[]{:S(2)}, u32[]{:S(2)}) collective-permute-start(bf16[4,112,1536]{2,1,0:T(8,128)(2,1)} %after.30.refs_4_.refs_8_.refs_10_.refs_7_), channel_id=1, source_target_pairs={{0,8},{8,0},{16,24},{24,16},{1,9},{9,1},{17,25},{25,17},{2,10},{10... | collective-permute-start | bytes 4128776 | tf_op jit(solution)/shard_map/ppermute | solution.py:875
  272.3 33.0 %collective-permute-start.41 = (bf16[4,112,1536]{2,1,0:T(8,128)(2,1)}, bf16[4,112,1536]{2,1,0:T(8,128)(2,1)}, u32[]{:S(2)}, u32[]{:S(2)}) collective-permute-start(bf16[4,112,1536]{2,1,0:T(8,128)(2,1)} %after.30.refs_4_.refs_8_.refs_10_.refs_7_), channel_id=1, source_target_pairs={{0,16},{8,24},{16,0},{24,8},{1,17},{9,25},{17,1},{25,9},{2,18},{10... | collective-permute-start | bytes 4128776 | tf_op jit(solution)/shard_map/ppermute | solution.py:875
  362.8 43.1 %collective-permute-start.72 = (bf16[2,192,1536]{2,1,0:T(8,128)(2,1)}, bf16[2,192,1536]{2,1,0:T(8,128)(2,1)S(1)}, u32[]{:S(2)}, u32[]{:S(2)}) collective-permute-start(bf16[2,192,1536]{2,1,0:T(8,128)(2,1)} %after.35.refs_11_.refs_12_), channel_id=1, source_target_pairs={{0,8},{8,0},{16,24},{24,16},{1,9},{9,1},{17,25},{25,17},{2,10},{10... | collective-permute-start | bytes 3538952 | tf_op jit(solution)/shard_map/ppermute | solution.py:875
  384.1 32.3 %collective-permute-start.73 = (bf16[2,192,1536]{2,1,0:T(8,128)(2,1)S(1)}, bf16[2,192,1536]{2,1,0:T(8,128)(2,1)}, u32[]{:S(2)}, u32[]{:S(2)}) collective-permute-start(bf16[2,192,1536]{2,1,0:T(8,128)(2,1)S(1)} %copy-done.21), channel_id=1, source_target_pairs={{0,16},{8,24},{16,0},{24,8},{1,17},{9,25},{17,1},{25,9},{2,18},{10... | collective-permute-start | bytes 3538952 | tf_op jit(solution)/shard_map/ppermute | solution.py:875
  388.5 47.8 %collective-permute-start.70 = (bf16[384,1536]{1,0:T(8,128)(2,1)}, bf16[384,1536]{1,0:T(8,128)(2,1)}, u32[]{:S(2)}, u32[]{:S(2)}) collective-permute-start(bf16[384,1536]{1,0:T(8,128)(2,1)} %after.34.refs_8_.refs_9_), channel_id=1, source_target_pairs={{0,8},{8,0},{16,24},{24,16},{1,9},{9,1},{17,25},{25,17},{2,10},{10... | collective-permute-start | bytes 3538952 | tf_op jit(solution)/shard_map/ppermute | solution.py:875
  389.9 44.8 %collective-permute-start.71 = (bf16[384,1536]{1,0:T(8,128)(2,1)}, bf16[384,1536]{1,0:T(8,128)(2,1)S(1)}, u32[]{:S(2)}, u32[]{:S(2)}) collective-permute-start(bf16[384,1536]{1,0:T(8,128)(2,1)} %after.34.refs_8_.refs_9_), channel_id=1, source_target_pairs={{0,16},{8,24},{16,0},{24,8},{1,17},{9,25},{17,1},{25,9},{2,18},{10... | collective-permute-start | bytes 3538952 | tf_op jit(solution)/shard_map/ppermute | solution.py:875
  436.3 37.4 %collective-permute-start.74 = (bf16[576,1536]{1,0:T(8,128)(2,1)}, bf16[576,1536]{1,0:T(8,128)(2,1)}, u32[]{:S(2)}, u32[]{:S(2)}) collective-permute-start(bf16[576,1536]{1,0:T(8,128)(2,1)} %get-tuple-element.138), channel_id=1, source_target_pairs={{0,16},{8,24},{16,0},{24,8},{1,17},{9,25},{17,1},{25,9},{2,18},{10... | collective-permute-start | bytes 5308424 | tf_op jit(solution)/shard_map/ppermute | solution.py:875
  437.9 37.2 %collective-permute-start.75 = (bf16[576,1536]{1,0:T(8,128)(2,1)}, bf16[576,1536]{1,0:T(8,128)(2,1)}, u32[]{:S(2)}, u32[]{:S(2)}) collective-permute-start(bf16[576,1536]{1,0:T(8,128)(2,1)} %get-tuple-element.139), channel_id=1, source_target_pairs={{0,8},{8,0},{16,24},{24,16},{1,9},{9,1},{17,25},{25,17},{2,10},{10... | collective-permute-start | bytes 5308424 | tf_op jit(solution)/shard_map/ppermute | solution.py:875
  450.1 51.0 %collective-permute-start.76 = (bf16[4,128,1536]{2,1,0:T(8,128)(2,1)S(1)}, bf16[4,128,1536]{2,1,0:T(8,128)(2,1)}, u32[]{:S(2)}, u32[]{:S(2)}) collective-permute-start(bf16[4,128,1536]{2,1,0:T(8,128)(2,1)S(1)} %copy-done.7), channel_id=1, source_target_pairs={{0,1},{1,0},{2,3},{3,2},{4,5},{5,4},{6,7},{7,6},{8,9},{9,8},{10,11... | collective-permute-start | bytes 4718600 | tf_op jit(solution)/shard_map/ppermute | solution.py:860
  545.4 40.9 %collective-permute-start.83 = (bf16[576,1536]{1,0:T(8,128)(2,1)}, bf16[576,1536]{1,0:T(8,128)(2,1)S(1)}, u32[]{:S(2)}, u32[]{:S(2)}) collective-permute-start(bf16[576,1536]{1,0:T(8,128)(2,1)} %get-tuple-element.150.refs_2_), channel_id=1, source_target_pairs={{0,8},{8,0},{16,24},{24,16},{1,9},{9,1},{17,25},{25,17},{2,10},{10... | collective-permute-start | bytes 5308424 | tf_op jit(solution)/shard_map/ppermute | solution.py:875
  545.7 40.7 %collective-permute-start.84 = (bf16[576,1536]{1,0:T(8,128)(2,1)}, bf16[576,1536]{1,0:T(8,128)(2,1)}, u32[]{:S(2)}, u32[]{:S(2)}) collective-permute-start(bf16[576,1536]{1,0:T(8,128)(2,1)} %get-tuple-element.151.refs_3_), channel_id=1, source_target_pairs={{0,16},{8,24},{16,0},{24,8},{1,17},{9,25},{17,1},{25,9},{2,18},{10... | collective-permute-start | bytes 5308424 | tf_op jit(solution)/shard_map/ppermute | solution.py:875
  627.5 47.5 %collective-permute-start.100 = (bf16[576,1536]{1,0:T(8,128)(2,1)}, bf16[576,1536]{1,0:T(8,128)(2,1)S(1)}, u32[]{:S(2)}, u32[]{:S(2)}) collective-permute-start(bf16[576,1536]{1,0:T(8,128)(2,1)} %get-tuple-element.158.refs_20_), channel_id=1, source_target_pairs={{0,8},{8,0},{16,24},{24,16},{1,9},{9,1},{17,25},{25,17},{2,10},{10... | collective-permute-start | bytes 5308424 | tf_op jit(solution)/shard_map/ppermute | solution.py:875
  628.2 47.9 %collective-permute-start.101 = (bf16[576,1536]{1,0:T(8,128)(2,1)}, bf16[576,1536]{1,0:T(8,128)(2,1)S(1)}, u32[]{:S(2)}, u32[]{:S(2)}) collective-permute-start(bf16[576,1536]{1,0:T(8,128)(2,1)} %get-tuple-element.160.refs_22_), channel_id=1, source_target_pairs={{0,16},{8,24},{16,0},{24,8},{1,17},{9,25},{17,1},{25,9},{2,18},{10... | collective-permute-start | bytes 5308424 | tf_op jit(solution)/shard_map/ppermute | solution.py:875
  674.4 64.3 %collective-permute-start.98 = (bf16[576,1536]{1,0:T(8,128)(2,1)}, bf16[576,1536]{1,0:T(8,128)(2,1)}, u32[]{:S(2)}, u32[]{:S(2)}) collective-permute-start(bf16[576,1536]{1,0:T(8,128)(2,1)} %get-tuple-element.159.refs_21_), channel_id=1, source_target_pairs={{0,8},{8,0},{16,24},{24,16},{1,9},{9,1},{17,25},{25,17},{2,10},{10... | collective-permute-start | bytes 5308424 | tf_op jit(solution)/shard_map/ppermute | solution.py:875
  675.0 63.7 %collective-permute-start.99 = (bf16[576,1536]{1,0:T(8,128)(2,1)}, bf16[576,1536]{1,0:T(8,128)(2,1)}, u32[]{:S(2)}, u32[]{:S(2)}) collective-permute-start(bf16[576,1536]{1,0:T(8,128)(2,1)} %get-tuple-element.161.refs_23_), channel_id=1, source_target_pairs={{0,16},{8,24},{16,0},{24,8},{1,17},{9,25},{17,1},{25,9},{2,18},{10... | collective-permute-start | bytes 5308424 | tf_op jit(solution)/shard_map/ppermute | solution.py:875
  707.3 31.4 %collective-permute-start.97 = (bf16[4,128,1536]{2,1,0:T(8,128)(2,1)S(1)}, bf16[4,128,1536]{2,1,0:T(8,128)(2,1)S(1)}, u32[]{:S(2)}, u32[]{:S(2)}) collective-permute-start(bf16[4,128,1536]{2,1,0:T(8,128)(2,1)S(1)} %constant_dynamic-slice_fusion.1), channel_id=1, source_target_pairs={{0,1},{1,0},{2,3},{3,2},{4,5},{5,4},{6,7},{7,6},{8,9},{9,8},{10,11... | collective-permute-start | bytes 4718600 | tf_op jit(solution)/shard_map/ppermute | solution.py:860
  731.4 36.1 %collective-permute-start.105 = (bf16[4,112,1536]{2,1,0:T(8,128)(2,1)}, bf16[4,112,1536]{2,1,0:T(8,128)(2,1)}, u32[]{:S(2)}, u32[]{:S(2)}) collective-permute-start(bf16[4,112,1536]{2,1,0:T(8,128)(2,1)} %pad_maximum_fusion.7), channel_id=1, source_target_pairs={{0,8},{8,0},{16,24},{24,16},{1,9},{9,1},{17,25},{25,17},{2,10},{10... | collective-permute-start | bytes 4128776 | tf_op jit(solution)/shard_map/ppermute | solution.py:875
  737.6 31.1 %collective-permute-start.108 = (bf16[4,112,1536]{2,1,0:T(8,128)(2,1)}, bf16[4,112,1536]{2,1,0:T(8,128)(2,1)}, u32[]{:S(2)}, u32[]{:S(2)}) collective-permute-start(bf16[4,112,1536]{2,1,0:T(8,128)(2,1)} %pad_maximum_fusion.8), channel_id=1, source_target_pairs={{0,16},{8,24},{16,0},{24,8},{1,17},{9,25},{17,1},{25,9},{2,18},{10... | collective-permute-start | bytes 4128776 | tf_op jit(solution)/shard_map/ppermute | solution.py:875
  785.2 40.8 %collective-permute-start.115 = (bf16[576,1536]{1,0:T(8,128)(2,1)}, bf16[576,1536]{1,0:T(8,128)(2,1)S(1)}, u32[]{:S(2)}, u32[]{:S(2)}) collective-permute-start(bf16[576,1536]{1,0:T(8,128)(2,1)} %get-tuple-element.185.refs_2_), channel_id=1, source_target_pairs={{0,8},{8,0},{16,24},{24,16},{1,9},{9,1},{17,25},{25,17},{2,10},{10... | collective-permute-start | bytes 5308424 | tf_op jit(solution)/shard_map/ppermute | solution.py:875
  786.7 40.5 %collective-permute-start.116 = (bf16[576,1536]{1,0:T(8,128)(2,1)}, bf16[576,1536]{1,0:T(8,128)(2,1)}, u32[]{:S(2)}, u32[]{:S(2)}) collective-permute-start(bf16[576,1536]{1,0:T(8,128)(2,1)} %get-tuple-element.186.refs_3_), channel_id=1, source_target_pairs={{0,16},{8,24},{16,0},{24,8},{1,17},{9,25},{17,1},{25,9},{2,18},{10... | collective-permute-start | bytes 5308424 | tf_op jit(solution)/shard_map/ppermute | solution.py:875
  827.3 29.5 %collective-permute-start.118 = (bf16[128,1536]{1,0:T(8,128)(2,1)}, bf16[128,1536]{1,0:T(8,128)(2,1)S(1)}, u32[]{:S(2)}, u32[]{:S(2)}) collective-permute-start(bf16[128,1536]{1,0:T(8,128)(2,1)} %get-tuple-element.190), channel_id=1, source_target_pairs={{2,0},{3,1},{4,2},{5,3},{6,4},{7,5},{10,8},{11,9},{12,10},{13,11},... | collective-permute-start | bytes 1179656 | tf_op jit(solution)/shard_map/ppermute | solution.py:866
  828.6 28.2 %collective-permute-start.117 = (bf16[128,1536]{1,0:T(8,128)(2,1)}, bf16[128,1536]{1,0:T(8,128)(2,1)S(1)}, u32[]{:S(2)}, u32[]{:S(2)}) collective-permute-start(bf16[128,1536]{1,0:T(8,128)(2,1)} %get-tuple-element.189), channel_id=1, source_target_pairs={{0,2},{1,3},{2,4},{3,5},{4,6},{5,7},{8,10},{9,11},{10,12},{11,13},... | collective-permute-start | bytes 1179656 | tf_op jit(solution)/shard_map/ppermute | solution.py:866
  872.5 41.2 %collective-permute-start.123 = (bf16[576,1536]{1,0:T(8,128)(2,1)}, bf16[576,1536]{1,0:T(8,128)(2,1)S(1)}, u32[]{:S(2)}, u32[]{:S(2)}) collective-permute-start(bf16[576,1536]{1,0:T(8,128)(2,1)} %get-tuple-element.194.refs_20_), channel_id=1, source_target_pairs={{0,8},{8,0},{16,24},{24,16},{1,9},{9,1},{17,25},{25,17},{2,10},{10... | collective-permute-start | bytes 5308424 | tf_op jit(solution)/shard_map/ppermute | solution.py:875
  873.9 41.0 %collective-permute-start.124 = (bf16[576,1536]{1,0:T(8,128)(2,1)}, bf16[576,1536]{1,0:T(8,128)(2,1)}, u32[]{:S(2)}, u32[]{:S(2)}) collective-permute-start(bf16[576,1536]{1,0:T(8,128)(2,1)} %get-tuple-element.196.refs_22_), channel_id=1, source_target_pairs={{0,16},{8,24},{16,0},{24,8},{1,17},{9,25},{17,1},{25,9},{2,18},{10... | collective-permute-start | bytes 5308424 | tf_op jit(solution)/shard_map/ppermute | solution.py:875
  876.9 50.6 %collective-permute-start.141 = (bf16[4,112,1536]{2,1,0:T(8,128)(2,1)}, bf16[4,112,1536]{2,1,0:T(8,128)(2,1)}, u32[]{:S(2)}, u32[]{:S(2)}) collective-permute-start(bf16[4,112,1536]{2,1,0:T(8,128)(2,1)} %get-tuple-element.227), channel_id=1, source_target_pairs={{0,1},{1,0},{2,3},{3,2},{4,5},{5,4},{6,7},{7,6},{8,9},{9,8},{10,11... | collective-permute-start | bytes 4128776 | tf_op jit(solution)/shard_map/ppermute | solution.py:860
  933.6 36.7 %collective-permute-start.142 = (bf16[112,1536]{1,0:T(8,128)(2,1)}, bf16[112,1536]{1,0:T(8,128)(2,1)}, u32[]{:S(2)}, u32[]{:S(2)}) collective-permute-start(bf16[112,1536]{1,0:T(8,128)(2,1)} %get-tuple-element.258), channel_id=1, source_target_pairs={{0,2},{1,3},{8,10},{9,11},{16,18},{17,19},{24,26},{25,27}} | collective-permute-start | bytes 1032200 | tf_op jit(solution)/shard_map/ppermute | solution.py:866
  940.0 61.4 %collective-permute-start.125 = (bf16[4,128,1536]{2,1,0:T(8,128)(2,1)}, bf16[4,128,1536]{2,1,0:T(8,128)(2,1)}, u32[]{:S(2)}, u32[]{:S(2)}) collective-permute-start(bf16[4,128,1536]{2,1,0:T(8,128)(2,1)} %get-tuple-element.213), channel_id=1, source_target_pairs={{0,1},{1,0},{2,3},{3,2},{4,5},{5,4},{6,7},{7,6},{8,9},{9,8},{10,11... | collective-permute-start | bytes 4718600 | tf_op jit(solution)/shard_map/ppermute | solution.py:860
  966.0 35.7 %collective-permute-start.132 = (bf16[4,128,1536]{2,1,0:T(8,128)(2,1)}, bf16[4,128,1536]{2,1,0:T(8,128)(2,1)S(1)}, u32[]{:S(2)}, u32[]{:S(2)}) collective-permute-start(bf16[4,128,1536]{2,1,0:T(8,128)(2,1)} %pad_maximum_fusion.6.rest_12_), channel_id=1, source_target_pairs={{0,16},{8,24},{16,0},{24,8},{1,17},{9,25},{17,1},{25,9},{2,18},{10... | collective-permute-start | bytes 4718600 | tf_op jit(solution)/shard_map/ppermute | solution.py:875
  968.9 35.5 %collective-permute-start.129 = (bf16[4,128,1536]{2,1,0:T(8,128)(2,1)}, bf16[4,128,1536]{2,1,0:T(8,128)(2,1)}, u32[]{:S(2)}, u32[]{:S(2)}) collective-permute-start(bf16[4,128,1536]{2,1,0:T(8,128)(2,1)} %pad_maximum_fusion.5.rest_11_), channel_id=1, source_target_pairs={{0,8},{8,0},{16,24},{24,16},{1,9},{9,1},{17,25},{25,17},{2,10},{10... | collective-permute-start | bytes 4718600 | tf_op jit(solution)/shard_map/ppermute | solution.py:875
  982.0 30.1 %collective-permute-start.146 = (bf16[112,1536]{1,0:T(8,128)(2,1)}, bf16[112,1536]{1,0:T(8,128)(2,1)}, u32[]{:S(2)}, u32[]{:S(2)}) collective-permute-start(bf16[112,1536]{1,0:T(8,128)(2,1)} %get-tuple-element.257), channel_id=1, source_target_pairs={{4,2},{5,3},{6,4},{7,5},{12,10},{13,11},{14,12},{15,13},{20,18},{2... | collective-permute-start | bytes 1032200 | tf_op jit(solution)/shard_map/ppermute | solution.py:866
  983.4 40.0 %collective-permute-start.144 = (bf16[112,1536]{1,0:T(8,128)(2,1)}, bf16[112,1536]{1,0:T(8,128)(2,1)}, u32[]{:S(2)}, u32[]{:S(2)}) collective-permute-start(bf16[112,1536]{1,0:T(8,128)(2,1)} %get-tuple-element.256), channel_id=1, source_target_pairs={{0,2},{1,3},{2,4},{3,5},{4,6},{5,7},{8,10},{9,11},{10,12},{11,13},... | collective-permute-start | bytes 1032200 | tf_op jit(solution)/shard_map/ppermute | solution.py:866
  1020.6 38.2 %collective-permute-start.137 = (bf16[576,1536]{1,0:T(8,128)(2,1)}, bf16[576,1536]{1,0:T(8,128)(2,1)}, u32[]{:S(2)}, u32[]{:S(2)}) collective-permute-start(bf16[576,1536]{1,0:T(8,128)(2,1)} %get-tuple-element.222), channel_id=1, source_target_pairs={{0,8},{8,0},{16,24},{24,16},{1,9},{9,1},{17,25},{25,17},{2,10},{10... | collective-permute-start | bytes 5308424 | tf_op jit(solution)/shard_map/ppermute | solution.py:875
  1021.2 37.9 %collective-permute-start.138 = (bf16[576,1536]{1,0:T(8,128)(2,1)}, bf16[576,1536]{1,0:T(8,128)(2,1)}, u32[]{:S(2)}, u32[]{:S(2)}) collective-permute-start(bf16[576,1536]{1,0:T(8,128)(2,1)} %get-tuple-element.223), channel_id=1, source_target_pairs={{0,16},{8,24},{16,0},{24,8},{1,17},{9,25},{17,1},{25,9},{2,18},{10... | collective-permute-start | bytes 5308424 | tf_op jit(solution)/shard_map/ppermute | solution.py:875
  (193 other events, 2029.8 us)
Sparse Core Ops, SparseCore 0:
  838.8 42.2 reduce-scatter.1
